TPU v7x, 256 devices: a whole 4x4x8 slice. The times are simulated.
256 devices in a mesh: orb: 64 (over x, z, core), rep: 4 (over y).
Axes of the slice: x: 4, y: 4, z: 8, core: 2. Of those that a mesh axis runs over, the one named last changes fastest.
Arguments:
- ints_block: bfloat16 [512, 1536, 512], P('orb', 'rep'), may hold values from -6 to 6
- pair_vectors: bfloat16 [6144, 2, 40, 512], P('orb'), may hold values from -0.0390625 to 0.0390625
- pair_orbitals: int32 [6144, 2], P('orb'), may hold values from 0 to 511, as said below
- orbital_place: int32 [512], replicated, may hold values from 0 to 511, as said below
- amplitudes: bfloat16 [6144, 1600], P(('orb', 'rep')), may hold values from -3 to 3
- pno_energy: float32 [6144, 40], P(('orb', 'rep')), may hold values from 0.2 to 3
- occupied_fock_diagonal: float32 [512], replicated, may hold values from -2 to -0.3
Outputs:
- residual: float32 [6144, 1600], P(('orb', 'rep'))
Inputs may be any that keep to these rules, and one draw needn't show every extreme that they name: `pair_orbitals`: within the 96 pairs of one index of orb, at most 4 of the 192 orbital entries have their block on one owner (owner = orbital_place // 8); some owner has exactly 4 entries from the pairs of every index of orb. `orbital_place`: A permutation of the orbitals.
All inputs are finite; a program needn't handle non-finite values.
Results may differ from a plain program's by a relative error of at most 0.0028.
Values may be sent and summed in bfloat16 or wider, within the bound.
No kernel may reach another device: no remote copies, remote signals or barrier semaphores. Data moves between devices by JAX's collectives and lax.ppermute only.
A program may use at most 128 MiB of HBM per device.

v0:
```python
import jax
import jax.numpy as jnp
from jax import lax
from jax.sharding import PartitionSpec as P


def as_sent(value):
    return jax.tree.map(lambda a: a.astype(jnp.bfloat16) if a.dtype == jnp.float32 else a, value)


def transform_all(ints_block, pieces):
    vectors, rows = pieces
    sources = vectors.shape[0]
    items = vectors.shape[1]
    group = 8
    grouped_vec = vectors.reshape(
        sources // group, group * items, vectors.shape[2], vectors.shape[3]
    )
    grouped_row = rows.reshape(sources // group, group * items)

    def one_group(args):
        vector_piece, row_ids = args
        selected_entries = ints_block[row_ids]
        return jnp.einsum(
            "skb,szb->szk", selected_entries, vector_piece, preferred_element_type=jnp.float32
        ).astype(jnp.bfloat16)

    halves = lax.map(one_group, (grouped_vec, grouped_row))
    return halves.reshape(sources, items, vectors.shape[2], ints_block.shape[1])


def body(
    ints_block,
    pair_vectors,
    pair_orbitals,
    orbital_place,
    amplitudes,
    pno_energy,
    occupied_fock_diagonal,
):
    n_orb = lax.axis_size("orb")
    n_rep = lax.axis_size("rep")
    orbital_keeper = ints_block.shape[0]
    pair_dev = pair_vectors.shape[0]
    npno = pair_vectors.shape[2]
    npao = pair_vectors.shape[3]
    halves = 2 * pair_dev
    cap = n_rep * (1 + halves // (n_orb * n_rep))
    slots = n_orb * cap
    flat_orbs = pair_orbitals.reshape(halves)
    places = orbital_place[flat_orbs]
    owners = places // orbital_keeper
    rows = places % orbital_keeper
    counter = jnp.arange(halves, dtype=jnp.int32)
    same_owner = owners[:, None] == owners[None, :]
    earlier = counter[None, :] < counter[:, None]
    slot_pos = jnp.sum((same_owner & earlier).astype(jnp.int32), axis=1)
    slot_id = owners * cap + slot_pos
    matching_entries = slot_id[None, :] == jnp.arange(slots, dtype=jnp.int32)[:, None]
    live = jnp.any(matching_entries, axis=1)
    source_half = jnp.sum(jnp.where(matching_entries, counter[None, :], 0), axis=1)
    vectors = pair_vectors.reshape(halves, npno, npao)
    send_vec = jnp.where(live[:, None, None], vectors[source_half], jnp.zeros((), jnp.bfloat16))
    send_vec = send_vec.reshape(n_orb, cap, npno, npao)
    send_row = jnp.where(live, rows[source_half], 0).reshape(n_orb, cap)
    results = transform_all(
        ints_block,
        (
            lax.all_to_all(send_vec, "orb", split_axis=0, concat_axis=0, tiled=True),
            lax.all_to_all(send_row, "orb", split_axis=0, concat_axis=0, tiled=True),
        ),
    )
    returned = lax.all_to_all(
        as_sent(results), "orb", split_axis=0, concat_axis=0, tiled=True
    ).astype(results.dtype)
    naux_local = returned.shape[3]
    selected_entries = returned.reshape(slots, npno, naux_local)[slot_id]
    selected_entries = selected_entries.reshape(pair_dev, 2, npno, naux_local)
    partial_value = jnp.einsum(
        "qxp,qyp->qxy",
        selected_entries[:, 0],
        selected_entries[:, 1],
        preferred_element_type=jnp.float32,
    )
    partial_value = partial_value.reshape(pair_dev, npno * npno)
    exchange = lax.psum_scatter(partial_value, "rep", scatter_dimension=0, tiled=True)
    mine = pair_dev // n_rep
    own_orbs = lax.dynamic_slice_in_dim(pair_orbitals, lax.axis_index("rep") * mine, mine, 0)
    first = occupied_fock_diagonal[own_orbs[:, 0]]
    second = occupied_fock_diagonal[own_orbs[:, 1]]
    gap = pno_energy[:, :, None] + pno_energy[:, None, :] - (first + second)[:, None, None]
    return exchange + gap.reshape(mine, npno * npno) * amplitudes.astype(jnp.float32)


def solution(mesh):
    placed = (
        P("orb", "rep", None),
        P("orb", None, None, None),
        P("orb", None),
        P(),
        P(("orb", "rep"), None),
        P(("orb", "rep"), None),
        P(),
    )
    return jax.shard_map(
        body, mesh=mesh, in_specs=placed, out_specs=P(("orb", "rep"), None), check_vma=False
    )
```

profile of v0, /device:TPU:1, one launch (start us, length us, event | category | flops | bytes accessed | tf_op | source)
XLA Modules:
  0.0 672.9 jit_solution(5957089251228837622)
XLA Ops:
  6.5 0.8 copy.34
  7.5 1.6 gather_fusion.1
  9.6 1.9 gather_fusion.3
  12.3 13.0 %all-to-all-start.1 = ((s32[64,1,4]{2,1,0:T(1,128)}), s32[64,1,4]{2,1,0:T(1,128)S(1)}, u32[]{:S(2)}, u32[]{:S(2)}) async-start(s32[64,1,4]{2,1,0:T(1,128)} %bitcast.10), calls=%async_computation.1 | async-start | bytes 65536 | tf_op jit(solution)/shard_map/all_to_all | solution.py:70
  25.4 12.8 %gather_fusion.2 = bf16[256,40,512]{2,1,0:T(8,128)(2,1)} fusion(bf16[192,40,512]{2,1,0:T(8,128)(2,1)} %bitcast.58, s32[1024]{0:T(1024)S(1)} %pad_clamp_fusion.4), kind=kCustom, calls=%fused_computation.2 | custom fusion | bytes 20972544 | tf_op jit(solution)/shard_map/gather | solution.py:63
  38.2 9.9 %broadcast_select_fusion = bf16[64,4,40,512]{3,2,1,0:T(8,128)(2,1)} fusion(bf16[64,4,40,512]{3,2,1,0:T(8,128)(2,1)} %bitcast.57, pred[64,4]{1,0:T(8,128)(4,1)S(1)} %broadcast_in_dim.36), kind=kLoop, calls=%fused_computation.18 | loop fusion | flops 5242880 | bytes 20971776 | tf_op jit(solution)/shard_map/jit(_where)/select_n | solution.py:63
  48.1 10.7 %all-to-all-start = ((bf16[64,4,40,512]{3,2,1,0:T(8,128)(2,1)}), bf16[64,4,40,512]{3,2,1,0:T(8,128)(2,1)}, u32[]{:S(2)}, u32[]{:S(2)}) async-start(bf16[64,4,40,512]{3,2,1,0:T(8,128)(2,1)} %broadcast_select_fusion), calls=%async_computation | async-start | bytes 20971520 | tf_op jit(solution)/shard_map/all_to_all | solution.py:69
  60.1 229.5 %all-to-all-done = bf16[64,4,40,512]{3,2,1,0:T(8,128)(2,1)} async-done(((bf16[64,4,40,512]{3,2,1,0:T(8,128)(2,1)}), bf16[64,4,40,512]{3,2,1,0:T(8,128)(2,1)}, u32[]{:S(2)}, u32[]{:S(2)}) %all-to-all-start) | async-done | bytes 10485792 | tf_op jit(solution)/shard_map/all_to_all | solution.py:69
  289.6 131.0 %while.10 = (s32[]{:T(128)}, bf16[8,32,40,384]{3,2,1,0:T(8,128)(2,1)}, bf16[8,32,40,512]{3,2,1,0:T(8,128)(2,1)}, s32[8,32]{1,0:T(8,128)S(1)}, bf16[8,384,512]{2,1,0:T(8,128)(2,1)S(1)}, /*index=5*/s32[]{:T(128)}) while((s32[]{:T(128)}, bf16[8,32,40,384]{3,2,1,0:T(8,128)(2,1)}, bf16[8,32,40,512]{3,2,1,0:T(8,128)(2,1)}, s32[8,32]{1,0:T(8,128)S(1)}, ...), condition=%wide.region_4.5_spmd, body=%wide.region_3.4_spmd.sunk | while | flops 503809120 | bytes 40048200 | solution.py:28
  289.7 6.7 %gather_fusion = bf16[32,384,512]{2,1,0:T(8,128)(2,1)} fusion(bf16[8,384,512]{2,1,0:T(8,128)(2,1)S(1)} %get-tuple-element.96, s32[1024]{0:T(1024)S(1)} %pad_clamp_fusion.7), kind=kCustom, calls=%fused_computation.clone.1 | custom fusion | bytes 25165952 | tf_op jit(solution)/shard_map/while/body/eval_jaxpr/gather | solution.py:23
  296.4 9.7 %fusion.20 = bf16[8,32,40,384]{3,2,1,0:T(8,128)(2,1)} fusion(bf16[8,32,40,384]{3,2,1,0:T(8,128)(2,1)} %get-tuple-element.87, s32[]{:T(128)} %get-tuple-element.86, bf16[32,384,512]{2,1,0:T(8,128)(2,1)} %gather_fusion, bf16[8,32,40,512]{3,2,1,0:T(8,128)(2,1)} %get-tuple-element.94), kind=kOutput, calls=%fused_computation.9.clone.1 | convolution fusion | flops 503808000 | bytes 14877696 | tf_op jit(solution)/shard_map/while/body/eval_jaxpr/skb,szb->szk/dot_general | solution.py:24
  306.1 6.6 gather_fusion
  312.7 9.7 %fusion.20 = bf16[8,32,40,384]{3,2,1,0:T(8,128)(2,1)} fusion(bf16[8,32,40,384]{3,2,1,0:T(8,128)(2,1)} %get-tuple-element.87, s32[]{:T(128)} %get-tuple-element.86, bf16[32,384,512]{2,1,0:T(8,128)(2,1)} %gather_fusion, bf16[8,32,40,512]{3,2,1,0:T(8,128)(2,1)} %get-tuple-element.94), kind=kOutput, calls=%fused_computation.9.clone.1 | convolution fusion | flops 503808000 | bytes 14877696 | tf_op jit(solution)/shard_map/while/body/eval_jaxpr/skb,szb->szk/dot_general | solution.py:24
  322.4 6.6 gather_fusion
  329.0 9.8 %fusion.20 = bf16[8,32,40,384]{3,2,1,0:T(8,128)(2,1)} fusion(bf16[8,32,40,384]{3,2,1,0:T(8,128)(2,1)} %get-tuple-element.87, s32[]{:T(128)} %get-tuple-element.86, bf16[32,384,512]{2,1,0:T(8,128)(2,1)} %gather_fusion, bf16[8,32,40,512]{3,2,1,0:T(8,128)(2,1)} %get-tuple-element.94), kind=kOutput, calls=%fused_computation.9.clone.1 | convolution fusion | flops 503808000 | bytes 14877696 | tf_op jit(solution)/shard_map/while/body/eval_jaxpr/skb,szb->szk/dot_general | solution.py:24
  338.8 6.7 gather_fusion
  345.5 9.7 %fusion.20 = bf16[8,32,40,384]{3,2,1,0:T(8,128)(2,1)} fusion(bf16[8,32,40,384]{3,2,1,0:T(8,128)(2,1)} %get-tuple-element.87, s32[]{:T(128)} %get-tuple-element.86, bf16[32,384,512]{2,1,0:T(8,128)(2,1)} %gather_fusion, bf16[8,32,40,512]{3,2,1,0:T(8,128)(2,1)} %get-tuple-element.94), kind=kOutput, calls=%fused_computation.9.clone.1 | convolution fusion | flops 503808000 | bytes 14877696 | tf_op jit(solution)/shard_map/while/body/eval_jaxpr/skb,szb->szk/dot_general | solution.py:24
  355.1 6.7 gather_fusion
  361.9 9.7 %fusion.20 = bf16[8,32,40,384]{3,2,1,0:T(8,128)(2,1)} fusion(bf16[8,32,40,384]{3,2,1,0:T(8,128)(2,1)} %get-tuple-element.87, s32[]{:T(128)} %get-tuple-element.86, bf16[32,384,512]{2,1,0:T(8,128)(2,1)} %gather_fusion, bf16[8,32,40,512]{3,2,1,0:T(8,128)(2,1)} %get-tuple-element.94), kind=kOutput, calls=%fused_computation.9.clone.1 | convolution fusion | flops 503808000 | bytes 14877696 | tf_op jit(solution)/shard_map/while/body/eval_jaxpr/skb,szb->szk/dot_general | solution.py:24
  371.6 6.6 gather_fusion
  378.2 9.7 %fusion.20 = bf16[8,32,40,384]{3,2,1,0:T(8,128)(2,1)} fusion(bf16[8,32,40,384]{3,2,1,0:T(8,128)(2,1)} %get-tuple-element.87, s32[]{:T(128)} %get-tuple-element.86, bf16[32,384,512]{2,1,0:T(8,128)(2,1)} %gather_fusion, bf16[8,32,40,512]{3,2,1,0:T(8,128)(2,1)} %get-tuple-element.94), kind=kOutput, calls=%fused_computation.9.clone.1 | convolution fusion | flops 503808000 | bytes 14877696 | tf_op jit(solution)/shard_map/while/body/eval_jaxpr/skb,szb->szk/dot_general | solution.py:24
  387.9 6.7 gather_fusion
  394.6 9.7 %fusion.20 = bf16[8,32,40,384]{3,2,1,0:T(8,128)(2,1)} fusion(bf16[8,32,40,384]{3,2,1,0:T(8,128)(2,1)} %get-tuple-element.87, s32[]{:T(128)} %get-tuple-element.86, bf16[32,384,512]{2,1,0:T(8,128)(2,1)} %gather_fusion, bf16[8,32,40,512]{3,2,1,0:T(8,128)(2,1)} %get-tuple-element.94), kind=kOutput, calls=%fused_computation.9.clone.1 | convolution fusion | flops 503808000 | bytes 14877696 | tf_op jit(solution)/shard_map/while/body/eval_jaxpr/skb,szb->szk/dot_general | solution.py:24
  404.3 6.7 gather_fusion
  411.0 9.7 %fusion.20 = bf16[8,32,40,384]{3,2,1,0:T(8,128)(2,1)} fusion(bf16[8,32,40,384]{3,2,1,0:T(8,128)(2,1)} %get-tuple-element.87, s32[]{:T(128)} %get-tuple-element.86, bf16[32,384,512]{2,1,0:T(8,128)(2,1)} %gather_fusion, bf16[8,32,40,512]{3,2,1,0:T(8,128)(2,1)} %get-tuple-element.94), kind=kOutput, calls=%fused_computation.9.clone.1 | convolution fusion | flops 503808000 | bytes 14877696 | tf_op jit(solution)/shard_map/while/body/eval_jaxpr/skb,szb->szk/dot_general | solution.py:24
  420.6 6.3 all-to-all-start.2
  427.2 174.3 %all-to-all-done.2 = bf16[64,4,40,384]{3,2,1,0:T(8,128)(2,1)} async-done(((bf16[64,4,40,384]{3,2,1,0:T(8,128)(2,1)}), bf16[64,4,40,384]{3,2,1,0:T(8,128)(2,1)}, u32[]{:S(2)}, u32[]{:S(2)}) %all-to-all-start.2) | async-done | bytes 7864352 | tf_op jit(solution)/shard_map/all_to_all | solution.py:73
  601.5 11.8 %gather_fusion.4 = bf16[192,40,384]{2,1,0:T(8,128)(2,1)} fusion(bf16[256,40,384]{2,1,0:T(8,128)(2,1)} %bitcast.12, s32[1024]{0:T(1024)S(1)} %pad_clamp_fusion.3), kind=kCustom, calls=%fused_computation.4 | custom fusion | bytes 11797248 | tf_op jit(solution)/shard_map/gather | solution.py:77
  613.3 4.0 fusion.7
  617.3 1.5 copy.38
  622.1 41.5 %all-reduce.3.cloned.1.call-done = f32[96,1600]{0,1:T(8,128)} async-done(((f32[96,1600]{0,1:T(8,128)}), f32[96,1600]{0,1:T(8,128)}) %all-reduce.3.cloned.1.call-update) | async-done | bytes 614416
  663.6 1.4 constant_dynamic-slice_fusion.1
  (65 shorter events, 6.6 us)
Async XLA Ops:
  6.5 1.0 copy-start
  12.3 35.9 %all-to-all-start.1 = ((s32[64,1,4]{2,1,0:T(1,128)}), s32[64,1,4]{2,1,0:T(1,128)S(1)}, u32[]{:S(2)}, u32[]{:S(2)}) async-start(s32[64,1,4]{2,1,0:T(1,128)} %bitcast.10), calls=%async_computation.1 | async-start | bytes 65536 | tf_op jit(solution)/shard_map/all_to_all | solution.py:70
  48.1 241.5 %copy-start.2 = (bf16[8,384,512]{2,1,0:T(8,128)(2,1)S(1)}, bf16[8,384,512]{2,1,0:T(8,128)(2,1)}, u32[]{:S(2)}) copy-start(bf16[8,384,512]{2,1,0:T(8,128)(2,1)} %param.9) | copy-start | bytes 9437188
  48.1 241.5 %all-to-all-start = ((bf16[64,4,40,512]{3,2,1,0:T(8,128)(2,1)}), bf16[64,4,40,512]{3,2,1,0:T(8,128)(2,1)}, u32[]{:S(2)}, u32[]{:S(2)}) async-start(bf16[64,4,40,512]{3,2,1,0:T(8,128)(2,1)} %broadcast_select_fusion), calls=%async_computation | async-start | bytes 20971520 | tf_op jit(solution)/shard_map/all_to_all | solution.py:69
  420.6 180.9 %all-to-all-start.2 = ((bf16[64,4,40,384]{3,2,1,0:T(8,128)(2,1)}), bf16[64,4,40,384]{3,2,1,0:T(8,128)(2,1)}, u32[]{:S(2)}, u32[]{:S(2)}) async-start(bf16[64,4,40,384]{3,2,1,0:T(8,128)(2,1)} %bitcast.59), calls=%async_computation.2 | async-start | bytes 15728640 | tf_op jit(solution)/shard_map/all_to_all | solution.py:73
  427.0 236.6 %all-reduce.3.cloned.1.call-start = ((), (), s32[]{:S(2)}) async-start(), calls=%async_computation.3 | async-start | bytes 1638400
  613.3 5.6 copy-start.6
  613.3 5.7 copy-start.3
  613.3 7.1 %copy-start.5 = (f32[24,40]{1,0:T(8,128)S(1)}, f32[24,40]{1,0:T(8,128)}, u32[]{:S(2)}) copy-start(f32[24,40]{1,0:T(8,128)} %param.14) | copy-start | bytes 11524
  613.3 7.5 %copy-start.7 = (u32[256]{0:T(256)S(1)}, u32[256]{0:T(256)}, u32[]{:S(2)}) copy-start(u32[256]{0:T(256)} %constant.75) | copy-start | bytes 3076
  613.3 52.7 %copy-start.1 = (s32[512]{0:T(512)S(1)}, s32[512]{0:T(512)}, u32[]{:S(2)}) copy-start(s32[512]{0:T(512)} %param.12) | copy-start | bytes 6148
  613.3 51.9 %copy-start.4 = (bf16[24,1600]{1,0:T(8,128)(2,1)S(1)}, bf16[24,1600]{1,0:T(8,128)(2,1)}, u32[]{:S(2)}) copy-start(bf16[24,1600]{1,0:T(8,128)(2,1)} %param.13) | copy-start | bytes 230404
Sparse Core Ops, SparseCore 0:
  619.0 44.5 all-reduce.2
where the time goes:
time: 674 us; the launch traced here: 673 us
  waiting for transfers between devices  445 us (66%)
  local copies, waits for them, and re-layouts  89.3 us (13%)
  matrix products  81.5 us (12%)
  starting transfers between devices  30.3 us (4%)
  between operations  14.3 us (2%)
  other arithmetic  12.1 us (2%)
    all_to_all x1, waiting for transfers between devices, body(): lax.all_to_all(send_vec, 'orb', split_axis=0, concat_axis=0, tiled=True)  229 us
    all_to_all x1, waiting for transfers between devices, body(): lax.all_to_all(as_sent(results), 'orb', split_axis=0, concat_axis=0, tile...  174 us
    dot_general x8, matrix products, one_group(): jnp.einsum('skb,szb->szk', selected_entries, vector_piece, preferred_elem...  77.6 us
    gather x8, local copies, waits for them, and re-layouts, one_group(): selected_entries = ints_block[row_ids]  53.3 us
    unnamed x2, waiting for transfers between devices  41.5 us
  transfers between devices with their start and end apart: 4, of which 3 were waited for; matrix products, arithmetic and copies ran while one was open for 4% of the time, Pallas kernels for 0%

commit v1 on v0

v1 whole, which is shorter than its diff:
```python
import functools

import jax
import jax.numpy as jnp
from jax import lax
from jax.experimental import pallas as pl
from jax.experimental.pallas import tpu as pltpu
from jax.sharding import PartitionSpec as P

CAP = 4
TOGETHER = 8


def route_kernel(keeper, orbitals, place, plane, vectors, sent, slot, row, count, source, sem):
    owners = sent.shape[0]
    entries = vectors.shape[0]

    def clear(o, _):
        count[o] = 0
        source[o] = 0
        for s in range(CAP):
            row[o * CAP + s] = keeper
        return 0

    lax.fori_loop(0, owners, clear, 0)
    mine = plane[0]

    def one(q, _):
        for side in range(2):
            at = place[orbitals[q, side]]
            owner = at // keeper
            position = count[owner]
            count[owner] = position + 1
            slot[q * 2 + side] = position * owners + owner
            row[owner * CAP + position] = at % keeper

            @pl.when(position == mine)
            def _():
                source[owner] = q * 2 + side

        return 0

    lax.fori_loop(0, entries // 2, one, 0)

    def send(o, _):
        pltpu.make_async_copy(vectors.at[source[o]], sent.at[o], sem).start()
        return 0

    lax.fori_loop(0, owners, send, 0)
    pltpu.make_async_copy(vectors.at[pl.ds(0, owners)], sent, sem).wait()


def route(pair_orbitals, orbital_place, plane, vectors, owners, keeper):
    entries, npno, npao = vectors.shape
    smem = pl.BlockSpec(memory_space=pltpu.SMEM)
    return pl.pallas_call(
        functools.partial(route_kernel, keeper),
        out_shape=(
            jax.ShapeDtypeStruct((owners, npno, npao), vectors.dtype),
            jax.ShapeDtypeStruct((entries,), jnp.int32),
            jax.ShapeDtypeStruct((owners * CAP,), jnp.int32),
        ),
        in_specs=[smem, smem, smem, pl.BlockSpec(memory_space=pl.ANY)],
        out_specs=(pl.BlockSpec(memory_space=pl.ANY), smem, smem),
        scratch_shapes=[
            pltpu.SMEM((owners,), jnp.int32),
            pltpu.SMEM((owners,), jnp.int32),
            pltpu.SemaphoreType.DMA,
        ],
        name="route",
    )(pair_orbitals, orbital_place, plane, vectors)


def half_kernel(rows, vectors, ints, out, order, count, stacked):
    keeper = ints.shape[0]
    items, npno, _ = vectors.shape

    for o in range(keeper + 1):
        count[o] = 0

    def sort(e, _):
        o = rows[e]
        n = count[o]
        order[o * items + n] = e
        count[o] = n + 1
        return 0

    lax.fori_loop(0, items, sort, 0)
    stacked[...] = jnp.zeros_like(stacked)
    deep = stacked.shape[1]

    def orbital(o, _):
        n = count[o]

        def block(b, _):
            ids = [
                order[o * items + jnp.minimum(b * TOGETHER + t, n - 1)] for t in range(TOGETHER)
            ]
            for t in range(TOGETHER):
                stacked[t, :npno] = vectors[ids[t]]
            value = jnp.dot(
                stacked[...].reshape(TOGETHER * deep, stacked.shape[2]),
                ints[o],
                preferred_element_type=jnp.float32,
            ).astype(out.dtype)
            for t in range(TOGETHER):
                out[ids[t]] = value[t * deep : t * deep + npno]
            return 0

        lax.fori_loop(0, (n + TOGETHER - 1) // TOGETHER, block, 0)
        return 0

    lax.fori_loop(0, keeper, orbital, 0)


def half(rows, vectors, ints):
    keeper, npao, naux = ints.shape
    items, npno, _ = vectors.shape
    deep = -(-npno // 16) * 16
    vmem = pl.BlockSpec(memory_space=pltpu.VMEM)
    return pl.pallas_call(
        half_kernel,
        out_shape=jax.ShapeDtypeStruct((items, npno, naux), jnp.bfloat16),
        in_specs=[pl.BlockSpec(memory_space=pltpu.SMEM), vmem, vmem],
        out_specs=vmem,
        scratch_shapes=[
            pltpu.SMEM(((keeper + 1) * items,), jnp.int32),
            pltpu.SMEM((keeper + 1,), jnp.int32),
            pltpu.VMEM((TOGETHER, deep, npao), jnp.bfloat16),
        ],
        compiler_params=pltpu.CompilerParams(vmem_limit_bytes=40 * 2**20),
        cost_estimate=pl.CostEstimate(
            flops=2 * items * npno * npao * naux,
            bytes_accessed=2 * (keeper * npao * naux + items * npno * (npao + naux)),
            transcendentals=0,
        ),
        name="half",
    )(rows, vectors, ints)


def exchange_kernel(place, first, second, third, out, halves, sems):
    owners = first.shape[0]
    copies = [
        pltpu.make_async_copy(first, halves.at[pl.ds(0, owners)], sems.at[0]),
        pltpu.make_async_copy(second, halves.at[pl.ds(owners, 2 * owners)], sems.at[1]),
        pltpu.make_async_copy(third, halves.at[pl.ds(3 * owners, owners)], sems.at[2]),
    ]
    for copy in copies:
        copy.start()
    for copy in copies:
        copy.wait()
    group = 8

    def some(g, _):
        for k in range(group):
            q = g * group + k
            out[q] = lax.dot_general(
                halves[place[2 * q]],
                halves[place[2 * q + 1]],
                (((1,), (1,)), ((), ())),
                preferred_element_type=jnp.float32,
            )
        return 0

    lax.fori_loop(0, out.shape[0] // group, some, 0)


def exchange_of(place, first, second, third):
    owners, npno, naux = first.shape
    pairs = place.shape[0] // 2
    return pl.pallas_call(
        exchange_kernel,
        out_shape=jax.ShapeDtypeStruct((pairs, npno, npno), jnp.float32),
        in_specs=[pl.BlockSpec(memory_space=pltpu.SMEM)] + [pl.BlockSpec(memory_space=pl.ANY)] * 3,
        out_specs=pl.BlockSpec(memory_space=pltpu.VMEM),
        scratch_shapes=[
            pltpu.VMEM((CAP * owners, npno, naux), first.dtype),
            pltpu.SemaphoreType.DMA((3,)),
        ],
        compiler_params=pltpu.CompilerParams(vmem_limit_bytes=40 * 2**20),
        name="exchange",
    )(place, first, second, third)


def body(
    ints_block,
    pair_vectors,
    pair_orbitals,
    orbital_place,
    amplitudes,
    pno_energy,
    occupied_fock_diagonal,
):
    n_orb = lax.axis_size("orb")
    n_rep = lax.axis_size("rep")
    orb = lax.axis_index("orb")
    rep = lax.axis_index("rep")
    keeper, naux, npao = ints_block.shape
    pair_dev = pair_vectors.shape[0]
    npno = pair_vectors.shape[2]
    vectors = pair_vectors.reshape(2 * pair_dev, npno, npao)

    sent, slot, row = route(
        pair_orbitals, orbital_place, rep.reshape(1).astype(jnp.int32), vectors, n_orb, keeper
    )
    rows_all = lax.all_gather(row, "orb", axis=0, tiled=False)
    own = lax.all_to_all(sent, "orb", split_axis=0, concat_axis=0, tiled=True)
    ints = jnp.swapaxes(ints_block, 1, 2)
    rows = lax.dynamic_slice_in_dim(rows_all, orb * CAP, CAP, 1)
    rows = jnp.roll(rows, -rep, axis=1).T

    def shifted(value, by):
        return lax.ppermute(value, "rep", [(i, (i + by) % n_rep) for i in range(n_rep)])

    below = shifted(own, 1)
    above = shifted(own, n_rep - 1)
    far_src, below, above = lax.optimization_barrier((own, below, above))
    far = shifted(far_src, 2)

    def back(value):
        return lax.all_to_all(value, "orb", split_axis=0, concat_axis=0, tiled=True)

    half_own = half(rows[0], own, ints)
    first = back(half_own)
    half_above = half(rows[1], above, ints)
    half_below = half(rows[3], below, ints)
    near = jnp.stack([half_above, half_below], axis=1)
    second = back(near)
    third = back(half(rows[2], far, ints))

    position = (slot // n_orb - rep) % n_rep
    owner = slot % n_orb
    place = jnp.where(
        position == 0,
        owner,
        jnp.where(
            position == 2,
            3 * n_orb + owner,
            n_orb + 2 * owner + (position == 3).astype(jnp.int32),
        ),
    )
    partial_value = exchange_of(place, first, second.reshape(2 * n_orb, npno, naux), third)
    mine = pair_dev // n_rep
    partial_value = partial_value.reshape(n_rep, mine, npno * npno)
    parts = lax.all_to_all(partial_value, "rep", split_axis=0, concat_axis=0, tiled=True)
    exchange = jnp.sum(parts, axis=0)
    own_orbs = lax.dynamic_slice_in_dim(pair_orbitals, rep * mine, mine, 0)
    first_fock = occupied_fock_diagonal[own_orbs[:, 0]]
    second_fock = occupied_fock_diagonal[own_orbs[:, 1]]
    gap = pno_energy[:, :, None] + pno_energy[:, None, :] - (first_fock + second_fock)[:, None, None]
    return exchange + gap.reshape(mine, npno * npno) * amplitudes.astype(jnp.float32)


def solution(mesh):
    placed = (
        P("orb", "rep", None),
        P("orb", None, None, None),
        P("orb", None),
        P(),
        P(("orb", "rep"), None),
        P(("orb", "rep"), None),
        P(),
    )
    return jax.shard_map(
        body, mesh=mesh, in_specs=placed, out_specs=P(("orb", "rep"), None), check_vma=False
    )
```

time: 674 us -> 473 us (0.70)
  waiting for transfers between devices: 445 us -> 190 us
  blocking collectives: 0 us -> 119 us
  Pallas kernels: 0 us -> 118 us
  matrix products: 81.5 us -> 0 us
  local copies, waits for them, and re-layouts: 89.3 us -> 13.1 us
  between operations: 14.3 us -> 0.24 us
  other arithmetic: 12.1 us -> 1.47 us
    all_to_all x3 -> x4, waiting for transfers between devices: 404 us -> 131 us  [the longest x3 123 us: back(): return lax.all_to_all(value, 'orb', split_axis=0, concat_axis=0, tiled=True)]
    pallas_call x0 -> x6, Pallas kernels: none -> 118 us  [the longest x1 85.9 us: route(): pl.pallas_call(functools.partial(route_kernel, keeper), out_shape=(jax.Sh...]
    dot_general x9 -> x0, matrix products: 81.5 us -> none  [the longest x8 77.6 us: one_group(): jnp.einsum('skb,szb->szk', selected_entries, vector_piece, preferred_elem...]
    gather x14 -> x2, local copies, waits for them, and re-layouts: 82.9 us -> 1.42 us  [the longest x1 0.71 us: body(): second_fock = occupied_fock_diagonal[own_orbs[:, 1]]]
    all_to_all x0 -> x1, blocking collectives: none -> 75.4 us  [body(): own = lax.all_to_all(sent, 'orb', split_axis=0, concat_axis=0, tiled=True)]
    ppermute x0 -> x3, waiting for transfers between devices: none -> 58.7 us  [shifted(): lax.ppermute(value, 'rep', [(i, (i + by) % n_rep) for i in range(n_rep)])]
    all_gather x0 -> x1, blocking collectives: none -> 43.5 us  [body(): rows_all = lax.all_gather(row, 'orb', axis=0, tiled=False)]
    unnamed x2 -> x0, waiting for transfers between devices: 41.5 us -> none
  transfers between devices with their start and end apart: 4 -> 7, of which waited for: 3 -> 4; matrix products, arithmetic and copies ran while one was open for 4% -> 2% of each run, Pallas kernels for 0% -> 5%
where the time goes in v1:
time: 473 us; the launch traced here: 472 us
  waiting for transfers between devices  190 us (40%)
  blocking collectives  119 us (25%)
  Pallas kernels  118 us (25%)
  starting transfers between devices  29.7 us (6%)
  local copies, waits for them, and re-layouts  13.1 us (3%)
    all_to_all x3, waiting for transfers between devices, back(): return lax.all_to_all(value, 'orb', split_axis=0, concat_axis=0, tiled=True)  123 us
    pallas_call x1, Pallas kernels, route(): pl.pallas_call(functools.partial(route_kernel, keeper), out_shape=(jax.Sh...  85.9 us
    all_to_all x1, blocking collectives, body(): own = lax.all_to_all(sent, 'orb', split_axis=0, concat_axis=0, tiled=True)  75.4 us
    ppermute x3, waiting for transfers between devices, shifted(): lax.ppermute(value, 'rep', [(i, (i + by) % n_rep) for i in range(n_rep)])  58.7 us
    all_gather x1, blocking collectives, body(): rows_all = lax.all_gather(row, 'orb', axis=0, tiled=False)  43.5 us
    pallas_call x4, Pallas kernels, half(): pl.pallas_call(half_kernel, out_shape=jax.ShapeDtypeStruct((items, npno,...  25.3 us
    all_to_all x3, starting transfers between devices, back(): return lax.all_to_all(value, 'orb', split_axis=0, concat_axis=0, tiled=True)  22.2 us
  transfers between devices with their start and end apart: 7, of which 4 were waited for; matrix products, arithmetic and copies ran while one was open for 2% of the time, Pallas kernels for 5%

profile of v1, /device:TPU:1, one launch (start us, length us, event | category | flops | bytes accessed | tf_op | source)
XLA Modules:
  0.0 471.5 jit_solution(18233178758620203054)
XLA Ops:
  0.0 1.4 copy.18.orbitals
  1.4 85.9 %route.1 = (bf16[64,40,512]{2,1,0:T(8,128)(2,1)}, s32[192]{0:T(256)}, s32[256]{0:T(256)}) custom-call(s32[96,2]{1,0:T(8,128)} %copy.18.orbitals, s32[512]{0:T(512)} %place.1, s32[1]{0:T(128)} %bitcast.plane, bf16[192,40,512]{2,1,0:T(8,128)(2,1)} %bitcast.28), custom_call_target="tpu_custom_call" | custom-call | tf_op jit(solution)/shard_map/route/pallas_call | solution.py:56
  87.3 75.4 %all_to_all.25.vectors = bf16[64,40,512]{2,1,0:T(8,128)(2,1)} all-to-all(bf16[64,40,512]{2,1,0:T(8,128)(2,1)} %get-tuple-element.13), channel_id=1, replica_groups=mesh['orb'=64,'rep'=4] {'orb'}, dimensions={0} | all-to-all | bytes 5242880 | tf_op jit(solution)/shard_map/all_to_all | solution.py:207
  162.6 1.3 collective-permute-start
  163.9 1.4 collective-permute-start.1
  165.4 43.5 %all-gather.1 = s32[64,1,256]{2,1,0:T(1,128)S(1)} all-gather(s32[1,1,256]{2,1,0:T(1,128)S(1)} %bitcast.30), channel_id=2, replica_groups=mesh['orb'=64,'rep'=4] {'orb'}, dimensions={0}, use_global_device_ids=true | all-gather | bytes 66560 | tf_op jit(solution)/shard_map/all_gather | solution.py:206
  208.9 0.1 constant_dynamic-slice_fusion.1
  209.1 3.5 copy.20
  212.6 7.5 %half.4 = bf16[64,40,384]{2,1,0:T(8,128)(2,1)S(1)} custom-call(s32[64]{0:T(128)S(1)} %get-tuple-element.20.rows, bf16[64,40,512]{2,1,0:T(8,128)(2,1)} %all_to_all.25.vectors, bf16[8,512,384]{2,1,0:T(8,128)(2,1)S(1)} %bitcast.22), custom_call_target="tpu_custom_call" | custom-call | flops 1006632960 | bytes 7733248 | tf_op jit(solution)/shard_map/half/pallas_call | solution.py:121
  220.2 1.3 copy-done.2
  221.5 5.1 %all-to-all-start.1 = ((bf16[64,40,384]{2,1,0:T(8,128)(2,1)}), bf16[64,40,384]{2,1,0:T(8,128)(2,1)}, u32[]{:S(2)}, u32[]{:S(2)}) async-start(bf16[64,40,384]{2,1,0:T(8,128)(2,1)} %copy-done.2), calls=%async_computation.1 | async-start | bytes 3932160 | tf_op jit(solution)/shard_map/all_to_all | solution.py:221
  226.6 1.0 collective-permute-start.2
  227.6 58.7 %collective-permute-done.2.vectors = bf16[64,40,512]{2,1,0:T(8,128)(2,1)S(1)} collective-permute-done((bf16[64,40,512]{2,1,0:T(8,128)(2,1)}, bf16[64,40,512]{2,1,0:T(8,128)(2,1)S(1)}, u32[]{:S(2)}, u32[]{:S(2)}) %collective-permute-start.2) | collective-permute-done | bytes 2621472 | tf_op jit(solution)/shard_map/ppermute | solution.py:213
  286.4 5.2 %half.7 = bf16[64,40,384]{2,1,0:T(8,128)(2,1)S(1)} custom-call(s32[64]{0:T(128)S(1)} %get-tuple-element.17.rows, bf16[64,40,512]{2,1,0:T(8,128)(2,1)S(1)} %collective-permute-done.2.vectors, bf16[8,512,384]{2,1,0:T(8,128)(2,1)S(1)} %bitcast.23), custom_call_target="tpu_custom_call" | custom-call | flops 1006632960 | bytes 7733248 | tf_op jit(solution)/shard_map/half/pallas_call | solution.py:121
  291.6 1.4 copy-done.1
  293.0 10.8 %all-to-all-start.3 = ((bf16[64,40,384]{2,1,0:T(8,128)(2,1)}), bf16[64,40,384]{2,1,0:T(8,128)(2,1)}, u32[]{:S(2)}, u32[]{:S(2)}) async-start(bf16[64,40,384]{2,1,0:T(8,128)(2,1)} %copy-done.1), calls=%async_computation.3 | async-start | bytes 3932160 | tf_op jit(solution)/shard_map/all_to_all | solution.py:221
  303.8 6.8 %half.5 = bf16[64,40,384]{2,1,0:T(8,128)(2,1)S(1)} custom-call(s32[64]{0:T(128)S(1)} %get-tuple-element.19.rows, bf16[64,40,512]{2,1,0:T(8,128)(2,1)} %collective-permute-done.1.vectors, bf16[8,512,384]{2,1,0:T(8,128)(2,1)S(1)} %bitcast.24), custom_call_target="tpu_custom_call" | custom-call | flops 1006632960 | bytes 7733248 | tf_op jit(solution)/shard_map/half/pallas_call | solution.py:121
  310.6 5.7 %half.6 = bf16[64,40,384]{2,1,0:T(8,128)(2,1)S(1)} custom-call(s32[64]{0:T(128)S(1)} %get-tuple-element.18.rows, bf16[64,40,512]{2,1,0:T(8,128)(2,1)} %collective-permute-done.vectors, bf16[8,512,384]{2,1,0:T(8,128)(2,1)S(1)} %bitcast.25), custom_call_target="tpu_custom_call" | custom-call | flops 1006632960 | bytes 7733248 | tf_op jit(solution)/shard_map/half/pallas_call | solution.py:121
  316.3 0.4 pad_maximum_fusion
  316.8 2.3 copy.21
  319.0 33.0 %all-to-all-done.3.third = bf16[64,40,384]{2,1,0:T(8,128)(2,1)} async-done(((bf16[64,40,384]{2,1,0:T(8,128)(2,1)}), bf16[64,40,384]{2,1,0:T(8,128)(2,1)}, u32[]{:S(2)}, u32[]{:S(2)}) %all-to-all-start.3) | async-done | bytes 1966112 | tf_op jit(solution)/shard_map/all_to_all | solution.py:221
  352.0 6.2 %all-to-all-start.2 = ((bf16[64,2,40,384]{3,2,1,0:T(8,128)(2,1)}), bf16[64,2,40,384]{3,2,1,0:T(8,128)(2,1)}, u32[]{:S(2)}, u32[]{:S(2)}) async-start(bf16[64,2,40,384]{3,2,1,0:T(8,128)(2,1)} %copy.21), calls=%async_computation.2 | async-start | bytes 7864320 | tf_op jit(solution)/shard_map/all_to_all | solution.py:221
  358.3 90.2 %all-to-all-done.2 = bf16[64,2,40,384]{3,2,1,0:T(8,128)(2,1)} async-done(((bf16[64,2,40,384]{3,2,1,0:T(8,128)(2,1)}), bf16[64,2,40,384]{3,2,1,0:T(8,128)(2,1)}, u32[]{:S(2)}, u32[]{:S(2)}) %all-to-all-start.2) | async-done | bytes 3932192 | tf_op jit(solution)/shard_map/all_to_all | solution.py:221
  448.5 6.8 %exchange.1 = f32[96,40,40]{2,1,0:T(8,128)S(1)} custom-call(s32[192]{0:T(256)S(1)} %compare_select_fusion.5.place, bf16[64,40,384]{2,1,0:T(8,128)(2,1)} %all-to-all-done.1.first, bf16[128,40,384]{2,1,0:T(8,128)(2,1)} %bitcast.11.second, bf16[64,40,384]{2,1,0:T(8,128)(2,1)} %all-to-all-done.3.third), custom_call_target="tpu_custom_call" | custom-call | tf_op jit(solution)/shard_map/exchange/pallas_call | solution.py:171
  455.3 1.4 reshape.26
  456.8 3.8 all-to-all-start.4
  460.6 0.7 gather_fusion
  461.3 0.7 gather_fusion.1
  462.0 0.2 broadcast_add_fusion
  462.2 0.2 add.87
  462.4 8.3 %all-to-all-done.4 = f32[4,24,1600]{2,1,0:T(8,128)S(1)} async-done(((f32[4,24,1600]{2,1,0:T(8,128)}), f32[4,24,1600]{2,1,0:T(8,128)S(1)}, u32[]{:S(2)}, u32[]{:S(2)}) %all-to-all-start.4) | async-done | bytes 614432 | tf_op jit(solution)/shard_map/all_to_all | solution.py:245
  470.7 0.8 multiply_add_fusion
  (27 shorter events, 0.3 us)
Async XLA Ops:
  0.0 460.6 %copy-start = (f32[512]{0:T(512)S(1)}, f32[512]{0:T(512)}, u32[]{:S(2)}) copy-start(f32[512]{0:T(512)} %param.13) | copy-start | bytes 6148
  87.3 78.1 %copy-start.6 = (s32[256]{0:T(256)S(1)}, s32[256]{0:T(256)}, u32[]{:S(2)}) copy-start(s32[256]{0:T(256)} %get-tuple-element.12) | copy-start | bytes 3076
  162.6 63.9 %collective-permute-start = (bf16[64,40,512]{2,1,0:T(8,128)(2,1)}, bf16[64,40,512]{2,1,0:T(8,128)(2,1)}, u32[]{:S(2)}, u32[]{:S(2)}) collective-permute-start(bf16[64,40,512]{2,1,0:T(8,128)(2,1)} %all_to_all.25.vectors), channel_id=1, source_target_pairs={{0,1},{1,2},{2,3},{3,0},{4,5},{5,6},{6,7},{7,4},{8,9},{9,10},{10,1... | collective-permute-start | bytes 7864328 | tf_op jit(solution)/shard_map/ppermute | solution.py:213
  163.9 62.7 %collective-permute-start.1 = (bf16[64,40,512]{2,1,0:T(8,128)(2,1)}, bf16[64,40,512]{2,1,0:T(8,128)(2,1)}, u32[]{:S(2)}, u32[]{:S(2)}) collective-permute-start(bf16[64,40,512]{2,1,0:T(8,128)(2,1)} %all_to_all.25.vectors), channel_id=1, source_target_pairs={{0,3},{1,0},{2,1},{3,2},{4,7},{5,4},{6,5},{7,6},{8,11},{9,8},{10,9... | collective-permute-start | bytes 7864328 | tf_op jit(solution)/shard_map/ppermute | solution.py:213
  220.2 1.3 copy-start.2
  221.5 71.5 %all-to-all-start.1 = ((bf16[64,40,384]{2,1,0:T(8,128)(2,1)}), bf16[64,40,384]{2,1,0:T(8,128)(2,1)}, u32[]{:S(2)}, u32[]{:S(2)}) async-start(bf16[64,40,384]{2,1,0:T(8,128)(2,1)} %copy-done.2), calls=%async_computation.1 | async-start | bytes 3932160 | tf_op jit(solution)/shard_map/all_to_all | solution.py:221
  226.6 59.8 %collective-permute-start.2 = (bf16[64,40,512]{2,1,0:T(8,128)(2,1)}, bf16[64,40,512]{2,1,0:T(8,128)(2,1)S(1)}, u32[]{:S(2)}, u32[]{:S(2)}) collective-permute-start(bf16[64,40,512]{2,1,0:T(8,128)(2,1)} %all_to_all.25.vectors), channel_id=1, source_target_pairs={{0,2},{1,3},{2,0},{3,1},{4,6},{5,7},{6,4},{7,5},{8,10},{9,11},{10,... | collective-permute-start | bytes 7864328 | tf_op jit(solution)/shard_map/ppermute | solution.py:213
  291.6 1.4 copy-start.1
  293.0 59.0 %all-to-all-start.3 = ((bf16[64,40,384]{2,1,0:T(8,128)(2,1)}), bf16[64,40,384]{2,1,0:T(8,128)(2,1)}, u32[]{:S(2)}, u32[]{:S(2)}) async-start(bf16[64,40,384]{2,1,0:T(8,128)(2,1)} %copy-done.1), calls=%async_computation.3 | async-start | bytes 3932160 | tf_op jit(solution)/shard_map/all_to_all | solution.py:221
  319.0 39.2 %copy-start.5 = (s32[96,2]{0,1:T(2,128)S(1)}, s32[96,2]{0,1:T(2,128)}, u32[]{:S(2)}) copy-start(s32[96,2]{0,1:T(2,128)} %param.9) | copy-start | bytes 2308
  319.0 39.3 %copy-start.7 = (s32[192]{0:T(256)S(1)}, s32[192]{0:T(256)}, u32[]{:S(2)}) copy-start(s32[192]{0:T(256)} %get-tuple-element.11) | copy-start | bytes 2308
  352.0 96.5 %all-to-all-start.2 = ((bf16[64,2,40,384]{3,2,1,0:T(8,128)(2,1)}), bf16[64,2,40,384]{3,2,1,0:T(8,128)(2,1)}, u32[]{:S(2)}, u32[]{:S(2)}) async-start(bf16[64,2,40,384]{3,2,1,0:T(8,128)(2,1)} %copy.21), calls=%async_computation.2 | async-start | bytes 7864320 | tf_op jit(solution)/shard_map/all_to_all | solution.py:221
  455.3 6.7 %copy-start.4 = (f32[24,40]{1,0:T(8,128)S(1)}, f32[24,40]{1,0:T(8,128)}, u32[]{:S(2)}) copy-start(f32[24,40]{1,0:T(8,128)} %param.12) | copy-start | bytes 11524
  456.8 14.0 %copy-start.3 = (bf16[24,1600]{1,0:T(8,128)(2,1)S(1)}, bf16[24,1600]{1,0:T(8,128)(2,1)}, u32[]{:S(2)}) copy-start(bf16[24,1600]{1,0:T(8,128)(2,1)} %param.11) | copy-start | bytes 230404
  456.8 13.9 %all-to-all-start.4 = ((f32[4,24,1600]{2,1,0:T(8,128)}), f32[4,24,1600]{2,1,0:T(8,128)S(1)}, u32[]{:S(2)}, u32[]{:S(2)}) async-start(f32[4,24,1600]{2,1,0:T(8,128)} %reshape.26), calls=%async_computation.4 | async-start | bytes 1277952 | tf_op jit(solution)/shard_map/all_to_all | solution.py:245

commit v2 on v1

v2 whole, which is shorter than its diff:
```python
import functools

import jax
import jax.numpy as jnp
from jax import lax
from jax.experimental import pallas as pl
from jax.experimental.pallas import tpu as pltpu
from jax.sharding import PartitionSpec as P

CAP = 4
TOGETHER = 8


LANES = 128
SPARE = 8


def pieces(npno, npao):
    whole = npno // 16 * 16
    blocks = npao // LANES
    cuts = []
    for c in range(blocks):
        lanes = slice(c * LANES, (c + 1) * LANES)
        cuts.append((slice(0, whole), lanes, slice(c * whole, (c + 1) * whole)))
        if npno > whole:
            at = blocks * whole + c * (npno - whole)
            cuts.append((slice(whole, npno), lanes, slice(at, at + npno - whole)))
    return cuts


def route_kernel(
    keeper, orbitals, place, plane, vectors, sent, slot, count, source, row, held, record, sems
):
    owners, npno, npao = held.shape
    pairs = orbitals.shape[1]
    together = 4

    def clear(o, _):
        count[o] = 0
        source[o] = 0
        row[o] = keeper
        return 0

    lax.fori_loop(0, owners, clear, 0, unroll=8)
    mine = plane[0]

    def some(g, _):
        for k in range(together):
            q = g * together + k
            for side in range(2):
                at = place[orbitals[side, q]]
                owner = at // keeper
                position = count[owner]
                count[owner] = position + 1
                slot[q * 2 + side] = position * owners + owner
                to = owner + jnp.where(position == mine, 0, owners)
                source[to] = q * 2 + side
                row[to] = at % keeper
        return 0

    lax.fori_loop(0, pairs // together, some, 0)

    def fetch(o, _):
        pltpu.make_async_copy(vectors.at[source[o]], held.at[o], sems.at[0]).start()
        return 0

    lax.fori_loop(0, owners, fetch, 0, unroll=8)
    pltpu.make_async_copy(vectors.at[pl.ds(0, owners)], held, sems.at[0]).wait()

    def lay(o, _):
        for rows, lanes, at in pieces(npno, npao):
            record[o, at, :] = held[o, rows, lanes]
        number = jnp.full((SPARE, LANES), row[o], jnp.int32).astype(jnp.float32)
        record[o, npno * npao // LANES :, :] = number.astype(record.dtype)
        return 0

    lax.fori_loop(0, owners, lay, 0, unroll=2)
    out = pltpu.make_async_copy(record, sent, sems.at[1])
    out.start()
    out.wait()


def route(orbitals, orbital_place, plane, vectors, owners, keeper):
    entries, npno, npao = vectors.shape
    depth = npno * npao // LANES + SPARE
    smem = pl.BlockSpec(memory_space=pltpu.SMEM)
    hbm = pl.BlockSpec(memory_space=pltpu.HBM)
    return pl.pallas_call(
        functools.partial(route_kernel, keeper),
        out_shape=(
            jax.ShapeDtypeStruct((owners, depth, LANES), vectors.dtype),
            jax.ShapeDtypeStruct((entries,), jnp.int32),
        ),
        in_specs=[smem, smem, smem, hbm],
        out_specs=(hbm, smem),
        scratch_shapes=[
            pltpu.SMEM((owners,), jnp.int32),
            pltpu.SMEM((2 * owners,), jnp.int32),
            pltpu.SMEM((2 * owners,), jnp.int32),
            pltpu.VMEM((owners, npno, npao), vectors.dtype),
            pltpu.VMEM((owners, depth, LANES), vectors.dtype),
            pltpu.SemaphoreType.DMA((2,)),
        ],
        compiler_params=pltpu.CompilerParams(vmem_limit_bytes=60 * 2**20),
        name="route",
    )(orbitals, orbital_place, plane, vectors)


def half_kernel(parts, npno, *refs):
    rows, records, (ints, out) = refs[:parts], refs[parts : 2 * parts], refs[2 * parts : 2 * parts + 2]
    order, count, stacked, vectors, blocks, halves, sems = refs[2 * parts + 2 :]
    keeper, npao, _ = ints.shape
    items = records[0].shape[0]
    deep = stacked.shape[1]
    copies = [
        pltpu.make_async_copy(records[part], vectors.at[part], sems.at[keeper + part])
        for part in range(parts)
    ]
    loads = [pltpu.make_async_copy(ints.at[o], blocks.at[o], sems.at[o]) for o in range(keeper)]
    copies[0].start()
    for load in loads:
        load.start()
    for copy in copies[1:]:
        copy.start()
    stacked[...] = jnp.zeros_like(stacked)

    for part in range(parts):
        for o in range(keeper + 1):
            count[o] = 0

        def sort(e, _):
            o = rows[part][e]
            n = count[o]
            order[o * items + n] = e
            count[o] = n + 1
            return 0

        lax.fori_loop(0, items, sort, 0, unroll=8)
        copies[part].wait()

        for o in range(keeper):
            if part == 0:
                loads[o].wait()
            n = count[o]

            def block(b, _):
                ids = [
                    order[o * items + jnp.minimum(b * TOGETHER + t, n - 1)]
                    for t in range(TOGETHER)
                ]
                for t in range(TOGETHER):
                    for held, lanes, at in pieces(npno, npao):
                        stacked[t, held, lanes] = vectors[part, ids[t], at, :]
                value = jnp.dot(
                    stacked[...].reshape(TOGETHER * deep, npao),
                    blocks[o],
                    preferred_element_type=jnp.float32,
                ).astype(out.dtype)
                for t in range(TOGETHER):
                    halves[ids[t], part] = value[t * deep : t * deep + npno]
                return 0

            lax.fori_loop(0, (n + TOGETHER - 1) // TOGETHER, block, 0)

    back = pltpu.make_async_copy(halves, out, sems.at[keeper + parts])
    back.start()
    back.wait()


def half(rows, records, ints, npno):
    parts = len(records)
    keeper, npao, naux = ints.shape
    items, depth, _ = records[0].shape
    deep = -(-npno // 16) * 16
    hbm = pl.BlockSpec(memory_space=pltpu.HBM)
    return pl.pallas_call(
        functools.partial(half_kernel, parts, npno),
        out_shape=jax.ShapeDtypeStruct((items, parts, npno, naux), jnp.bfloat16),
        in_specs=[pl.BlockSpec(memory_space=pltpu.SMEM)] * parts + [hbm] * (parts + 1),
        out_specs=hbm,
        scratch_shapes=[
            pltpu.SMEM(((keeper + 1) * items,), jnp.int32),
            pltpu.SMEM((keeper + 1,), jnp.int32),
            pltpu.VMEM((TOGETHER, deep, npao), jnp.bfloat16),
            pltpu.VMEM((parts, items, depth, LANES), jnp.bfloat16),
            pltpu.VMEM((keeper, npao, naux), jnp.bfloat16),
            pltpu.VMEM((items, parts, npno, naux), jnp.bfloat16),
            pltpu.SemaphoreType.DMA((keeper + parts + 1,)),
        ],
        compiler_params=pltpu.CompilerParams(vmem_limit_bytes=60 * 2**20),
        cost_estimate=pl.CostEstimate(
            flops=16 * parts * items * npno * npao * naux,
            bytes_accessed=2 * (keeper * npao * naux + parts * items * npno * (npao + naux)),
            transcendentals=0,
        ),
        name="half",
    )(*rows, *records, ints)


def exchange_kernel(place, first, second, third, out, halves, sems):
    owners = first.shape[0]
    copies = [
        pltpu.make_async_copy(first, halves.at[pl.ds(0, owners)], sems.at[0]),
        pltpu.make_async_copy(second, halves.at[pl.ds(owners, 2 * owners)], sems.at[1]),
        pltpu.make_async_copy(third, halves.at[pl.ds(3 * owners, owners)], sems.at[2]),
    ]
    for copy in copies:
        copy.start()
    for copy in copies:
        copy.wait()
    group = 8

    def some(g, _):
        for k in range(group):
            q = g * group + k
            out[q] = lax.dot_general(
                halves[place[2 * q]],
                halves[place[2 * q + 1]],
                (((1,), (1,)), ((), ())),
                preferred_element_type=jnp.float32,
            )
        return 0

    lax.fori_loop(0, out.shape[0] // group, some, 0)


def exchange_of(place, first, second, third):
    owners, npno, naux = first.shape
    pairs = place.shape[0] // 2
    return pl.pallas_call(
        exchange_kernel,
        out_shape=jax.ShapeDtypeStruct((pairs, npno, npno), jnp.float32),
        in_specs=[pl.BlockSpec(memory_space=pltpu.SMEM)] + [pl.BlockSpec(memory_space=pltpu.HBM)] * 3,
        out_specs=pl.BlockSpec(memory_space=pltpu.VMEM),
        scratch_shapes=[
            pltpu.VMEM((CAP * owners, npno, naux), first.dtype),
            pltpu.SemaphoreType.DMA((3,)),
        ],
        compiler_params=pltpu.CompilerParams(vmem_limit_bytes=60 * 2**20),
        name="exchange",
    )(place, first, second, third)


def body(
    ints_block,
    pair_vectors,
    pair_orbitals,
    orbital_place,
    amplitudes,
    pno_energy,
    occupied_fock_diagonal,
):
    n_orb = lax.axis_size("orb")
    n_rep = lax.axis_size("rep")
    rep = lax.axis_index("rep")
    keeper, naux, npao = ints_block.shape
    pair_dev = pair_vectors.shape[0]
    npno = pair_vectors.shape[2]
    vectors = pair_vectors.reshape(2 * pair_dev, npno, npao)

    def shifted(value, by):
        return lax.ppermute(value, "rep", [(i, (i + by) % n_rep) for i in range(n_rep)])

    def there(value):
        return lax.all_to_all(value, "orb", split_axis=0, concat_axis=0, tiled=True)

    def row_of(record):
        return record[:, npno * npao // LANES, 0].astype(jnp.int32)

    def halves(*records):
        return half(tuple(row_of(record) for record in records), records, ints, npno)

    sent, slot = route(
        pair_orbitals.T, orbital_place, rep.reshape(1).astype(jnp.int32), vectors, n_orb, keeper
    )
    own = there(sent)
    ints = jnp.swapaxes(lax.optimization_barrier((ints_block, sent))[0], 1, 2)
    own, ints = lax.optimization_barrier((own, ints))
    below = shifted(own, 1)
    above = shifted(own, n_rep - 1)
    first = there(halves(own))
    near = halves(above, below)
    near, first = lax.optimization_barrier((near, first))
    second = there(near)
    far = halves(shifted(lax.optimization_barrier((own, below, above))[0], 2))
    far, second = lax.optimization_barrier((far, second))
    third = there(far)

    position = (slot // n_orb - rep) % n_rep
    owner = slot % n_orb
    place = jnp.where(
        position == 0,
        owner,
        jnp.where(
            position == 2,
            3 * n_orb + owner,
            n_orb + 2 * owner + (position == 3).astype(jnp.int32),
        ),
    )
    partial_value = exchange_of(
        place, *(part.reshape(-1, npno, naux) for part in (first, second, third))
    )
    mine = pair_dev // n_rep
    partial_value = partial_value.reshape(n_rep, mine, npno * npno)
    exchange = lax.dynamic_index_in_dim(partial_value, rep, 0, keepdims=False)
    for by in (1, n_rep - 1, 2):
        leaving = lax.dynamic_index_in_dim(partial_value, (rep + by) % n_rep, 0, keepdims=False)
        exchange = exchange + shifted(leaving, by)
    own_orbs = lax.dynamic_slice_in_dim(pair_orbitals, rep * mine, mine, 0)
    first_fock = occupied_fock_diagonal[own_orbs[:, 0]]
    second_fock = occupied_fock_diagonal[own_orbs[:, 1]]
    gap = pno_energy[:, :, None] + pno_energy[:, None, :] - (first_fock + second_fock)[:, None, None]
    return exchange + gap.reshape(mine, npno * npno) * amplitudes.astype(jnp.float32)


def solution(mesh):
    placed = (
        P("orb", "rep", None),
        P("orb", None, None, None),
        P("orb", None),
        P(),
        P(("orb", "rep"), None),
        P(("orb", "rep"), None),
        P(),
    )
    return jax.shard_map(
        body, mesh=mesh, in_specs=placed, out_specs=P(("orb", "rep"), None), check_vma=False
    )
```

time: 473 us -> 346 us (0.73)
  blocking collectives: 119 us -> 0 us
  Pallas kernels: 118 us -> 43.3 us
  waiting for transfers between devices: 190 us -> 240 us
  starting transfers between devices: 29.7 us -> 40.9 us
  other arithmetic: 1.47 us -> 11.4 us
    pallas_call x1, Pallas kernels: 85.9 us -> 7.54 us  [route(): pl.pallas_call(functools.partial(route_kernel, keeper), out_shape=(jax.Sh...]
    all_to_all x1 -> x0, blocking collectives: 75.4 us -> none  [body(): own = lax.all_to_all(sent, 'orb', split_axis=0, concat_axis=0, tiled=True)]
    ppermute x3 -> x6, waiting for transfers between devices: 58.7 us -> 113 us  [shifted(): lax.ppermute(value, 'rep', [(i, (i + by) % n_rep) for i in range(n_rep)])]
    all_gather x1 -> x0, blocking collectives: 43.5 us -> none  [body(): rows_all = lax.all_gather(row, 'orb', axis=0, tiled=False)]
    convert_element_type x0 -> x4, other arithmetic: none -> 9.82 us  [row_of(): return record[:, npno * npao // LANES, 0].astype(jnp.int32)]
    all_to_all x4, starting transfers between devices: 25.9 us -> 33 us  [there(): return lax.all_to_all(value, 'orb', split_axis=0, concat_axis=0, tiled=True)]
    unnamed x18, local copies, waits for them, and re-layouts: 7.53 us -> 2.61 us
    pallas_call x4 -> x3, Pallas kernels: 25.3 us -> 27.5 us  [half(): pl.pallas_call(functools.partial(half_kernel, parts, npno), out_shape=jax...]
  transfers between devices with their start and end apart: 7 -> 10, of which waited for: 4 -> 7; matrix products, arithmetic and copies ran while one was open for 2% -> 4% of each run, Pallas kernels for 5% -> 8%
where the time goes in v2:
time: 346 us; the launch traced here: 345 us
  waiting for transfers between devices  240 us (69%)
  Pallas kernels  43.3 us (13%)
  starting transfers between devices  40.9 us (12%)
  other arithmetic  11.4 us (3%)
  local copies, waits for them, and re-layouts  9.34 us (3%)
    all_to_all x4, waiting for transfers between devices, there(): return lax.all_to_all(value, 'orb', split_axis=0, concat_axis=0, tiled=True)  127 us
    ppermute x6, waiting for transfers between devices, shifted(): lax.ppermute(value, 'rep', [(i, (i + by) % n_rep) for i in range(n_rep)])  113 us
    all_to_all x4, starting transfers between devices, there(): return lax.all_to_all(value, 'orb', split_axis=0, concat_axis=0, tiled=True)  33 us
    pallas_call x3, Pallas kernels, half(): pl.pallas_call(functools.partial(half_kernel, parts, npno), out_shape=jax...  27.5 us
    convert_element_type x4, other arithmetic, row_of(): return record[:, npno * npao // LANES, 0].astype(jnp.int32)  9.82 us
    pallas_call x1, Pallas kernels, exchange_of(): pl.pallas_call(exchange_kernel, out_shape=jax.ShapeDtypeStruct((pairs, np...  8.22 us
    ppermute x6, starting transfers between devices, shifted(): lax.ppermute(value, 'rep', [(i, (i + by) % n_rep) for i in range(n_rep)])  7.97 us
    pallas_call x1, Pallas kernels, route(): pl.pallas_call(functools.partial(route_kernel, keeper), out_shape=(jax.Sh...  7.54 us
  transfers between devices with their start and end apart: 10, of which 7 were waited for; matrix products, arithmetic and copies ran while one was open for 4% of the time, Pallas kernels for 8%

profile of v2, /device:TPU:1, one launch (start us, length us, event | category | flops | bytes accessed | tf_op | source)
XLA Modules:
  0.0 345.3 jit_solution(15179216981477957197)
XLA Ops:
  0.0 7.5 %route.1 = (bf16[64,168,128]{2,1,0:T(8,128)(2,1)}, s32[192]{0:T(256)}) custom-call(s32[2,96]{1,0:T(2,128)} %bitcast.31, s32[512]{0:T(512)} %place.1, s32[1]{0:T(128)} %bitcast.1.plane, bf16[192,40,512]{2,1,0:T(8,128)(2,1)} %bitcast.27), custom_call_target="tpu_custom_call" | custom-call | tf_op jit(solution)/shard_map/route/pallas_call | solution.py:88
  7.6 13.4 %all-to-all-start = ((bf16[64,168,128]{2,1,0:T(8,128)(2,1)}), bf16[64,168,128]{2,1,0:T(8,128)(2,1)}, u32[]{:S(2)}, u32[]{:S(2)}) async-start(bf16[64,168,128]{2,1,0:T(8,128)(2,1)} %get-tuple-element.16), calls=%async_computation | async-start | bytes 5505024 | tf_op jit(solution)/shard_map/all_to_all | solution.py:265
  21.0 2.9 copy.14
  23.9 62.1 %all-to-all-done.refs_1_ = bf16[64,168,128]{2,1,0:T(8,128)(2,1)} async-done(((bf16[64,168,128]{2,1,0:T(8,128)(2,1)}), bf16[64,168,128]{2,1,0:T(8,128)(2,1)}, u32[]{:S(2)}, u32[]{:S(2)}) %all-to-all-start) | async-done | bytes 2752544 | tf_op jit(solution)/shard_map/all_to_all | solution.py:265
  86.0 5.1 %collective-permute-start = (bf16[64,168,128]{2,1,0:T(8,128)(2,1)}, bf16[64,168,128]{2,1,0:T(8,128)(2,1)}, u32[]{:S(2)}, u32[]{:S(2)}) collective-permute-start(bf16[64,168,128]{2,1,0:T(8,128)(2,1)} %all-to-all-done.refs_1_), channel_id=1, source_target_pairs={{0,3},{1,0},{2,1},{3,2},{4,7},{5,4},{6,5},{7,6},{8,11},{9,8},{10,9... | collective-permute-start | bytes 8257544 | tf_op jit(solution)/shard_map/ppermute | solution.py:262
  91.1 2.7 convert_reduce_fusion.refs_0_
  93.9 8.2 %half.4 = bf16[64,1,40,384]{3,2,1,0:T(8,128)(2,1)} custom-call(s32[64]{0:T(128)} %convert_reduce_fusion.refs_0_, bf16[64,168,128]{2,1,0:T(8,128)(2,1)} %all-to-all-done.refs_1_, bf16[8,512,384]{2,1,0:T(8,128)(2,1)} %bitcast.28), custom_call_target="tpu_custom_call" | custom-call | flops 8053063680 | bytes 7733248 | tf_op jit(solution)/shard_map/half/pallas_call | solution.py:176
  102.0 6.6 %all-to-all-start.1 = ((bf16[64,1,40,384]{3,2,1,0:T(8,128)(2,1)}), bf16[64,1,40,384]{3,2,1,0:T(8,128)(2,1)S(1)}, u32[]{:S(2)}, u32[]{:S(2)}) async-start(bf16[64,1,40,384]{3,2,1,0:T(8,128)(2,1)} %half.4), calls=%async_computation.1 | async-start | bytes 3932160 | tf_op jit(solution)/shard_map/all_to_all | solution.py:265
  108.6 45.0 %collective-permute-done.1.refs_3_ = bf16[64,168,128]{2,1,0:T(8,128)(2,1)} collective-permute-done((bf16[64,168,128]{2,1,0:T(8,128)(2,1)}, bf16[64,168,128]{2,1,0:T(8,128)(2,1)}, u32[]{:S(2)}, u32[]{:S(2)}) %collective-permute-start.1) | collective-permute-done | bytes 2752544 | tf_op jit(solution)/shard_map/ppermute | solution.py:262
  153.6 2.7 fusion.4.refs_1_
  156.3 2.7 fusion.5.refs_0_
  159.0 12.0 %half.3 = bf16[64,2,40,384]{3,2,1,0:T(8,128)(2,1)} custom-call(s32[64]{0:T(128)} %fusion.5.refs_0_, s32[64]{0:T(128)} %fusion.4.refs_1_, bf16[64,168,128]{2,1,0:T(8,128)(2,1)} %collective-permute-done.refs_2_, bf16[64,168,128]{2,1,0:T(8,128)(2,1)} %collective-permute-done.1.refs_3_, bf16[8,512,384]{2,1,0:T(8,128)(2,1)} %bitcast.29), custom_call_target="tpu_custom_call" | custom-call | flops 16106127360 | bytes 12320768 | tf_op jit(solution)/shard_map/half/pallas_call | solution.py:176
  171.0 1.3 copy-done.1
  172.3 7.2 %all-to-all-start.2 = ((bf16[64,2,40,384]{3,2,1,0:T(8,128)(2,1)}), bf16[64,2,40,384]{3,2,1,0:T(8,128)(2,1)}, u32[]{:S(2)}, u32[]{:S(2)}) async-start(bf16[64,2,40,384]{3,2,1,0:T(8,128)(2,1)} %half.3), calls=%async_computation.2 | async-start | bytes 7864320 | tf_op jit(solution)/shard_map/all_to_all | solution.py:265
  179.6 62.5 %collective-permute-done.2.refs_1_ = bf16[64,168,128]{2,1,0:T(8,128)(2,1)S(1)} collective-permute-done((bf16[64,168,128]{2,1,0:T(8,128)(2,1)}, bf16[64,168,128]{2,1,0:T(8,128)(2,1)S(1)}, u32[]{:S(2)}, u32[]{:S(2)}) %collective-permute-start.2) | collective-permute-done | bytes 2752544 | tf_op jit(solution)/shard_map/ppermute | solution.py:262
  242.1 1.8 fusion.3.refs_0_
  243.9 7.4 %half.5 = bf16[64,1,40,384]{3,2,1,0:T(8,128)(2,1)} custom-call(s32[64]{0:T(128)} %fusion.3.refs_0_, bf16[64,168,128]{2,1,0:T(8,128)(2,1)} %copy-done.8, bf16[8,512,384]{2,1,0:T(8,128)(2,1)} %bitcast.30), custom_call_target="tpu_custom_call" | custom-call | flops 8053063680 | bytes 7733248 | tf_op jit(solution)/shard_map/half/pallas_call | solution.py:176
  251.3 18.5 %all-to-all-done.2 = bf16[64,2,40,384]{3,2,1,0:T(8,128)(2,1)} async-done(((bf16[64,2,40,384]{3,2,1,0:T(8,128)(2,1)}), bf16[64,2,40,384]{3,2,1,0:T(8,128)(2,1)}, u32[]{:S(2)}, u32[]{:S(2)}) %all-to-all-start.2) | async-done | bytes 3932192 | tf_op jit(solution)/shard_map/all_to_all | solution.py:265
  269.8 5.7 %all-to-all-start.3 = ((bf16[64,1,40,384]{3,2,1,0:T(8,128)(2,1)}), bf16[64,1,40,384]{3,2,1,0:T(8,128)(2,1)S(1)}, u32[]{:S(2)}, u32[]{:S(2)}) async-start(bf16[64,1,40,384]{3,2,1,0:T(8,128)(2,1)} %half.5), calls=%async_computation.3 | async-start | bytes 3932160 | tf_op jit(solution)/shard_map/all_to_all | solution.py:265
  275.7 0.7 gather_fusion
  276.4 0.7 gather_fusion.1
  277.1 0.6 compare_select_fusion.5.place
  277.7 46.0 %all-to-all-done.3 = bf16[64,1,40,384]{3,2,1,0:T(8,128)(2,1)S(1)} async-done(((bf16[64,1,40,384]{3,2,1,0:T(8,128)(2,1)}), bf16[64,1,40,384]{3,2,1,0:T(8,128)(2,1)S(1)}, u32[]{:S(2)}, u32[]{:S(2)}) %all-to-all-start.3) | async-done | bytes 1966112 | tf_op jit(solution)/shard_map/all_to_all | solution.py:265
  323.8 1.3 copy-done.2
  325.1 8.2 %exchange.1 = f32[96,40,40]{2,1,0:T(8,128)} custom-call(s32[192]{0:T(256)} %compare_select_fusion.5.place, bf16[64,40,384]{2,1,0:T(8,128)(2,1)} %bitcast.25, bf16[128,40,384]{2,1,0:T(8,128)(2,1)} %bitcast.5.second, bf16[64,40,384]{2,1,0:T(8,128)(2,1)} %bitcast.26), custom_call_target="tpu_custom_call" | custom-call | tf_op jit(solution)/shard_map/exchange/pallas_call | solution.py:230
  333.3 2.1 reshape.42
  335.6 2.7 collective-permute-start.4
  338.3 0.2 broadcast_add_fusion
  338.5 0.2 add.125
  338.7 3.4 collective-permute-done.3
  342.1 2.4 collective-permute-done.5
  344.5 0.8 fusion.2
  (28 shorter events, 0.4 us)
Async XLA Ops:
  0.0 275.7 %copy-start = (f32[512]{0:T(512)S(1)}, f32[512]{0:T(512)}, u32[]{:S(2)}) copy-start(f32[512]{0:T(512)} %param.13) | copy-start | bytes 6148
  7.6 13.4 %copy-start.3 = (bf16[8,384,512]{2,1,0:T(8,128)(2,1)S(1)}, bf16[8,384,512]{2,1,0:T(8,128)(2,1)}, u32[]{:S(2)}) copy-start(bf16[8,384,512]{2,1,0:T(8,128)(2,1)} %param.7) | copy-start | bytes 9437188
  7.6 78.4 %all-to-all-start = ((bf16[64,168,128]{2,1,0:T(8,128)(2,1)}), bf16[64,168,128]{2,1,0:T(8,128)(2,1)}, u32[]{:S(2)}, u32[]{:S(2)}) async-start(bf16[64,168,128]{2,1,0:T(8,128)(2,1)} %get-tuple-element.16), calls=%async_computation | async-start | bytes 5505024 | tf_op jit(solution)/shard_map/all_to_all | solution.py:265
  86.0 70.3 %collective-permute-start = (bf16[64,168,128]{2,1,0:T(8,128)(2,1)}, bf16[64,168,128]{2,1,0:T(8,128)(2,1)}, u32[]{:S(2)}, u32[]{:S(2)}) collective-permute-start(bf16[64,168,128]{2,1,0:T(8,128)(2,1)} %all-to-all-done.refs_1_), channel_id=1, source_target_pairs={{0,3},{1,0},{2,1},{3,2},{4,7},{5,4},{6,5},{7,6},{8,11},{9,8},{10,9... | collective-permute-start | bytes 8257544 | tf_op jit(solution)/shard_map/ppermute | solution.py:262
  91.1 62.5 %collective-permute-start.1 = (bf16[64,168,128]{2,1,0:T(8,128)(2,1)}, bf16[64,168,128]{2,1,0:T(8,128)(2,1)}, u32[]{:S(2)}, u32[]{:S(2)}) collective-permute-start(bf16[64,168,128]{2,1,0:T(8,128)(2,1)} %all-to-all-done.refs_1_), channel_id=1, source_target_pairs={{0,1},{1,2},{2,3},{3,0},{4,5},{5,6},{6,7},{7,4},{8,9},{9,10},{10,1... | collective-permute-start | bytes 8257544 | tf_op jit(solution)/shard_map/ppermute | solution.py:262
  102.0 69.0 %all-to-all-start.1 = ((bf16[64,1,40,384]{3,2,1,0:T(8,128)(2,1)}), bf16[64,1,40,384]{3,2,1,0:T(8,128)(2,1)S(1)}, u32[]{:S(2)}, u32[]{:S(2)}) async-start(bf16[64,1,40,384]{3,2,1,0:T(8,128)(2,1)} %half.4), calls=%async_computation.1 | async-start | bytes 3932160 | tf_op jit(solution)/shard_map/all_to_all | solution.py:265
  171.0 1.3 copy-start.1
  172.3 97.5 %all-to-all-start.2 = ((bf16[64,2,40,384]{3,2,1,0:T(8,128)(2,1)}), bf16[64,2,40,384]{3,2,1,0:T(8,128)(2,1)}, u32[]{:S(2)}, u32[]{:S(2)}) async-start(bf16[64,2,40,384]{3,2,1,0:T(8,128)(2,1)} %half.3), calls=%async_computation.2 | async-start | bytes 7864320 | tf_op jit(solution)/shard_map/all_to_all | solution.py:265
  179.5 62.6 %collective-permute-start.2 = (bf16[64,168,128]{2,1,0:T(8,128)(2,1)}, bf16[64,168,128]{2,1,0:T(8,128)(2,1)S(1)}, u32[]{:S(2)}, u32[]{:S(2)}) collective-permute-start(bf16[64,168,128]{2,1,0:T(8,128)(2,1)} %all-to-all-done.refs_1_), channel_id=1, source_target_pairs={{0,2},{1,3},{2,0},{3,1},{4,6},{5,7},{6,4},{7,5},{8,10},{9,11},{10,... | collective-permute-start | bytes 8257544 | tf_op jit(solution)/shard_map/ppermute | solution.py:262
  242.1 1.8 copy-start.8
  251.3 24.3 %copy-start.6 = (s32[96,2]{0,1:T(2,128)S(1)}, s32[96,2]{0,1:T(2,128)}, u32[]{:S(2)}) copy-start(s32[96,2]{0,1:T(2,128)} %param.9) | copy-start | bytes 2308
  251.3 25.9 %copy-start.7 = (s32[192]{0:T(256)S(1)}, s32[192]{0:T(256)}, u32[]{:S(2)}) copy-start(s32[192]{0:T(256)} %get-tuple-element.15) | copy-start | bytes 2308
  269.8 54.0 %all-to-all-start.3 = ((bf16[64,1,40,384]{3,2,1,0:T(8,128)(2,1)}), bf16[64,1,40,384]{3,2,1,0:T(8,128)(2,1)S(1)}, u32[]{:S(2)}, u32[]{:S(2)}) async-start(bf16[64,1,40,384]{3,2,1,0:T(8,128)(2,1)} %half.5), calls=%async_computation.3 | async-start | bytes 3932160 | tf_op jit(solution)/shard_map/all_to_all | solution.py:265
  323.8 1.3 copy-start.2
  333.3 5.0 %copy-start.5 = (f32[24,40]{1,0:T(8,128)S(1)}, f32[24,40]{1,0:T(8,128)}, u32[]{:S(2)}) copy-start(f32[24,40]{1,0:T(8,128)} %param.12) | copy-start | bytes 11524
  333.3 11.2 %copy-start.4 = (bf16[24,1600]{1,0:T(8,128)(2,1)S(1)}, bf16[24,1600]{1,0:T(8,128)(2,1)}, u32[]{:S(2)}) copy-start(bf16[24,1600]{1,0:T(8,128)(2,1)} %param.11) | copy-start | bytes 230404
  335.5 6.6 %collective-permute-start.3 = (f32[24,1600]{1,0:T(8,128)S(1)}, f32[24,1600]{1,0:T(8,128)S(1)}, u32[]{:S(2)}, u32[]{:S(2)}) collective-permute-start(f32[24,1600]{1,0:T(8,128)S(1)} %get-tuple-element.25), channel_id=1, source_target_pairs={{0,1},{1,2},{2,3},{3,0},{4,5},{5,6},{6,7},{7,4},{8,9},{9,10},{10,1... | collective-permute-start | bytes 460808 | tf_op jit(solution)/shard_map/ppermute | solution.py:262
  335.6 6.5 %collective-permute-start.4 = (f32[24,1600]{1,0:T(8,128)S(1)}, f32[24,1600]{1,0:T(8,128)S(1)}, u32[]{:S(2)}, u32[]{:S(2)}) collective-permute-start(f32[24,1600]{1,0:T(8,128)S(1)} %get-tuple-element.27), channel_id=1, source_target_pairs={{0,3},{1,0},{2,1},{3,2},{4,7},{5,4},{6,5},{7,6},{8,11},{9,8},{10,9... | collective-permute-start | bytes 460808 | tf_op jit(solution)/shard_map/ppermute | solution.py:262
  338.3 6.2 %collective-permute-start.5 = (f32[24,1600]{1,0:T(8,128)S(1)}, f32[24,1600]{1,0:T(8,128)S(1)}, u32[]{:S(2)}, u32[]{:S(2)}) collective-permute-start(f32[24,1600]{1,0:T(8,128)S(1)} %get-tuple-element.26), channel_id=1, source_target_pairs={{0,2},{1,3},{2,0},{3,1},{4,6},{5,7},{6,4},{7,5},{8,10},{9,11},{10,... | collective-permute-start | bytes 460808 | tf_op jit(solution)/shard_map/ppermute | solution.py:262

commit v3 on v2

v3 whole, which is shorter than its diff:
```python
import functools

import jax
import jax.numpy as jnp
from jax import lax
from jax.experimental import pallas as pl
from jax.experimental.pallas import tpu as pltpu
from jax.sharding import PartitionSpec as P

CAP = 4
TOGETHER = 8
WEIGHT = 8


LANES = 128
SPARE = 8


def pieces(npno, npao):
    whole = npno // 16 * 16
    blocks = npao // LANES
    cuts = []
    for c in range(blocks):
        lanes = slice(c * LANES, (c + 1) * LANES)
        cuts.append((slice(0, whole), lanes, slice(c * whole, (c + 1) * whole)))
        if npno > whole:
            at = blocks * whole + c * (npno - whole)
            cuts.append((slice(whole, npno), lanes, slice(at, at + npno - whole)))
    return cuts


def route_kernel(
    keeper, orbitals, place, plane, vectors, sent, slot, count, source, row, held, record, sems
):
    owners, npno, npao = held.shape
    pairs = orbitals.shape[1]
    together = 4

    def clear(o, _):
        count[o] = 0
        source[o] = 0
        row[o] = keeper
        return 0

    lax.fori_loop(0, owners, clear, 0, unroll=8)
    mine = plane[0]

    def some(g, _):
        for k in range(together):
            q = g * together + k
            for side in range(2):
                at = place[orbitals[side, q]]
                owner = at // keeper
                position = count[owner]
                count[owner] = position + 1
                slot[q * 2 + side] = position * owners + owner
                to = owner + jnp.where(position == mine, 0, owners)
                source[to] = q * 2 + side
                row[to] = at % keeper
        return 0

    lax.fori_loop(0, pairs // together, some, 0)

    def fetch(o, _):
        pltpu.make_async_copy(vectors.at[source[o]], held.at[o], sems.at[0]).start()
        return 0

    lax.fori_loop(0, owners, fetch, 0, unroll=8)
    pltpu.make_async_copy(vectors.at[pl.ds(0, owners)], held, sems.at[0]).wait()

    def lay(o, _):
        for rows, lanes, at in pieces(npno, npao):
            record[o, at, :] = held[o, rows, lanes]
        number = jnp.full((SPARE, LANES), row[o], jnp.int32).astype(jnp.float32)
        record[o, npno * npao // LANES :, :] = number.astype(record.dtype)
        return 0

    lax.fori_loop(0, owners, lay, 0, unroll=2)
    out = pltpu.make_async_copy(record, sent, sems.at[1])
    out.start()
    out.wait()


def route(orbitals, orbital_place, plane, vectors, owners, keeper):
    entries, npno, npao = vectors.shape
    depth = npno * npao // LANES + SPARE
    smem = pl.BlockSpec(memory_space=pltpu.SMEM)
    hbm = pl.BlockSpec(memory_space=pltpu.HBM)
    return pl.pallas_call(
        functools.partial(route_kernel, keeper),
        out_shape=(
            jax.ShapeDtypeStruct((owners, depth, LANES), vectors.dtype),
            jax.ShapeDtypeStruct((entries,), jnp.int32),
        ),
        in_specs=[smem, smem, smem, hbm],
        out_specs=(hbm, smem),
        scratch_shapes=[
            pltpu.SMEM((owners,), jnp.int32),
            pltpu.SMEM((2 * owners,), jnp.int32),
            pltpu.SMEM((2 * owners,), jnp.int32),
            pltpu.VMEM((owners, npno, npao), vectors.dtype),
            pltpu.VMEM((owners, depth, LANES), vectors.dtype),
            pltpu.SemaphoreType.DMA((2,)),
        ],
        compiler_params=pltpu.CompilerParams(vmem_limit_bytes=60 * 2**20),
        name="route",
    )(orbitals, orbital_place, plane, vectors)


def half_kernel(shares, record, *refs):
    ints, out = refs[:shares], refs[shares]
    held, order, count, number, row, stacked, blocks, halves, sems = refs[shares + 1 :]
    items, _, npno, naux = out.shape
    keeper, _, npao = blocks.shape
    deep = stacked.shape[1]
    whole = pltpu.make_async_copy(record, held, sems.at[0])
    whole.start()
    loads = [
        pltpu.make_async_copy(
            ints[k].at[o], blocks.at[o, pl.ds(k * naux, naux)], sems.at[2 + shares + o * shares + k]
        )
        for o in range(keeper)
        for k in range(shares)
    ]
    for load in loads:
        load.start()
    stacked[...] = jnp.zeros_like(stacked)
    whole.wait()

    tile = held[:, npno * npao // LANES :, :].astype(jnp.float32)
    own = lax.broadcasted_iota(jnp.int32, tile.shape, 0)
    lane = lax.broadcasted_iota(jnp.int32, tile.shape, 2)
    number[...] = jnp.sum(jnp.where(own == lane, tile, 0.0), axis=0).astype(jnp.int32)
    move = pltpu.make_async_copy(number, row, sems.at[1])
    move.start()
    move.wait()
    for o in range(keeper + 1):
        count[o] = 0

    def sort(e, _):
        o = row[0, e]
        n = count[o]
        order[o * items + n] = e
        count[o] = n + 1
        return 0

    lax.fori_loop(0, items, sort, 0, unroll=8)

    for o in range(keeper):
        for k in range(shares):
            loads[o * shares + k].wait()
        n = count[o]

        def block(b, _):
            ids = [
                order[o * items + jnp.minimum(b * TOGETHER + t, n - 1)] for t in range(TOGETHER)
            ]
            for t in range(TOGETHER):
                for rows, lanes, at in pieces(npno, npao):
                    stacked[t, rows, lanes] = held[ids[t], at, :]
            value = lax.dot_general(
                stacked[...].reshape(TOGETHER * deep, npao),
                blocks[o],
                (((1,), (1,)), ((), ())),
                preferred_element_type=jnp.float32,
            ).astype(out.dtype)
            for t in range(TOGETHER):
                for k in range(shares):
                    halves[k, ids[t]] = value[
                        t * deep : t * deep + npno, k * naux : (k + 1) * naux
                    ]
            return 0

        lax.fori_loop(0, (n + TOGETHER - 1) // TOGETHER, block, 0)

    backs = [
        pltpu.make_async_copy(halves.at[k], out.at[:, k], sems.at[2 + k]) for k in range(shares)
    ]
    for back in backs:
        back.start()
    for back in backs:
        back.wait()


def half(record, ints, npno, weight):
    shares = len(ints)
    keeper, naux, npao = ints[0].shape
    items = record.shape[0]
    hbm = pl.BlockSpec(memory_space=pltpu.HBM)
    return pl.pallas_call(
        functools.partial(half_kernel, shares),
        out_shape=jax.ShapeDtypeStruct((items, shares, npno, naux), jnp.bfloat16),
        in_specs=[hbm] * (1 + shares),
        out_specs=hbm,
        scratch_shapes=[
            pltpu.VMEM(record.shape, record.dtype),
            pltpu.SMEM(((keeper + 1) * items,), jnp.int32),
            pltpu.SMEM((keeper + 1,), jnp.int32),
            pltpu.VMEM((SPARE, LANES), jnp.int32),
            pltpu.SMEM((SPARE, LANES), jnp.int32),
            pltpu.VMEM((TOGETHER, -(-npno // 16) * 16, npao), jnp.bfloat16),
            pltpu.VMEM((keeper, shares * naux, npao), jnp.bfloat16),
            pltpu.VMEM((shares, items, npno, naux), jnp.bfloat16),
            pltpu.SemaphoreType.DMA((2 + shares + keeper * shares,)),
        ],
        compiler_params=pltpu.CompilerParams(vmem_limit_bytes=60 * 2**20),
        cost_estimate=pl.CostEstimate(
            flops=weight * 2 * shares * items * npno * npao * naux,
            bytes_accessed=2 * shares * (keeper * npao * naux + items * npno * (npao + naux)),
            transcendentals=0,
        ),
        name="half",
    )(record, *ints)


def exchange_kernel(place, *refs):
    out, halves, sems = refs[CAP:]
    owners = refs[0].shape[0]
    copies = [
        pltpu.make_async_copy(refs[k], halves.at[pl.ds(k * owners, owners)], sems.at[k])
        for k in range(CAP)
    ]
    for copy in copies:
        copy.start()
    for copy in copies:
        copy.wait()
    group = 16

    def some(g, _):
        for k in range(group):
            q = g * group + k
            out[q] = lax.dot_general(
                halves[place[2 * q]],
                halves[place[2 * q + 1]],
                (((1,), (1,)), ((), ())),
                preferred_element_type=jnp.float32,
            )
        return 0

    lax.fori_loop(0, out.shape[0] // group, some, 0)


def exchange_of(place, parts):
    owners, npno, naux = parts[0].shape
    pairs = place.shape[0] // 2
    hbm = pl.BlockSpec(memory_space=pltpu.HBM)
    return pl.pallas_call(
        exchange_kernel,
        out_shape=jax.ShapeDtypeStruct((pairs, npno, npno), jnp.float32),
        in_specs=[pl.BlockSpec(memory_space=pltpu.SMEM)] + [hbm] * CAP,
        out_specs=pl.BlockSpec(memory_space=pltpu.VMEM),
        scratch_shapes=[
            pltpu.VMEM((CAP * owners, npno, naux), jnp.bfloat16),
            pltpu.SemaphoreType.DMA((CAP,)),
        ],
        compiler_params=pltpu.CompilerParams(vmem_limit_bytes=60 * 2**20),
        name="exchange",
    )(place, *parts)


def body(
    ints_block,
    pair_vectors,
    pair_orbitals,
    orbital_place,
    amplitudes,
    pno_energy,
    occupied_fock_diagonal,
):
    n_orb = lax.axis_size("orb")
    n_rep = lax.axis_size("rep")
    rep = lax.axis_index("rep")
    keeper, naux, npao = ints_block.shape
    pair_dev = pair_vectors.shape[0]
    npno = pair_vectors.shape[2]
    vectors = pair_vectors.reshape(2 * pair_dev, npno, npao)

    def shifted(value, by):
        return lax.ppermute(value, "rep", [(i, (i + by) % n_rep) for i in range(n_rep)])

    def there(value):
        return lax.all_to_all(value, "orb", split_axis=0, concat_axis=0, tiled=True)

    sent, slot = route(
        pair_orbitals.T, orbital_place, rep.reshape(1).astype(jnp.int32), vectors, n_orb, keeper
    )
    own = there(sent)

    above = shifted(ints_block, n_rep - 1)
    below = shifted(ints_block, 1)
    opposite = shifted(own, 2)

    first = there(half(own, (ints_block,), npno, WEIGHT))
    near, first = lax.optimization_barrier((half(own, (above, below), npno, WEIGHT), first))
    near = there(near)
    far, near = lax.optimization_barrier((half(opposite, (ints_block,), npno, WEIGHT), near))
    far = there(far)

    parts = (
        first[:, 0],
        shifted(near[:, 1], n_rep - 1),
        far[:, 0],
        shifted(near[:, 0], 1),
    )
    place = (slot // n_orb - rep) % n_rep * n_orb + slot % n_orb
    partial_value = exchange_of(place, parts)
    mine = pair_dev // n_rep
    partial_value = partial_value.reshape(n_rep, mine, npno * npno)
    exchange = lax.dynamic_index_in_dim(partial_value, rep, 0, keepdims=False)
    for by in (1, n_rep - 1, 2):
        leaving = lax.dynamic_index_in_dim(partial_value, (rep + by) % n_rep, 0, keepdims=False)
        exchange = exchange + shifted(leaving, by)
    own_orbs = lax.dynamic_slice_in_dim(pair_orbitals, rep * mine, mine, 0)
    first_fock = occupied_fock_diagonal[own_orbs[:, 0]]
    second_fock = occupied_fock_diagonal[own_orbs[:, 1]]
    gap = pno_energy[:, :, None] + pno_energy[:, None, :] - (first_fock + second_fock)[:, None, None]
    return exchange + gap.reshape(mine, npno * npno) * amplitudes.astype(jnp.float32)


def solution(mesh):
    placed = (
        P("orb", "rep", None),
        P("orb", None, None, None),
        P("orb", None),
        P(),
        P(("orb", "rep"), None),
        P(("orb", "rep"), None),
        P(),
    )
    return jax.shard_map(
        body, mesh=mesh, in_specs=placed, out_specs=P(("orb", "rep"), None), check_vma=False
    )
```

time: 346 us -> 330 us (0.954)
  waiting for transfers between devices: 240 us -> 225 us
  other arithmetic: 11.4 us -> 1.54 us
  starting transfers between devices: 40.9 us -> 45.8 us
  local copies, waits for them, and re-layouts: 9.34 us -> 14.2 us
    all_to_all x4, waiting for transfers between devices: 127 us -> 114 us  [there(): return lax.all_to_all(value, 'orb', split_axis=0, concat_axis=0, tiled=True)]
    convert_element_type x4 -> x0, other arithmetic: 9.82 us -> none  [row_of(): return record[:, npno * npao // LANES, 0].astype(jnp.int32)]
    ppermute x6 -> x8, starting transfers between devices: 7.97 us -> 15.2 us  [shifted(): lax.ppermute(value, 'rep', [(i, (i + by) % n_rep) for i in range(n_rep)])]
    squeeze x0 -> x1, local copies, waits for them, and re-layouts: none -> 4.55 us  [body(): near[:, 0]]
    ppermute x6 -> x8, waiting for transfers between devices: 113 us -> 111 us  [shifted(): lax.ppermute(value, 'rep', [(i, (i + by) % n_rep) for i in range(n_rep)])]
  transfers between devices with their start and end apart: 10 -> 12, of which waited for: 7 -> 9; matrix products, arithmetic and copies ran while one was open for 4% -> 2% of each run, Pallas kernels for 8% -> 9%
where the time goes in v3:
time: 330 us
  waiting for transfers between devices  225 us (68%)
  starting transfers between devices  45.8 us (14%)
  Pallas kernels  43.2 us (13%)
  local copies, waits for them, and re-layouts  14.2 us (4%)
    all_to_all x4, waiting for transfers between devices, there(): return lax.all_to_all(value, 'orb', split_axis=0, concat_axis=0, tiled=True)  114 us
    ppermute x8, waiting for transfers between devices, shifted(): lax.ppermute(value, 'rep', [(i, (i + by) % n_rep) for i in range(n_rep)])  111 us
    all_to_all x4, starting transfers between devices, there(): return lax.all_to_all(value, 'orb', split_axis=0, concat_axis=0, tiled=True)  30.6 us
    pallas_call x3, Pallas kernels, half(): pl.pallas_call(functools.partial(half_kernel, shares), out_shape=jax.Shap...  28.3 us
    ppermute x8, starting transfers between devices, shifted(): lax.ppermute(value, 'rep', [(i, (i + by) % n_rep) for i in range(n_rep)])  15.2 us
    pallas_call x1, Pallas kernels, route(): pl.pallas_call(functools.partial(route_kernel, keeper), out_shape=(jax.Sh...  7.54 us
    pallas_call x1, Pallas kernels, exchange_of(): pl.pallas_call(exchange_kernel, out_shape=jax.ShapeDtypeStruct((pairs, np...  7.42 us
  transfers between devices with their start and end apart: 12, of which 9 were waited for; matrix products, arithmetic and copies ran while one was open for 2% of the time, Pallas kernels for 9%

profile of v3, /device:TPU:1, one launch (start us, length us, event | category | flops | bytes accessed | tf_op | source)
XLA Modules:
  0.0 329.9 jit_solution(14096710881914362723)
XLA Ops:
  0.0 7.5 %route.1 = (bf16[64,168,128]{2,1,0:T(8,128)(2,1)}, s32[192]{0:T(256)}) custom-call(s32[2,96]{1,0:T(2,128)} %bitcast.30, s32[512]{0:T(512)} %place.1, s32[1]{0:T(128)} %bitcast.1.plane, bf16[192,40,512]{2,1,0:T(8,128)(2,1)} %bitcast.29), custom_call_target="tpu_custom_call" | custom-call | tf_op jit(solution)/shard_map/route/pallas_call | solution.py:89
  7.6 13.0 %all-to-all-start = ((bf16[64,168,128]{2,1,0:T(8,128)(2,1)}), bf16[64,168,128]{2,1,0:T(8,128)(2,1)S(1)}, u32[]{:S(2)}, u32[]{:S(2)}) async-start(bf16[64,168,128]{2,1,0:T(8,128)(2,1)} %get-tuple-element.12), calls=%async_computation | async-start | bytes 5505024 | tf_op jit(solution)/shard_map/all_to_all | solution.py:282
  20.6 5.2 %collective-permute-start = (bf16[8,384,512]{2,1,0:T(8,128)(2,1)}, bf16[8,384,512]{2,1,0:T(8,128)(2,1)}, u32[]{:S(2)}, u32[]{:S(2)}) collective-permute-start(bf16[8,384,512]{2,1,0:T(8,128)(2,1)} %refs_0_.3), channel_id=1, source_target_pairs={{0,3},{1,0},{2,1},{3,2},{4,7},{5,4},{6,5},{7,6},{8,11},{9,8},{10,9... | collective-permute-start | bytes 9437192 | tf_op jit(solution)/shard_map/ppermute | solution.py:279
  25.8 59.8 %all-to-all-done.record = bf16[64,168,128]{2,1,0:T(8,128)(2,1)S(1)} async-done(((bf16[64,168,128]{2,1,0:T(8,128)(2,1)}), bf16[64,168,128]{2,1,0:T(8,128)(2,1)S(1)}, u32[]{:S(2)}, u32[]{:S(2)}) %all-to-all-start) | async-done | bytes 2752544 | tf_op jit(solution)/shard_map/all_to_all | solution.py:282
  85.6 1.6 copy-done.3
  87.3 9.1 %half.4 = bf16[64,1,40,384]{3,2,1,0:T(8,128)(2,1)} custom-call(bf16[64,168,128]{2,1,0:T(8,128)(2,1)} %copy-done.3, bf16[8,384,512]{2,1,0:T(8,128)(2,1)} %refs_0_.3), custom_call_target="tpu_custom_call" | custom-call | flops 8053063680 | bytes 7733248 | tf_op jit(solution)/shard_map/half/pallas_call | solution.py:190
  96.4 5.7 %all-to-all-start.1 = ((bf16[64,1,40,384]{3,2,1,0:T(8,128)(2,1)}), bf16[64,1,40,384]{3,2,1,0:T(8,128)(2,1)S(1)}, u32[]{:S(2)}, u32[]{:S(2)}) async-start(bf16[64,1,40,384]{3,2,1,0:T(8,128)(2,1)} %half.4), calls=%async_computation.1 | async-start | bytes 3932160 | tf_op jit(solution)/shard_map/all_to_all | solution.py:282
  102.1 11.1 %half.3 = bf16[64,2,40,384]{3,2,1,0:T(8,128)(2,1)} custom-call(bf16[64,168,128]{2,1,0:T(8,128)(2,1)} %copy-done.3, bf16[8,384,512]{2,1,0:T(8,128)(2,1)} %collective-permute-done.refs_0_, bf16[8,384,512]{2,1,0:T(8,128)(2,1)} %collective-permute-done.1.refs_1_), custom_call_target="tpu_custom_call" | custom-call | flops 16106127360 | bytes 15466496 | tf_op jit(solution)/shard_map/half/pallas_call | solution.py:190
  113.2 37.1 %all-to-all-done.1 = bf16[64,1,40,384]{3,2,1,0:T(8,128)(2,1)S(1)} async-done(((bf16[64,1,40,384]{3,2,1,0:T(8,128)(2,1)}), bf16[64,1,40,384]{3,2,1,0:T(8,128)(2,1)S(1)}, u32[]{:S(2)}, u32[]{:S(2)}) %all-to-all-start.1) | async-done | bytes 1966112 | tf_op jit(solution)/shard_map/all_to_all | solution.py:282
  150.3 1.3 copy-done.1
  151.5 6.2 %all-to-all-start.2 = ((bf16[64,2,40,384]{3,2,1,0:T(8,128)(2,1)}), bf16[64,2,40,384]{3,2,1,0:T(8,128)(2,1)}, u32[]{:S(2)}, u32[]{:S(2)}) async-start(bf16[64,2,40,384]{3,2,1,0:T(8,128)(2,1)} %half.3), calls=%async_computation.2 | async-start | bytes 7864320 | tf_op jit(solution)/shard_map/all_to_all | solution.py:282
  157.8 3.5 %collective-permute-start.2 = (bf16[64,168,128]{2,1,0:T(8,128)(2,1)}, bf16[64,168,128]{2,1,0:T(8,128)(2,1)S(1)}, u32[]{:S(2)}, u32[]{:S(2)}) collective-permute-start(bf16[64,168,128]{2,1,0:T(8,128)(2,1)} %copy-done.3), channel_id=1, source_target_pairs={{0,2},{1,3},{2,0},{3,1},{4,6},{5,7},{6,4},{7,5},{8,10},{9,11},{10,... | collective-permute-start | bytes 8257544 | tf_op jit(solution)/shard_map/ppermute | solution.py:279
  161.3 59.9 %collective-permute-done.2.record = bf16[64,168,128]{2,1,0:T(8,128)(2,1)S(1)} collective-permute-done((bf16[64,168,128]{2,1,0:T(8,128)(2,1)}, bf16[64,168,128]{2,1,0:T(8,128)(2,1)S(1)}, u32[]{:S(2)}, u32[]{:S(2)}) %collective-permute-start.2) | collective-permute-done | bytes 2752544 | tf_op jit(solution)/shard_map/ppermute | solution.py:279
  221.2 1.6 copy-done.8
  222.8 8.1 %half.5 = bf16[64,1,40,384]{3,2,1,0:T(8,128)(2,1)} custom-call(bf16[64,168,128]{2,1,0:T(8,128)(2,1)} %copy-done.8, bf16[8,384,512]{2,1,0:T(8,128)(2,1)} %refs_0_.3), custom_call_target="tpu_custom_call" | custom-call | flops 8053063680 | bytes 7733248 | tf_op jit(solution)/shard_map/half/pallas_call | solution.py:190
  230.9 17.1 %all-to-all-done.2 = bf16[64,2,40,384]{3,2,1,0:T(8,128)(2,1)} async-done(((bf16[64,2,40,384]{3,2,1,0:T(8,128)(2,1)}), bf16[64,2,40,384]{3,2,1,0:T(8,128)(2,1)}, u32[]{:S(2)}, u32[]{:S(2)}) %all-to-all-start.2) | async-done | bytes 3932192 | tf_op jit(solution)/shard_map/all_to_all | solution.py:282
  248.0 5.7 %all-to-all-start.3 = ((bf16[64,1,40,384]{3,2,1,0:T(8,128)(2,1)}), bf16[64,1,40,384]{3,2,1,0:T(8,128)(2,1)S(1)}, u32[]{:S(2)}, u32[]{:S(2)}) async-start(bf16[64,1,40,384]{3,2,1,0:T(8,128)(2,1)} %half.5), calls=%async_computation.3 | async-start | bytes 3932160 | tf_op jit(solution)/shard_map/all_to_all | solution.py:282
  253.8 4.6 %slice_bitcast_fusion = (bf16[64,40,384]{2,1,0:T(8,128)(2,1)}, bf16[64,40,384]{2,1,0:T(8,128)(2,1)}) fusion(bf16[64,2,40,384]{3,2,1,0:T(8,128)(2,1)} %all-to-all-done.2), kind=kLoop, calls=%fused_computation.2 | loop fusion | bytes 7864320 | tf_op jit(solution)/shard_map/squeeze | solution.py:303
  258.4 4.7 %collective-permute-start.3 = (bf16[64,40,384]{2,1,0:T(8,128)(2,1)}, bf16[64,40,384]{2,1,0:T(8,128)(2,1)}, u32[]{:S(2)}, u32[]{:S(2)}) collective-permute-start(bf16[64,40,384]{2,1,0:T(8,128)(2,1)} %get-tuple-element.18), channel_id=1, source_target_pairs={{0,3},{1,0},{2,1},{3,2},{4,7},{5,4},{6,5},{7,6},{8,11},{9,8},{10,9... | collective-permute-start | bytes 5898248 | tf_op jit(solution)/shard_map/ppermute | solution.py:279
  263.2 0.6 fusion.4.place
  264.0 41.2 %collective-permute-done.3.refs_1_ = bf16[64,40,384]{2,1,0:T(8,128)(2,1)} collective-permute-done((bf16[64,40,384]{2,1,0:T(8,128)(2,1)}, bf16[64,40,384]{2,1,0:T(8,128)(2,1)}, u32[]{:S(2)}, u32[]{:S(2)}) %collective-permute-start.3) | collective-permute-done | bytes 1966112 | tf_op jit(solution)/shard_map/ppermute | solution.py:279
  305.2 3.1 collective-permute-done.4.refs_3_
  308.3 1.3 copy-done.2
  309.6 7.4 %exchange.1 = f32[96,40,40]{2,1,0:T(8,128)} custom-call(s32[192]{0:T(256)} %fusion.4.place, bf16[64,40,384]{2,1,0:T(8,128)(2,1)} %bitcast.27, bf16[64,40,384]{2,1,0:T(8,128)(2,1)} %collective-permute-done.3.refs_1_, bf16[64,40,384]{2,1,0:T(8,128)(2,1)} %bitcast.28, bf16[64,40,384]{2,1,0:T(8,128)(2,1)} %collective-permute-done.4.refs_3_), custom_call_target="tpu_custom_call" | custom-call | tf_op jit(solution)/shard_map/exchange/pallas_call | solution.py:247
  317.0 2.1 reshape.22
  319.3 1.5 collective-permute-start.6
  321.1 0.7 gather_fusion
  321.8 0.7 gather_fusion.1
  322.5 2.5 collective-permute-done.7
  325.0 1.5 collective-permute-done.6
  326.5 2.7 collective-permute-done.5
  329.2 0.8 fusion.2
  (28 shorter events, 0.7 us)
Async XLA Ops:
  0.0 321.1 %copy-start = (f32[512]{0:T(512)S(1)}, f32[512]{0:T(512)}, u32[]{:S(2)}) copy-start(f32[512]{0:T(512)} %param.13) | copy-start | bytes 6148
  7.6 78.1 %all-to-all-start = ((bf16[64,168,128]{2,1,0:T(8,128)(2,1)}), bf16[64,168,128]{2,1,0:T(8,128)(2,1)S(1)}, u32[]{:S(2)}, u32[]{:S(2)}) async-start(bf16[64,168,128]{2,1,0:T(8,128)(2,1)} %get-tuple-element.12), calls=%async_computation | async-start | bytes 5505024 | tf_op jit(solution)/shard_map/all_to_all | solution.py:282
  20.6 81.5 %collective-permute-start = (bf16[8,384,512]{2,1,0:T(8,128)(2,1)}, bf16[8,384,512]{2,1,0:T(8,128)(2,1)}, u32[]{:S(2)}, u32[]{:S(2)}) collective-permute-start(bf16[8,384,512]{2,1,0:T(8,128)(2,1)} %refs_0_.3), channel_id=1, source_target_pairs={{0,3},{1,0},{2,1},{3,2},{4,7},{5,4},{6,5},{7,6},{8,11},{9,8},{10,9... | collective-permute-start | bytes 9437192 | tf_op jit(solution)/shard_map/ppermute | solution.py:279
  25.8 76.3 %collective-permute-start.1 = (bf16[8,384,512]{2,1,0:T(8,128)(2,1)}, bf16[8,384,512]{2,1,0:T(8,128)(2,1)}, u32[]{:S(2)}, u32[]{:S(2)}) collective-permute-start(bf16[8,384,512]{2,1,0:T(8,128)(2,1)} %refs_0_.3), channel_id=1, source_target_pairs={{0,1},{1,2},{2,3},{3,0},{4,5},{5,6},{6,7},{7,4},{8,9},{9,10},{10,1... | collective-permute-start | bytes 9437192 | tf_op jit(solution)/shard_map/ppermute | solution.py:279
  85.6 1.6 copy-start.3
  96.4 53.9 %all-to-all-start.1 = ((bf16[64,1,40,384]{3,2,1,0:T(8,128)(2,1)}), bf16[64,1,40,384]{3,2,1,0:T(8,128)(2,1)S(1)}, u32[]{:S(2)}, u32[]{:S(2)}) async-start(bf16[64,1,40,384]{3,2,1,0:T(8,128)(2,1)} %half.4), calls=%async_computation.1 | async-start | bytes 3932160 | tf_op jit(solution)/shard_map/all_to_all | solution.py:282
  150.3 1.3 copy-start.1
  151.5 96.5 %all-to-all-start.2 = ((bf16[64,2,40,384]{3,2,1,0:T(8,128)(2,1)}), bf16[64,2,40,384]{3,2,1,0:T(8,128)(2,1)}, u32[]{:S(2)}, u32[]{:S(2)}) async-start(bf16[64,2,40,384]{3,2,1,0:T(8,128)(2,1)} %half.3), calls=%async_computation.2 | async-start | bytes 7864320 | tf_op jit(solution)/shard_map/all_to_all | solution.py:282
  157.8 63.4 %collective-permute-start.2 = (bf16[64,168,128]{2,1,0:T(8,128)(2,1)}, bf16[64,168,128]{2,1,0:T(8,128)(2,1)S(1)}, u32[]{:S(2)}, u32[]{:S(2)}) collective-permute-start(bf16[64,168,128]{2,1,0:T(8,128)(2,1)} %copy-done.3), channel_id=1, source_target_pairs={{0,2},{1,3},{2,0},{3,1},{4,6},{5,7},{6,4},{7,5},{8,10},{9,11},{10,... | collective-permute-start | bytes 8257544 | tf_op jit(solution)/shard_map/ppermute | solution.py:279
  221.2 1.6 copy-start.8
  248.0 60.2 %all-to-all-start.3 = ((bf16[64,1,40,384]{3,2,1,0:T(8,128)(2,1)}), bf16[64,1,40,384]{3,2,1,0:T(8,128)(2,1)S(1)}, u32[]{:S(2)}, u32[]{:S(2)}) async-start(bf16[64,1,40,384]{3,2,1,0:T(8,128)(2,1)} %half.5), calls=%async_computation.3 | async-start | bytes 3932160 | tf_op jit(solution)/shard_map/all_to_all | solution.py:282
  253.8 9.3 %copy-start.6 = (s32[96,2]{0,1:T(2,128)S(1)}, s32[96,2]{0,1:T(2,128)}, u32[]{:S(2)}) copy-start(s32[96,2]{0,1:T(2,128)} %param.9) | copy-start | bytes 2308
  253.8 9.4 %copy-start.7 = (s32[192]{0:T(256)S(1)}, s32[192]{0:T(256)}, u32[]{:S(2)}) copy-start(s32[192]{0:T(256)} %get-tuple-element.11) | copy-start | bytes 2308
  253.8 10.0 %copy-start.5 = (f32[24,40]{1,0:T(8,128)S(1)}, f32[24,40]{1,0:T(8,128)}, u32[]{:S(2)}) copy-start(f32[24,40]{1,0:T(8,128)} %param.12) | copy-start | bytes 11524
  258.4 46.8 %collective-permute-start.3 = (bf16[64,40,384]{2,1,0:T(8,128)(2,1)}, bf16[64,40,384]{2,1,0:T(8,128)(2,1)}, u32[]{:S(2)}, u32[]{:S(2)}) collective-permute-start(bf16[64,40,384]{2,1,0:T(8,128)(2,1)} %get-tuple-element.18), channel_id=1, source_target_pairs={{0,3},{1,0},{2,1},{3,2},{4,7},{5,4},{6,5},{7,6},{8,11},{9,8},{10,9... | collective-permute-start | bytes 5898248 | tf_op jit(solution)/shard_map/ppermute | solution.py:279
  263.1 45.1 %collective-permute-start.4 = (bf16[64,40,384]{2,1,0:T(8,128)(2,1)}, bf16[64,40,384]{2,1,0:T(8,128)(2,1)}, u32[]{:S(2)}, u32[]{:S(2)}) collective-permute-start(bf16[64,40,384]{2,1,0:T(8,128)(2,1)} %get-tuple-element.17), channel_id=1, source_target_pairs={{0,1},{1,2},{2,3},{3,0},{4,5},{5,6},{6,7},{7,4},{8,9},{9,10},{10,1... | collective-permute-start | bytes 5898248 | tf_op jit(solution)/shard_map/ppermute | solution.py:279
  308.3 1.3 copy-start.2
  317.0 12.2 %copy-start.4 = (bf16[24,1600]{1,0:T(8,128)(2,1)S(1)}, bf16[24,1600]{1,0:T(8,128)(2,1)}, u32[]{:S(2)}) copy-start(bf16[24,1600]{1,0:T(8,128)(2,1)} %param.11) | copy-start | bytes 230404
  319.2 5.8 %collective-permute-start.7 = (f32[24,1600]{1,0:T(8,128)S(1)}, f32[24,1600]{1,0:T(8,128)S(1)}, u32[]{:S(2)}, u32[]{:S(2)}) collective-permute-start(f32[24,1600]{1,0:T(8,128)S(1)} %get-tuple-element.20), channel_id=1, source_target_pairs={{0,2},{1,3},{2,0},{3,1},{4,6},{5,7},{6,4},{7,5},{8,10},{9,11},{10,... | collective-permute-start | bytes 460808 | tf_op jit(solution)/shard_map/ppermute | solution.py:279
  319.3 7.2 %collective-permute-start.6 = (f32[24,1600]{1,0:T(8,128)S(1)}, f32[24,1600]{1,0:T(8,128)S(1)}, u32[]{:S(2)}, u32[]{:S(2)}) collective-permute-start(f32[24,1600]{1,0:T(8,128)S(1)} %get-tuple-element.21), channel_id=1, source_target_pairs={{0,3},{1,0},{2,1},{3,2},{4,7},{5,4},{6,5},{7,6},{8,11},{9,8},{10,9... | collective-permute-start | bytes 460808 | tf_op jit(solution)/shard_map/ppermute | solution.py:279
  320.8 8.4 %collective-permute-start.5 = (f32[24,1600]{1,0:T(8,128)S(1)}, f32[24,1600]{1,0:T(8,128)S(1)}, u32[]{:S(2)}, u32[]{:S(2)}) collective-permute-start(f32[24,1600]{1,0:T(8,128)S(1)} %get-tuple-element.19), channel_id=1, source_target_pairs={{0,1},{1,2},{2,3},{3,0},{4,5},{5,6},{6,7},{7,4},{8,9},{9,10},{10,1... | collective-permute-start | bytes 460808 | tf_op jit(solution)/shard_map/ppermute | solution.py:279

commit v4 on v3

--- a/solution.py
+++ b/solution.py
@@ -9,7 +9,6 @@
 
 CAP = 4
 TOGETHER = 8
-WEIGHT = 8
 
 
 LANES = 128
@@ -107,90 +106,191 @@
     )(orbitals, orbital_place, plane, vectors)
 
 
-def half_kernel(shares, record, *refs):
-    ints, out = refs[:shares], refs[shares]
-    held, order, count, number, row, stacked, blocks, halves, sems = refs[shares + 1 :]
-    items, _, npno, naux = out.shape
-    keeper, _, npao = blocks.shape
+def sort_entries(held, number, row, count, order, sem, keeper, at):
+    items = held.shape[0]
+    tile = held[:, at:, :].astype(jnp.float32)
+    own = lax.broadcasted_iota(jnp.int32, tile.shape, 0)
+    lane = lax.broadcasted_iota(jnp.int32, tile.shape, 2)
+    number[...] = jnp.sum(jnp.where(own == lane, tile, 0.0), axis=0).astype(jnp.int32)
+    move = pltpu.make_async_copy(number, row, sem)
+    move.start()
+    move.wait()
+    for o in range(keeper + 1):
+        count[o] = 0
+
+    def sort(e, _):
+        o = row[0, e]
+        n = count[o]
+        order[o * items + n] = e
+        count[o] = n + 1
+        return 0
+
+    lax.fori_loop(0, items, sort, 0, unroll=8)
+
+
+def stack(stacked, held, ids, npno):
+    npao = stacked.shape[2]
+    for t, e in enumerate(ids):
+        for rows, lanes, at in pieces(npno, npao):
+            stacked[t, rows, lanes] = held[e, at, :]
+    return stacked[...].reshape(-1, npao)
+
+
+def near_kernel(
+    npno, record, own, above, below, out, rest_out,
+    held, order, count, number, row, stacked, blocks, halves, rest, sems,
+):
+    keeper, naux, npao = own.shape
+    items, tail, _ = rest.shape
+    main = npno - tail
     deep = stacked.shape[1]
     whole = pltpu.make_async_copy(record, held, sems.at[0])
     whole.start()
     loads = [
         pltpu.make_async_copy(
-            ints[k].at[o], blocks.at[o, pl.ds(k * naux, naux)], sems.at[2 + shares + o * shares + k]
+            share.at[o], blocks.at[o, pl.ds(k * naux, naux)], sems.at[4 + 3 * o + k]
         )
         for o in range(keeper)
-        for k in range(shares)
+        for k, share in enumerate((own, above, below))
     ]
     for load in loads:
         load.start()
     stacked[...] = jnp.zeros_like(stacked)
     whole.wait()
-
-    tile = held[:, npno * npao // LANES :, :].astype(jnp.float32)
-    own = lax.broadcasted_iota(jnp.int32, tile.shape, 0)
-    lane = lax.broadcasted_iota(jnp.int32, tile.shape, 2)
-    number[...] = jnp.sum(jnp.where(own == lane, tile, 0.0), axis=0).astype(jnp.int32)
-    move = pltpu.make_async_copy(number, row, sems.at[1])
-    move.start()
-    move.wait()
-    for o in range(keeper + 1):
-        count[o] = 0
-
-    def sort(e, _):
-        o = row[0, e]
+    sort_entries(held, number, row, count, order, sems.at[1], keeper, npno * npao // LANES)
+
+    def goes(e):
+        return pltpu.make_async_copy(halves.at[e], out.at[e], sems.at[2])
+
+    for o in range(keeper):
+        for k in range(3):
+            loads[3 * o + k].wait()
         n = count[o]
-        order[o * items + n] = e
-        count[o] = n + 1
-        return 0
-
-    lax.fori_loop(0, items, sort, 0, unroll=8)
-
+
+        def block(b, _):
+            at = [b * TOGETHER + t for t in range(TOGETHER)]
+            ids = [order[o * items + jnp.minimum(k, n - 1)] for k in at]
+            value = lax.dot_general(
+                stack(stacked, held, ids, npno),
+                blocks[o],
+                (((1,), (1,)), ((), ())),
+                preferred_element_type=jnp.float32,
+            ).astype(out.dtype)
+            for t, e in enumerate(ids):
+                rows = value[t * deep : t * deep + npno]
+                halves[e, :main] = rows[:main, :naux]
+                rest[e] = rows[main:, :naux]
+                halves[e, main : main + npno] = rows[:, naux : 2 * naux]
+                halves[e, main + npno :] = rows[:, 2 * naux :]
+            for k, e in zip(at, ids):
+
+                @pl.when(k < n)
+                def _():
+                    goes(e).start()
+
+            return 0
+
+        lax.fori_loop(0, (n + TOGETHER - 1) // TOGETHER, block, 0)
+
+    back = pltpu.make_async_copy(rest, rest_out, sems.at[3])
+    back.start()
+
+    def arrive(e, _):
+        goes(0).wait()
+        return 0
+
+    lax.fori_loop(0, items - count[keeper], arrive, 0)
+    back.wait()
+
+
+def near_halves(record, own, above, below, npno):
+    keeper, naux, npao = own.shape
+    items = record.shape[0]
+    tail = npno % 16
+    rows = 3 * npno - tail
+    hbm = pl.BlockSpec(memory_space=pltpu.HBM)
+    return pl.pallas_call(
+        functools.partial(near_kernel, npno),
+        out_shape=[
+            jax.ShapeDtypeStruct((items, rows, naux), jnp.bfloat16),
+            jax.ShapeDtypeStruct((items, tail, naux), jnp.bfloat16),
+        ],
+        in_specs=[hbm] * 4,
+        out_specs=[hbm] * 2,
+        scratch_shapes=[
+            pltpu.VMEM(record.shape, record.dtype),
+            pltpu.SMEM(((keeper + 1) * items,), jnp.int32),
+            pltpu.SMEM((keeper + 1,), jnp.int32),
+            pltpu.VMEM((SPARE, LANES), jnp.int32),
+            pltpu.SMEM((SPARE, LANES), jnp.int32),
+            pltpu.VMEM((TOGETHER, -(-npno // 16) * 16, npao), jnp.bfloat16),
+            pltpu.VMEM((keeper, 3 * naux, npao), jnp.bfloat16),
+            pltpu.VMEM((items, rows, naux), jnp.bfloat16),
+            pltpu.VMEM((items, tail, naux), jnp.bfloat16),
+            pltpu.SemaphoreType.DMA((4 + 3 * keeper,)),
+        ],
+        compiler_params=pltpu.CompilerParams(vmem_limit_bytes=60 * 2**20),
+        cost_estimate=pl.CostEstimate(
+            flops=6 * items * npno * npao * naux,
+            bytes_accessed=2 * (3 * keeper * npao * naux + items * npno * (npao + 3 * naux)),
+            transcendentals=0,
+        ),
+        name="near",
+    )(record, own, above, below)
+
+
+def far_kernel(npno, record, ints, rest_in, out, held, order, count, number, row, stacked, blocks, halves, rest, sems):
+    keeper, naux, npao = ints.shape
+    items = held.shape[0]
+    deep = stacked.shape[1]
+    whole = pltpu.make_async_copy(record, held, sems.at[0])
+    load = pltpu.make_async_copy(ints, blocks, sems.at[1])
+    rest_load = pltpu.make_async_copy(rest_in, rest, sems.at[2])
+    for copy in (whole, load, rest_load):
+        copy.start()
+    stacked[...] = jnp.zeros_like(stacked)
+    whole.wait()
+    sort_entries(held, number, row, count, order, sems.at[3], keeper, npno * npao // LANES)
+    load.wait()
     for o in range(keeper):
-        for k in range(shares):
-            loads[o * shares + k].wait()
         n = count[o]
 
         def block(b, _):
             ids = [
                 order[o * items + jnp.minimum(b * TOGETHER + t, n - 1)] for t in range(TOGETHER)
             ]
-            for t in range(TOGETHER):
-                for rows, lanes, at in pieces(npno, npao):
-                    stacked[t, rows, lanes] = held[ids[t], at, :]
             value = lax.dot_general(
-                stacked[...].reshape(TOGETHER * deep, npao),
+                stack(stacked, held, ids, npno),
                 blocks[o],
                 (((1,), (1,)), ((), ())),
                 preferred_element_type=jnp.float32,
             ).astype(out.dtype)
-            for t in range(TOGETHER):
-                for k in range(shares):
-                    halves[k, ids[t]] = value[
-                        t * deep : t * deep + npno, k * naux : (k + 1) * naux
-                    ]
+            for t, e in enumerate(ids):
+                halves[e, :npno] = value[t * deep : t * deep + npno]
             return 0
 
         lax.fori_loop(0, (n + TOGETHER - 1) // TOGETHER, block, 0)
 
-    backs = [
-        pltpu.make_async_copy(halves.at[k], out.at[:, k], sems.at[2 + k]) for k in range(shares)
-    ]
-    for back in backs:
-        back.start()
-    for back in backs:
-        back.wait()
-
-
-def half(record, ints, npno, weight):
-    shares = len(ints)
-    keeper, naux, npao = ints[0].shape
-    items = record.shape[0]
+    rest_load.wait()
+
+    def join(e, _):
+        halves[e, npno:] = rest[e]
+        return 0
+
+    lax.fori_loop(0, items, join, 0, unroll=8)
+    back = pltpu.make_async_copy(halves, out, sems.at[4])
+    back.start()
+    back.wait()
+
+
+def far_halves(record, ints, rest, npno):
+    keeper, naux, npao = ints.shape
+    items, tail, _ = rest.shape
     hbm = pl.BlockSpec(memory_space=pltpu.HBM)
     return pl.pallas_call(
-        functools.partial(half_kernel, shares),
-        out_shape=jax.ShapeDtypeStruct((items, shares, npno, naux), jnp.bfloat16),
-        in_specs=[hbm] * (1 + shares),
+        functools.partial(far_kernel, npno),
+        out_shape=jax.ShapeDtypeStruct((items, npno + tail, naux), jnp.bfloat16),
+        in_specs=[hbm] * 3,
         out_specs=hbm,
         scratch_shapes=[
             pltpu.VMEM(record.shape, record.dtype),
@@ -199,37 +299,71 @@
             pltpu.VMEM((SPARE, LANES), jnp.int32),
             pltpu.SMEM((SPARE, LANES), jnp.int32),
             pltpu.VMEM((TOGETHER, -(-npno // 16) * 16, npao), jnp.bfloat16),
-            pltpu.VMEM((keeper, shares * naux, npao), jnp.bfloat16),
-            pltpu.VMEM((shares, items, npno, naux), jnp.bfloat16),
-            pltpu.SemaphoreType.DMA((2 + shares + keeper * shares,)),
+            pltpu.VMEM(ints.shape, jnp.bfloat16),
+            pltpu.VMEM((items, npno + tail, naux), jnp.bfloat16),
+            pltpu.VMEM(rest.shape, jnp.bfloat16),
+            pltpu.SemaphoreType.DMA((5,)),
         ],
         compiler_params=pltpu.CompilerParams(vmem_limit_bytes=60 * 2**20),
         cost_estimate=pl.CostEstimate(
-            flops=weight * 2 * shares * items * npno * npao * naux,
-            bytes_accessed=2 * shares * (keeper * npao * naux + items * npno * (npao + naux)),
+            flops=16 * items * npno * npao * naux,
+            bytes_accessed=2 * (keeper * npao * naux + items * npno * (npao + naux)),
             transcendentals=0,
         ),
-        name="half",
-    )(record, *ints)
-
-
-def exchange_kernel(place, *refs):
-    out, halves, sems = refs[CAP:]
-    owners = refs[0].shape[0]
+        name="far",
+    )(record, ints, rest)
+
+
+def hold_kernel(above_in, below_in, above, below):
+    pass
+
+
+def hold(above, below):
+    hbm = pl.BlockSpec(memory_space=pltpu.HBM)
+    return pl.pallas_call(
+        hold_kernel,
+        out_shape=[jax.ShapeDtypeStruct(above.shape, above.dtype)] * 2,
+        in_specs=[hbm] * 2,
+        out_specs=[hbm] * 2,
+        input_output_aliases={0: 0, 1: 1},
+        compiler_params=pltpu.CompilerParams(vmem_limit_bytes=60 * 2**20),
+        cost_estimate=pl.CostEstimate(flops=10**11, bytes_accessed=0, transcendentals=0),
+        name="hold",
+    )(above, below)
+
+
+def exchange_kernel(place, first, above, last, below, *refs):
+    planes = len(refs) - 4
+    outs, (halves, late, product, sems) = refs[:planes], refs[planes:]
+    owners, main, _ = first.shape
+    npno = halves.shape[1]
     copies = [
-        pltpu.make_async_copy(refs[k], halves.at[pl.ds(k * owners, owners)], sems.at[k])
-        for k in range(CAP)
+        pltpu.make_async_copy(last, late, sems.at[0]),
+        pltpu.make_async_copy(
+            first, halves.at[pl.ds(0, owners), pl.ds(0, main)], sems.at[1]
+        ),
+        pltpu.make_async_copy(above, halves.at[pl.ds(owners, owners)], sems.at[2]),
+        pltpu.make_async_copy(below, halves.at[pl.ds(3 * owners, owners)], sems.at[3]),
     ]
     for copy in copies:
         copy.start()
-    for copy in copies:
+    copies[0].wait()
+
+    def join(e, _):
+        halves[e, main:] = late[e, npno:]
+        halves[2 * owners + e] = late[e, :npno]
+        return 0
+
+    lax.fori_loop(0, owners, join, 0, unroll=4)
+    for copy in copies[1:]:
         copy.wait()
-    group = 16
+    each = outs[0].shape[0]
 
     def some(g, _):
-        for k in range(group):
-            q = g * group + k
-            out[q] = lax.dot_general(
+        for k in range(each):
+            q = g * each + k
+            at = pl.multiple_of(q * npno, 8)
+            product[pl.ds(at, npno), :npno] = lax.dot_general(
                 halves[place[2 * q]],
                 halves[place[2 * q + 1]],
                 (((1,), (1,)), ((), ())),
@@ -237,25 +371,33 @@
             )
         return 0
 
-    lax.fori_loop(0, out.shape[0] // group, some, 0)
-
-
-def exchange_of(place, parts):
-    owners, npno, naux = parts[0].shape
+    lax.fori_loop(0, planes, some, 0)
+    for g in range(planes):
+        for x in range(npno):
+            rows = product[pl.ds(g * each * npno + x, each, stride=npno), :]
+            outs[g][:, x * npno : (x + 1) * npno] = rows[:, :npno]
+
+
+def exchange_of(place, planes, first, above, last, below):
+    owners, npno, naux = above.shape
     pairs = place.shape[0] // 2
     hbm = pl.BlockSpec(memory_space=pltpu.HBM)
+    vmem = pl.BlockSpec(memory_space=pltpu.VMEM)
+    out = jax.ShapeDtypeStruct((pairs // planes, npno * npno), jnp.float32)
     return pl.pallas_call(
         exchange_kernel,
-        out_shape=jax.ShapeDtypeStruct((pairs, npno, npno), jnp.float32),
-        in_specs=[pl.BlockSpec(memory_space=pltpu.SMEM)] + [hbm] * CAP,
-        out_specs=pl.BlockSpec(memory_space=pltpu.VMEM),
+        out_shape=[out] * planes,
+        in_specs=[pl.BlockSpec(memory_space=pltpu.SMEM)] + [hbm] * 4,
+        out_specs=[vmem] * planes,
         scratch_shapes=[
             pltpu.VMEM((CAP * owners, npno, naux), jnp.bfloat16),
-            pltpu.SemaphoreType.DMA((CAP,)),
+            pltpu.VMEM(last.shape, jnp.bfloat16),
+            pltpu.VMEM((pairs * npno, LANES), jnp.float32),
+            pltpu.SemaphoreType.DMA((4,)),
         ],
         compiler_params=pltpu.CompilerParams(vmem_limit_bytes=60 * 2**20),
         name="exchange",
-    )(place, *parts)
+    )(place, first, above, last, below)
 
 
 def body(
@@ -286,30 +428,26 @@
     )
     own = there(sent)
 
-    above = shifted(ints_block, n_rep - 1)
-    below = shifted(ints_block, 1)
+    above, below = hold(shifted(ints_block, n_rep - 1), shifted(ints_block, 1))
+    own, above, below = lax.optimization_barrier((own, above, below))
     opposite = shifted(own, 2)
 
-    first = there(half(own, (ints_block,), npno, WEIGHT))
-    near, first = lax.optimization_barrier((half(own, (above, below), npno, WEIGHT), first))
+    near, rest = near_halves(own, ints_block, above, below, npno)
     near = there(near)
-    far, near = lax.optimization_barrier((half(opposite, (ints_block,), npno, WEIGHT), near))
-    far = there(far)
-
-    parts = (
-        first[:, 0],
-        shifted(near[:, 1], n_rep - 1),
-        far[:, 0],
-        shifted(near[:, 0], 1),
-    )
+    last, near = lax.optimization_barrier((far_halves(opposite, ints_block, rest, npno), near))
+    last = there(last)
+
+    main = npno // 16 * 16
+    first = near[:, :main]
+    above = shifted(near[:, main + npno :], n_rep - 1)
+    below = shifted(near[:, main : main + npno], 1)
     place = (slot // n_orb - rep) % n_rep * n_orb + slot % n_orb
-    partial_value = exchange_of(place, parts)
     mine = pair_dev // n_rep
-    partial_value = partial_value.reshape(n_rep, mine, npno * npno)
-    exchange = lax.dynamic_index_in_dim(partial_value, rep, 0, keepdims=False)
-    for by in (1, n_rep - 1, 2):
-        leaving = lax.dynamic_index_in_dim(partial_value, (rep + by) % n_rep, 0, keepdims=False)
-        exchange = exchange + shifted(leaving, by)
+    place = jnp.roll(place.reshape(n_rep, 2 * mine), -rep, axis=0).reshape(-1)
+    products = exchange_of(place, n_rep, first, above, last, below)
+    exchange = products[0]
+    for by in (2, 1, n_rep - 1):
+        exchange = exchange + shifted(products[by], by)
     own_orbs = lax.dynamic_slice_in_dim(pair_orbitals, rep * mine, mine, 0)
     first_fock = occupied_fock_diagonal[own_orbs[:, 0]]
     second_fock = occupied_fock_diagonal[own_orbs[:, 1]]

time: 330 us -> 318 us (0.964)
  starting transfers between devices: 45.8 us -> 35.8 us
  Pallas kernels: 43.2 us -> 34.1 us
  waiting for transfers between devices: 225 us -> 231 us
    ppermute x8, waiting for transfers between devices: 111 us -> 159 us  [shifted(): lax.ppermute(value, 'rep', [(i, (i + by) % n_rep) for i in range(n_rep)])]
    all_to_all x4 -> x3, waiting for transfers between devices: 114 us -> 72.1 us  [there(): return lax.all_to_all(value, 'orb', split_axis=0, concat_axis=0, tiled=True)]
    pallas_call x4, Pallas kernels: 35.7 us -> 26.6 us  [the longest x1 11.9 us: near_halves(): pl.pallas_call(functools.partial(near_kernel, npno), out_shape=[jax.Shape...]
    slice x0 -> x2, local copies, waits for them, and re-layouts: none -> 7.23 us  [the longest x1 4.41 us: body(): below = shifted(near[:, main:main + npno], 1)]
    all_to_all x4 -> x3, starting transfers between devices: 30.6 us -> 25.1 us  [there(): return lax.all_to_all(value, 'orb', split_axis=0, concat_axis=0, tiled=True)]
    squeeze x2 -> x0, local copies, waits for them, and re-layouts: 4.6 us -> none  [the longest x1 4.55 us: body(): near[:, 0]]
    ppermute x8, starting transfers between devices: 15.2 us -> 10.7 us  [shifted(): lax.ppermute(value, 'rep', [(i, (i + by) % n_rep) for i in range(n_rep)])]
  transfers between devices with their start and end apart: 12 -> 11, of which waited for: 9 -> 10; matrix products, arithmetic and copies ran while one was open for 2% -> 3% of each run, Pallas kernels for 9% -> 5%
where the time goes in v4:
time: 318 us; the launch traced here: 317 us
  waiting for transfers between devices  231 us (73%)
  starting transfers between devices  35.8 us (11%)
  Pallas kernels  34.1 us (11%)
  local copies, waits for them, and re-layouts  14.1 us (4%)
    ppermute x8, waiting for transfers between devices, shifted(): lax.ppermute(value, 'rep', [(i, (i + by) % n_rep) for i in range(n_rep)])  159 us
    all_to_all x3, waiting for transfers between devices, there(): return lax.all_to_all(value, 'orb', split_axis=0, concat_axis=0, tiled=True)  72.1 us
    all_to_all x3, starting transfers between devices, there(): return lax.all_to_all(value, 'orb', split_axis=0, concat_axis=0, tiled=True)  25.1 us
    pallas_call x1, Pallas kernels, near_halves(): pl.pallas_call(functools.partial(near_kernel, npno), out_shape=[jax.Shape...  11.9 us
    ppermute x8, starting transfers between devices, shifted(): lax.ppermute(value, 'rep', [(i, (i + by) % n_rep) for i in range(n_rep)])  10.7 us
    pallas_call x1, Pallas kernels, far_halves(): pl.pallas_call(functools.partial(far_kernel, npno), out_shape=jax.ShapeDt...  7.63 us
    pallas_call x1, Pallas kernels, route(): pl.pallas_call(functools.partial(route_kernel, keeper), out_shape=(jax.Sh...  7.46 us
    pallas_call x1, Pallas kernels, exchange_of(): pl.pallas_call(exchange_kernel, out_shape=[out] * planes, in_specs=[pl.Bl...  7.08 us
  transfers between devices with their start and end apart: 11, of which 10 were waited for; matrix products, arithmetic and copies ran while one was open for 3% of the time, Pallas kernels for 5%

profile of v4, /device:TPU:1, one launch (start us, length us, event | category | flops | bytes accessed | tf_op | source)
XLA Modules:
  0.0 316.8 jit_solution(10010572622948957465)
XLA Ops:
  0.0 3.6 %collective-permute-start = (bf16[8,384,512]{2,1,0:T(8,128)(2,1)}, bf16[8,384,512]{2,1,0:T(8,128)(2,1)}, u32[]{:S(2)}, u32[]{:S(2)}) collective-permute-start(bf16[8,384,512]{2,1,0:T(8,128)(2,1)} %ints.1), channel_id=1, source_target_pairs={{0,3},{1,0},{2,1},{3,2},{4,7},{5,4},{6,5},{7,6},{8,11},{9,8},{10,9... | collective-permute-start | bytes 9437192 | tf_op jit(solution)/shard_map/ppermute | solution.py:421
  3.6 7.5 %route.1 = (bf16[64,168,128]{2,1,0:T(8,128)(2,1)}, s32[192]{0:T(256)}) custom-call(s32[2,96]{1,0:T(2,128)} %bitcast.8, s32[512]{0:T(512)} %place.1, s32[1]{0:T(128)} %bitcast.1.plane, bf16[192,40,512]{2,1,0:T(8,128)(2,1)} %bitcast.7), custom_call_target="tpu_custom_call" | custom-call | tf_op jit(solution)/shard_map/route/pallas_call | solution.py:88
  11.0 12.4 %all-to-all-start = ((bf16[64,168,128]{2,1,0:T(8,128)(2,1)}), bf16[64,168,128]{2,1,0:T(8,128)(2,1)S(1)}, u32[]{:S(2)}, u32[]{:S(2)}) async-start(bf16[64,168,128]{2,1,0:T(8,128)(2,1)} %get-tuple-element.21), calls=%async_computation | async-start | bytes 5505024 | tf_op jit(solution)/shard_map/all_to_all | solution.py:424
  23.5 47.2 %collective-permute-done.above_in = bf16[8,384,512]{2,1,0:T(8,128)(2,1)} collective-permute-done((bf16[8,384,512]{2,1,0:T(8,128)(2,1)}, bf16[8,384,512]{2,1,0:T(8,128)(2,1)}, u32[]{:S(2)}, u32[]{:S(2)}) %collective-permute-start) | collective-permute-done | bytes 3145760 | tf_op jit(solution)/shard_map/ppermute | solution.py:421
  70.7 3.1 collective-permute-done.1.below_in
  73.7 14.8 %all-to-all-done.record = bf16[64,168,128]{2,1,0:T(8,128)(2,1)S(1)} async-done(((bf16[64,168,128]{2,1,0:T(8,128)(2,1)}), bf16[64,168,128]{2,1,0:T(8,128)(2,1)S(1)}, u32[]{:S(2)}, u32[]{:S(2)}) %all-to-all-start) | async-done | bytes 2752544 | tf_op jit(solution)/shard_map/all_to_all | solution.py:424
  88.6 1.5 copy-done.1
  90.1 11.9 %near.1 = (bf16[64,112,384]{2,1,0:T(8,128)(2,1)}, bf16[64,8,384]{2,1,0:T(8,128)(2,1)}) custom-call(bf16[64,168,128]{2,1,0:T(8,128)(2,1)} %copy-done.1, bf16[8,384,512]{2,1,0:T(8,128)(2,1)} %ints.1, bf16[8,384,512]{2,1,0:T(8,128)(2,1)} %get-tuple-element.25.above, bf16[8,384,512]{2,1,0:T(8,128)(2,1)} %get-tuple-element.26.below), custom_call_target="tpu_custom_call" | custom-call | flops 3019898880 | bytes 17956864 | tf_op jit(solution)/shard_map/near/pallas_call | solution.py:212
  102.0 6.9 %all-to-all-start.1 = ((bf16[64,112,384]{2,1,0:T(8,128)(2,1)}), bf16[64,112,384]{2,1,0:T(8,128)(2,1)}, u32[]{:S(2)}, u32[]{:S(2)}) async-start(bf16[64,112,384]{2,1,0:T(8,128)(2,1)} %get-tuple-element.28), calls=%async_computation.1 | async-start | bytes 11010048 | tf_op jit(solution)/shard_map/all_to_all | solution.py:424
  108.9 1.1 collective-permute-start.2
  110.0 61.3 %collective-permute-done.2.record = bf16[64,168,128]{2,1,0:T(8,128)(2,1)S(1)} collective-permute-done((bf16[64,168,128]{2,1,0:T(8,128)(2,1)S(1)}, bf16[64,168,128]{2,1,0:T(8,128)(2,1)S(1)}, u32[]{:S(2)}, u32[]{:S(2)}) %collective-permute-start.2) | collective-permute-done | bytes 2752544 | tf_op jit(solution)/shard_map/ppermute | solution.py:421
  171.3 1.5 copy-done.8
  172.8 7.6 %far.1 = bf16[64,48,384]{2,1,0:T(8,128)(2,1)} custom-call(bf16[64,168,128]{2,1,0:T(8,128)(2,1)} %copy-done.8, bf16[8,384,512]{2,1,0:T(8,128)(2,1)} %ints.1, bf16[64,8,384]{2,1,0:T(8,128)(2,1)} %get-tuple-element.27.rest_in), custom_call_target="tpu_custom_call" | custom-call | flops 8053063680 | bytes 7733248 | tf_op jit(solution)/shard_map/far/pallas_call | solution.py:290
  180.5 52.4 %all-to-all-done.1 = bf16[64,112,384]{2,1,0:T(8,128)(2,1)} async-done(((bf16[64,112,384]{2,1,0:T(8,128)(2,1)}), bf16[64,112,384]{2,1,0:T(8,128)(2,1)}, u32[]{:S(2)}, u32[]{:S(2)}) %all-to-all-start.1) | async-done | bytes 5505056 | tf_op jit(solution)/shard_map/all_to_all | solution.py:424
  232.9 5.8 %all-to-all-start.2 = ((bf16[64,48,384]{2,1,0:T(8,128)(2,1)}), bf16[64,48,384]{2,1,0:T(8,128)(2,1)S(1)}, u32[]{:S(2)}, u32[]{:S(2)}) async-start(bf16[64,48,384]{2,1,0:T(8,128)(2,1)} %far.1), calls=%async_computation.2 | async-start | bytes 4718592 | tf_op jit(solution)/shard_map/all_to_all | solution.py:424
  238.7 4.4 %fusion.5 = (bf16[64,40,384]{2,1,0:T(8,128)(2,1)}, bf16[64,40,384]{2,1,0:T(8,128)(2,1)}) fusion(bf16[64,112,384]{2,1,0:T(8,128)(2,1)} %all-to-all-done.1), kind=kLoop, calls=%fused_computation.24 | loop fusion | bytes 7864320 | tf_op jit(solution)/shard_map/slice | solution.py:443
  243.1 2.2 collective-permute-start.3
  245.5 0.6 reshape.26.place
  246.2 0.7 gather_fusion
  246.9 0.7 gather_fusion.1
  247.6 2.8 slice.15.first
  250.4 36.9 %collective-permute-done.3.above = bf16[64,40,384]{2,1,0:T(8,128)(2,1)} collective-permute-done((bf16[64,40,384]{2,1,0:T(8,128)(2,1)}, bf16[64,40,384]{2,1,0:T(8,128)(2,1)}, u32[]{:S(2)}, u32[]{:S(2)}) %collective-permute-start.3) | collective-permute-done | bytes 1966112 | tf_op jit(solution)/shard_map/ppermute | solution.py:421
  287.4 3.1 collective-permute-done.4.below
  290.5 4.9 %all-to-all-done.2.last = bf16[64,48,384]{2,1,0:T(8,128)(2,1)S(1)} async-done(((bf16[64,48,384]{2,1,0:T(8,128)(2,1)}), bf16[64,48,384]{2,1,0:T(8,128)(2,1)S(1)}, u32[]{:S(2)}, u32[]{:S(2)}) %all-to-all-start.2) | async-done | bytes 2359328 | tf_op jit(solution)/shard_map/all_to_all | solution.py:424
  295.3 1.4 copy-done.3
  296.8 7.1 %exchange.1 = (f32[24,1600]{1,0:T(8,128)}, f32[24,1600]{1,0:T(8,128)}, f32[24,1600]{1,0:T(8,128)}, f32[24,1600]{1,0:T(8,128)}) custom-call(s32[192]{0:T(256)} %reshape.26.place, bf16[64,32,384]{2,1,0:T(8,128)(2,1)} %slice.15.first, bf16[64,40,384]{2,1,0:T(8,128)(2,1)} %collective-permute-done.3.above, bf16[64,48,384]{2,1,0:T(8,128)(2,1)} %copy-done.3, ...), custom_call_target="tpu_custom_call" | custom-call | tf_op jit(solution)/shard_map/exchange/pallas_call | solution.py:387
  303.8 1.1 collective-permute-start.5
  304.9 1.8 collective-permute-start.6
  306.7 0.9 collective-permute-start.7
  308.0 3.2 %collective-permute-done.5 = f32[24,1600]{1,0:T(8,128)S(1)} collective-permute-done((f32[24,1600]{1,0:T(8,128)}, f32[24,1600]{1,0:T(8,128)S(1)}, u32[]{:S(2)}, u32[]{:S(2)}) %collective-permute-start.5) | collective-permute-done | bytes 153632 | tf_op jit(solution)/shard_map/ppermute | solution.py:421
  311.3 3.9 %collective-permute-done.6 = f32[24,1600]{1,0:T(8,128)S(1)} collective-permute-done((f32[24,1600]{1,0:T(8,128)}, f32[24,1600]{1,0:T(8,128)S(1)}, u32[]{:S(2)}, u32[]{:S(2)}) %collective-permute-start.6) | collective-permute-done | bytes 153632 | tf_op jit(solution)/shard_map/ppermute | solution.py:421
  315.1 1.7 multiply_add_fusion
  (29 shorter events, 0.6 us)
Async XLA Ops:
  0.0 246.2 %copy-start = (f32[512]{0:T(512)S(1)}, f32[512]{0:T(512)}, u32[]{:S(2)}) copy-start(f32[512]{0:T(512)} %param.13) | copy-start | bytes 6148
  0.0 70.6 %collective-permute-start = (bf16[8,384,512]{2,1,0:T(8,128)(2,1)}, bf16[8,384,512]{2,1,0:T(8,128)(2,1)}, u32[]{:S(2)}, u32[]{:S(2)}) collective-permute-start(bf16[8,384,512]{2,1,0:T(8,128)(2,1)} %ints.1), channel_id=1, source_target_pairs={{0,3},{1,0},{2,1},{3,2},{4,7},{5,4},{6,5},{7,6},{8,11},{9,8},{10,9... | collective-permute-start | bytes 9437192 | tf_op jit(solution)/shard_map/ppermute | solution.py:421
  3.6 70.2 %collective-permute-start.1 = (bf16[8,384,512]{2,1,0:T(8,128)(2,1)}, bf16[8,384,512]{2,1,0:T(8,128)(2,1)}, u32[]{:S(2)}, u32[]{:S(2)}) collective-permute-start(bf16[8,384,512]{2,1,0:T(8,128)(2,1)} %ints.1), channel_id=1, source_target_pairs={{0,1},{1,2},{2,3},{3,0},{4,5},{5,6},{6,7},{7,4},{8,9},{9,10},{10,1... | collective-permute-start | bytes 9437192 | tf_op jit(solution)/shard_map/ppermute | solution.py:421
  11.0 77.5 %all-to-all-start = ((bf16[64,168,128]{2,1,0:T(8,128)(2,1)}), bf16[64,168,128]{2,1,0:T(8,128)(2,1)S(1)}, u32[]{:S(2)}, u32[]{:S(2)}) async-start(bf16[64,168,128]{2,1,0:T(8,128)(2,1)} %get-tuple-element.21), calls=%async_computation | async-start | bytes 5505024 | tf_op jit(solution)/shard_map/all_to_all | solution.py:424
  88.6 1.5 copy-start.1
  102.0 6.9 %copy-start.2 = (bf16[64,168,128]{2,1,0:T(8,128)(2,1)S(1)}, bf16[64,168,128]{2,1,0:T(8,128)(2,1)}, u32[]{:S(2)}) copy-start(bf16[64,168,128]{2,1,0:T(8,128)(2,1)} %copy-done.1) | copy-start | bytes 8257540
  102.0 130.9 %all-to-all-start.1 = ((bf16[64,112,384]{2,1,0:T(8,128)(2,1)}), bf16[64,112,384]{2,1,0:T(8,128)(2,1)}, u32[]{:S(2)}, u32[]{:S(2)}) async-start(bf16[64,112,384]{2,1,0:T(8,128)(2,1)} %get-tuple-element.28), calls=%async_computation.1 | async-start | bytes 11010048 | tf_op jit(solution)/shard_map/all_to_all | solution.py:424
  108.9 62.4 %collective-permute-start.2 = (bf16[64,168,128]{2,1,0:T(8,128)(2,1)S(1)}, bf16[64,168,128]{2,1,0:T(8,128)(2,1)S(1)}, u32[]{:S(2)}, u32[]{:S(2)}) collective-permute-start(bf16[64,168,128]{2,1,0:T(8,128)(2,1)S(1)} %copy-done.2), channel_id=1, source_target_pairs={{0,2},{1,3},{2,0},{3,1},{4,6},{5,7},{6,4},{7,5},{8,10},{9,11},{10,... | collective-permute-start | bytes 8257544 | tf_op jit(solution)/shard_map/ppermute | solution.py:421
  171.3 1.5 copy-start.8
  232.9 62.4 %all-to-all-start.2 = ((bf16[64,48,384]{2,1,0:T(8,128)(2,1)}), bf16[64,48,384]{2,1,0:T(8,128)(2,1)S(1)}, u32[]{:S(2)}, u32[]{:S(2)}) async-start(bf16[64,48,384]{2,1,0:T(8,128)(2,1)} %far.1), calls=%async_computation.2 | async-start | bytes 4718592 | tf_op jit(solution)/shard_map/all_to_all | solution.py:424
  238.7 6.6 %copy-start.7 = (s32[192]{0:T(256)S(1)}, s32[192]{0:T(256)}, u32[]{:S(2)}) copy-start(s32[192]{0:T(256)} %get-tuple-element.20) | copy-start | bytes 2308
  238.7 7.4 %copy-start.6 = (s32[96,2]{0,1:T(2,128)S(1)}, s32[96,2]{0,1:T(2,128)}, u32[]{:S(2)}) copy-start(s32[96,2]{0,1:T(2,128)} %param.9) | copy-start | bytes 2308
  243.1 44.3 %collective-permute-start.3 = (bf16[64,40,384]{2,1,0:T(8,128)(2,1)}, bf16[64,40,384]{2,1,0:T(8,128)(2,1)}, u32[]{:S(2)}, u32[]{:S(2)}) collective-permute-start(bf16[64,40,384]{2,1,0:T(8,128)(2,1)} %get-tuple-element.36), channel_id=1, source_target_pairs={{0,3},{1,0},{2,1},{3,2},{4,7},{5,4},{6,5},{7,6},{8,11},{9,8},{10,9... | collective-permute-start | bytes 5898248 | tf_op jit(solution)/shard_map/ppermute | solution.py:421
  245.3 45.1 %collective-permute-start.4 = (bf16[64,40,384]{2,1,0:T(8,128)(2,1)}, bf16[64,40,384]{2,1,0:T(8,128)(2,1)}, u32[]{:S(2)}, u32[]{:S(2)}) collective-permute-start(bf16[64,40,384]{2,1,0:T(8,128)(2,1)} %get-tuple-element.35), channel_id=1, source_target_pairs={{0,1},{1,2},{2,3},{3,0},{4,5},{5,6},{6,7},{7,4},{8,9},{9,10},{10,1... | collective-permute-start | bytes 5898248 | tf_op jit(solution)/shard_map/ppermute | solution.py:421
  250.4 57.2 %copy-start.5 = (f32[24,40]{1,0:T(8,128)S(1)}, f32[24,40]{1,0:T(8,128)}, u32[]{:S(2)}) copy-start(f32[24,40]{1,0:T(8,128)} %param.12) | copy-start | bytes 11524
  250.4 64.7 %copy-start.4 = (bf16[24,1600]{1,0:T(8,128)(2,1)S(1)}, bf16[24,1600]{1,0:T(8,128)(2,1)}, u32[]{:S(2)}) copy-start(bf16[24,1600]{1,0:T(8,128)(2,1)} %param.11) | copy-start | bytes 230404
  295.3 1.4 copy-start.3
  303.8 7.4 %collective-permute-start.5 = (f32[24,1600]{1,0:T(8,128)}, f32[24,1600]{1,0:T(8,128)S(1)}, u32[]{:S(2)}, u32[]{:S(2)}) collective-permute-start(f32[24,1600]{1,0:T(8,128)} %get-tuple-element.32), channel_id=1, source_target_pairs={{0,2},{1,3},{2,0},{3,1},{4,6},{5,7},{6,4},{7,5},{8,10},{9,11},{10,... | collective-permute-start | bytes 460808 | tf_op jit(solution)/shard_map/ppermute | solution.py:421
  304.9 10.2 %collective-permute-start.6 = (f32[24,1600]{1,0:T(8,128)}, f32[24,1600]{1,0:T(8,128)S(1)}, u32[]{:S(2)}, u32[]{:S(2)}) collective-permute-start(f32[24,1600]{1,0:T(8,128)} %get-tuple-element.33), channel_id=1, source_target_pairs={{0,1},{1,2},{2,3},{3,0},{4,5},{5,6},{6,7},{7,4},{8,9},{9,10},{10,1... | collective-permute-start | bytes 460808 | tf_op jit(solution)/shard_map/ppermute | solution.py:421
  306.7 8.4 %collective-permute-start.7 = (f32[24,1600]{1,0:T(8,128)}, f32[24,1600]{1,0:T(8,128)S(1)}, u32[]{:S(2)}, u32[]{:S(2)}) collective-permute-start(f32[24,1600]{1,0:T(8,128)} %get-tuple-element.34), channel_id=1, source_target_pairs={{0,3},{1,0},{2,1},{3,2},{4,7},{5,4},{6,5},{7,6},{8,11},{9,8},{10,9... | collective-permute-start | bytes 460808 | tf_op jit(solution)/shard_map/ppermute | solution.py:421

commit v5 on v4

--- a/solution.py
+++ b/solution.py
@@ -13,6 +13,7 @@
 
 LANES = 128
 SPARE = 8
+PARTS = 4
 
 
 def pieces(npno, npao):
@@ -28,44 +29,56 @@
     return cuts
 
 
+def parted(at, keeper):
+    if keeper & (keeper - 1):
+        return lax.div(at, keeper), lax.rem(at, keeper)
+    return lax.shift_right_logical(at, keeper.bit_length() - 1), lax.bitwise_and(at, keeper - 1)
+
+
 def route_kernel(
-    keeper, orbitals, place, plane, vectors, sent, slot, count, source, row, held, record, sems
+    keeper, orbitals, place, plane, vectors, sent, slot, count, row, held, record, sems
 ):
     owners, npno, npao = held.shape
     pairs = orbitals.shape[1]
-    together = 4
+    together = 8
 
     def clear(o, _):
         count[o] = 0
-        source[o] = 0
         row[o] = keeper
         return 0
 
-    lax.fori_loop(0, owners, clear, 0, unroll=8)
+    lax.fori_loop(0, owners, clear, 0, unroll=16)
     mine = plane[0]
+
+    def fetch(e, owner):
+        return pltpu.make_async_copy(vectors.at[e], held.at[owner], sems.at[0])
 
     def some(g, _):
         for k in range(together):
             q = g * together + k
             for side in range(2):
-                at = place[orbitals[side, q]]
-                owner = at // keeper
+                owner, of = parted(place[orbitals[side, q]], keeper)
                 position = count[owner]
                 count[owner] = position + 1
                 slot[q * 2 + side] = position * owners + owner
-                to = owner + jnp.where(position == mine, 0, owners)
-                source[to] = q * 2 + side
-                row[to] = at % keeper
+
+                @pl.when(position == mine)
+                def _():
+                    row[owner] = of
+                    fetch(q * 2 + side, owner).start()
+
         return 0
 
     lax.fori_loop(0, pairs // together, some, 0)
 
-    def fetch(o, _):
-        pltpu.make_async_copy(vectors.at[source[o]], held.at[o], sems.at[0]).start()
-        return 0
-
-    lax.fori_loop(0, owners, fetch, 0, unroll=8)
-    pltpu.make_async_copy(vectors.at[pl.ds(0, owners)], held, sems.at[0]).wait()
+    def arrive(o, _):
+        @pl.when(row[o] < keeper)
+        def _():
+            fetch(0, 0).wait()
+
+        return 0
+
+    lax.fori_loop(0, owners, arrive, 0, unroll=8)
 
     def lay(o, _):
         for rows, lanes, at in pieces(npno, npao):
@@ -74,10 +87,14 @@
         record[o, npno * npao // LANES :, :] = number.astype(record.dtype)
         return 0
 
-    lax.fori_loop(0, owners, lay, 0, unroll=2)
-    out = pltpu.make_async_copy(record, sent, sems.at[1])
-    out.start()
-    out.wait()
+    outs = []
+    for part in range(PARTS):
+        own = pl.ds(part * owners // PARTS, owners // PARTS)
+        lax.fori_loop(part * owners // PARTS, (part + 1) * owners // PARTS, lay, 0, unroll=2)
+        outs.append(pltpu.make_async_copy(record.at[own], sent.at[own], sems.at[1 + part]))
+        outs[-1].start()
+    for out in outs:
+        out.wait()
 
 
 def route(orbitals, orbital_place, plane, vectors, owners, keeper):
@@ -95,11 +112,10 @@
         out_specs=(hbm, smem),
         scratch_shapes=[
             pltpu.SMEM((owners,), jnp.int32),
-            pltpu.SMEM((2 * owners,), jnp.int32),
-            pltpu.SMEM((2 * owners,), jnp.int32),
+            pltpu.SMEM((owners,), jnp.int32),
             pltpu.VMEM((owners, npno, npao), vectors.dtype),
             pltpu.VMEM((owners, depth, LANES), vectors.dtype),
-            pltpu.SemaphoreType.DMA((2,)),
+            pltpu.SemaphoreType.DMA((1 + PARTS,)),
         ],
         compiler_params=pltpu.CompilerParams(vmem_limit_bytes=60 * 2**20),
         name="route",
@@ -137,15 +153,12 @@
 
 
 def near_kernel(
-    npno, record, own, above, below, out, rest_out,
-    held, order, count, number, row, stacked, blocks, halves, rest, sems,
+    npno, held, own, above, below, out, rest_out,
+    order, count, number, row, stacked, blocks, halves, rest, sems,
 ):
     keeper, naux, npao = own.shape
     items, tail, _ = rest.shape
     main = npno - tail
-    deep = stacked.shape[1]
-    whole = pltpu.make_async_copy(record, held, sems.at[0])
-    whole.start()
     loads = [
         pltpu.make_async_copy(
             share.at[o], blocks.at[o, pl.ds(k * naux, naux)], sems.at[4 + 3 * o + k]
@@ -155,8 +168,6 @@
     ]
     for load in loads:
         load.start()
-    stacked[...] = jnp.zeros_like(stacked)
-    whole.wait()
     sort_entries(held, number, row, count, order, sems.at[1], keeper, npno * npao // LANES)
 
     def goes(e):
@@ -170,14 +181,14 @@
         def block(b, _):
             at = [b * TOGETHER + t for t in range(TOGETHER)]
             ids = [order[o * items + jnp.minimum(k, n - 1)] for k in at]
+            for t, e in enumerate(ids):
+                for rows, lanes, place in pieces(npno, npao):
+                    stacked[t * npno + rows.start : t * npno + rows.stop, lanes] = held[e, place, :]
             value = lax.dot_general(
-                stack(stacked, held, ids, npno),
-                blocks[o],
-                (((1,), (1,)), ((), ())),
-                preferred_element_type=jnp.float32,
-            ).astype(out.dtype)
+                stacked[...], blocks[o], (((1,), (1,)), ((), ())), preferred_element_type=jnp.float32
+            )
             for t, e in enumerate(ids):
-                rows = value[t * deep : t * deep + npno]
+                rows = value[t * npno : (t + 1) * npno].astype(out.dtype)
                 halves[e, :main] = rows[:main, :naux]
                 rest[e] = rows[main:, :naux]
                 halves[e, main : main + npno] = rows[:, naux : 2 * naux]
@@ -215,21 +226,20 @@
             jax.ShapeDtypeStruct((items, rows, naux), jnp.bfloat16),
             jax.ShapeDtypeStruct((items, tail, naux), jnp.bfloat16),
         ],
-        in_specs=[hbm] * 4,
+        in_specs=[pl.BlockSpec(memory_space=pltpu.VMEM)] + [hbm] * 3,
         out_specs=[hbm] * 2,
         scratch_shapes=[
-            pltpu.VMEM(record.shape, record.dtype),
             pltpu.SMEM(((keeper + 1) * items,), jnp.int32),
             pltpu.SMEM((keeper + 1,), jnp.int32),
             pltpu.VMEM((SPARE, LANES), jnp.int32),
             pltpu.SMEM((SPARE, LANES), jnp.int32),
-            pltpu.VMEM((TOGETHER, -(-npno // 16) * 16, npao), jnp.bfloat16),
+            pltpu.VMEM((TOGETHER * npno, npao), jnp.bfloat16),
             pltpu.VMEM((keeper, 3 * naux, npao), jnp.bfloat16),
             pltpu.VMEM((items, rows, naux), jnp.bfloat16),
             pltpu.VMEM((items, tail, naux), jnp.bfloat16),
             pltpu.SemaphoreType.DMA((4 + 3 * keeper,)),
         ],
-        compiler_params=pltpu.CompilerParams(vmem_limit_bytes=60 * 2**20),
+        compiler_params=pltpu.CompilerParams(vmem_limit_bytes=48 * 2**20),
         cost_estimate=pl.CostEstimate(
             flops=6 * items * npno * npao * naux,
             bytes_accessed=2 * (3 * keeper * npao * naux + items * npno * (npao + 3 * naux)),
@@ -395,7 +405,7 @@
             pltpu.VMEM((pairs * npno, LANES), jnp.float32),
             pltpu.SemaphoreType.DMA((4,)),
         ],
-        compiler_params=pltpu.CompilerParams(vmem_limit_bytes=60 * 2**20),
+        compiler_params=pltpu.CompilerParams(vmem_limit_bytes=48 * 2**20),
         name="exchange",
     )(place, first, above, last, below)
 
@@ -443,16 +453,18 @@
     below = shifted(near[:, main : main + npno], 1)
     place = (slot // n_orb - rep) % n_rep * n_orb + slot % n_orb
     mine = pair_dev // n_rep
+    own_orbs = lax.dynamic_slice_in_dim(pair_orbitals, rep * mine, mine, 0)
+    first_fock = occupied_fock_diagonal[own_orbs[:, 0]]
+    second_fock = occupied_fock_diagonal[own_orbs[:, 1]]
+    gap = pno_energy[:, :, None] + pno_energy[:, None, :] - (first_fock + second_fock)[:, None, None]
+    local = gap.reshape(mine, npno * npno) * amplitudes.astype(jnp.float32)
+    last, local = lax.optimization_barrier((last, local))
     place = jnp.roll(place.reshape(n_rep, 2 * mine), -rep, axis=0).reshape(-1)
     products = exchange_of(place, n_rep, first, above, last, below)
     exchange = products[0]
     for by in (2, 1, n_rep - 1):
         exchange = exchange + shifted(products[by], by)
-    own_orbs = lax.dynamic_slice_in_dim(pair_orbitals, rep * mine, mine, 0)
-    first_fock = occupied_fock_diagonal[own_orbs[:, 0]]
-    second_fock = occupied_fock_diagonal[own_orbs[:, 1]]
-    gap = pno_energy[:, :, None] + pno_energy[:, None, :] - (first_fock + second_fock)[:, None, None]
-    return exchange + gap.reshape(mine, npno * npno) * amplitudes.astype(jnp.float32)
+    return exchange + local
 
 
 def solution(mesh):

time: 318 us -> 308 us (0.969)
  Pallas kernels: 34.1 us -> 28 us
  local copies, waits for them, and re-layouts: 14.1 us -> 10.4 us
    ppermute x8, waiting for transfers between devices: 159 us -> 119 us  [shifted(): lax.ppermute(value, 'rep', [(i, (i + by) % n_rep) for i in range(n_rep)])]
    all_to_all x3, waiting for transfers between devices: 72.1 us -> 112 us  [there(): return lax.all_to_all(value, 'orb', split_axis=0, concat_axis=0, tiled=True)]
  transfers between devices with their start and end apart: 11 -> 11, of which waited for: 10 -> 8; matrix products, arithmetic and copies ran while one was open for 3% -> 3% of each run, Pallas kernels for 5% -> 4%
where the time goes in v5:
time: 308 us; the launch traced here: 307 us
  waiting for transfers between devices  231 us (75%)
  starting transfers between devices  36 us (12%)
  Pallas kernels  28 us (9%)
  local copies, waits for them, and re-layouts  10.4 us (3%)
    ppermute x8, waiting for transfers between devices, shifted(): lax.ppermute(value, 'rep', [(i, (i + by) % n_rep) for i in range(n_rep)])  119 us
    all_to_all x3, waiting for transfers between devices, there(): return lax.all_to_all(value, 'orb', split_axis=0, concat_axis=0, tiled=True)  112 us
    all_to_all x3, starting transfers between devices, there(): return lax.all_to_all(value, 'orb', split_axis=0, concat_axis=0, tiled=True)  25.5 us
    ppermute x8, starting transfers between devices, shifted(): lax.ppermute(value, 'rep', [(i, (i + by) % n_rep) for i in range(n_rep)])  10.5 us
    pallas_call x1, Pallas kernels, near_halves(): pl.pallas_call(functools.partial(near_kernel, npno), out_shape=[jax.Shape...  9.25 us
    pallas_call x1, Pallas kernels, far_halves(): pl.pallas_call(functools.partial(far_kernel, npno), out_shape=jax.ShapeDt...  8.42 us
  transfers between devices with their start and end apart: 11, of which 8 were waited for; matrix products, arithmetic and copies ran while one was open for 3% of the time, Pallas kernels for 4%

profile of v5, /device:TPU:1, one launch (start us, length us, event | category | flops | bytes accessed | tf_op | source)
XLA Modules:
  0.0 307.0 jit_solution(2405885851069704841)
XLA Ops:
  0.0 2.1 collective-permute-start.1
  2.1 1.5 collective-permute-start
  3.7 5.1 %route.1 = (bf16[64,168,128]{2,1,0:T(8,128)(2,1)}, s32[192]{0:T(256)}) custom-call(s32[2,96]{1,0:T(2,128)} %bitcast.8, s32[512]{0:T(512)} %place.1, s32[1]{0:T(128)} %bitcast.1.plane, bf16[192,40,512]{2,1,0:T(8,128)(2,1)} %bitcast.7), custom_call_target="tpu_custom_call" | custom-call | tf_op jit(solution)/shard_map/route/pallas_call | solution.py:105
  8.8 12.4 %all-to-all-start = ((bf16[64,168,128]{2,1,0:T(8,128)(2,1)}), bf16[64,168,128]{2,1,0:T(8,128)(2,1)S(1)}, u32[]{:S(2)}, u32[]{:S(2)}) async-start(bf16[64,168,128]{2,1,0:T(8,128)(2,1)} %get-tuple-element.23), calls=%async_computation | async-start | bytes 5505024 | tf_op jit(solution)/shard_map/all_to_all | solution.py:434
  21.2 48.4 %collective-permute-done.1.below_in = bf16[8,384,512]{2,1,0:T(8,128)(2,1)} collective-permute-done((bf16[8,384,512]{2,1,0:T(8,128)(2,1)}, bf16[8,384,512]{2,1,0:T(8,128)(2,1)}, u32[]{:S(2)}, u32[]{:S(2)}) %collective-permute-start.1) | collective-permute-done | bytes 3145760 | tf_op jit(solution)/shard_map/ppermute | solution.py:431
  69.7 1.3 collective-permute-done.above_in
  70.9 15.4 %all-to-all-done.held = bf16[64,168,128]{2,1,0:T(8,128)(2,1)S(1)} async-done(((bf16[64,168,128]{2,1,0:T(8,128)(2,1)}), bf16[64,168,128]{2,1,0:T(8,128)(2,1)S(1)}, u32[]{:S(2)}, u32[]{:S(2)}) %all-to-all-start) | async-done | bytes 2752544 | tf_op jit(solution)/shard_map/all_to_all | solution.py:434
  86.3 9.2 %near.1 = (bf16[64,112,384]{2,1,0:T(8,128)(2,1)}, bf16[64,8,384]{2,1,0:T(8,128)(2,1)S(1)}) custom-call(bf16[64,168,128]{2,1,0:T(8,128)(2,1)S(1)} %all-to-all-done.held, bf16[8,384,512]{2,1,0:T(8,128)(2,1)} %ints.1, bf16[8,384,512]{2,1,0:T(8,128)(2,1)} %get-tuple-element.27.above, bf16[8,384,512]{2,1,0:T(8,128)(2,1)} %get-tuple-element.28.below), custom_call_target="tpu_custom_call" | custom-call | flops 3019898880 | bytes 17956864 | tf_op jit(solution)/shard_map/near/pallas_call | solution.py:223
  95.6 0.8 copy-done.1
  96.3 7.1 %all-to-all-start.1 = ((bf16[64,112,384]{2,1,0:T(8,128)(2,1)}), bf16[64,112,384]{2,1,0:T(8,128)(2,1)}, u32[]{:S(2)}, u32[]{:S(2)}) async-start(bf16[64,112,384]{2,1,0:T(8,128)(2,1)} %get-tuple-element.30), calls=%async_computation.1 | async-start | bytes 11010048 | tf_op jit(solution)/shard_map/all_to_all | solution.py:434
  103.4 0.7 collective-permute-start.2
  104.2 61.7 %collective-permute-done.2.record = bf16[64,168,128]{2,1,0:T(8,128)(2,1)S(1)} collective-permute-done((bf16[64,168,128]{2,1,0:T(8,128)(2,1)S(1)}, bf16[64,168,128]{2,1,0:T(8,128)(2,1)S(1)}, u32[]{:S(2)}, u32[]{:S(2)}) %collective-permute-start.2) | collective-permute-done | bytes 2752544 | tf_op jit(solution)/shard_map/ppermute | solution.py:431
  165.8 1.6 copy-done.7
  167.5 8.4 %far.1 = bf16[64,48,384]{2,1,0:T(8,128)(2,1)} custom-call(bf16[64,168,128]{2,1,0:T(8,128)(2,1)} %copy-done.7, bf16[8,384,512]{2,1,0:T(8,128)(2,1)} %ints.1, bf16[64,8,384]{2,1,0:T(8,128)(2,1)} %copy-done.1), custom_call_target="tpu_custom_call" | custom-call | flops 8053063680 | bytes 7733248 | tf_op jit(solution)/shard_map/far/pallas_call | solution.py:300
  175.9 51.5 %all-to-all-done.1 = bf16[64,112,384]{2,1,0:T(8,128)(2,1)} async-done(((bf16[64,112,384]{2,1,0:T(8,128)(2,1)}), bf16[64,112,384]{2,1,0:T(8,128)(2,1)}, u32[]{:S(2)}, u32[]{:S(2)}) %all-to-all-start.1) | async-done | bytes 5505056 | tf_op jit(solution)/shard_map/all_to_all | solution.py:434
  227.4 6.0 %all-to-all-start.2 = ((bf16[64,48,384]{2,1,0:T(8,128)(2,1)}), bf16[64,48,384]{2,1,0:T(8,128)(2,1)}, u32[]{:S(2)}, u32[]{:S(2)}) async-start(bf16[64,48,384]{2,1,0:T(8,128)(2,1)} %far.1), calls=%async_computation.2 | async-start | bytes 4718592 | tf_op jit(solution)/shard_map/all_to_all | solution.py:434
  233.4 4.6 %fusion.5 = (bf16[64,40,384]{2,1,0:T(8,128)(2,1)}, bf16[64,40,384]{2,1,0:T(8,128)(2,1)}) fusion(bf16[64,112,384]{2,1,0:T(8,128)(2,1)} %all-to-all-done.1), kind=kLoop, calls=%fused_computation.25 | loop fusion | bytes 7864320 | tf_op jit(solution)/shard_map/slice | solution.py:453
  238.0 2.7 collective-permute-start.3
  240.8 0.7 gather_fusion.1
  241.5 0.7 gather_fusion
  242.2 0.2 broadcast_add_fusion
  242.4 0.2 add.79
  242.7 0.1 reshape.25
  242.9 0.7 convert_multiply_fusion
  243.6 1.6 slice.15.first
  245.2 44.8 %all-to-all-done.2.last = bf16[64,48,384]{2,1,0:T(8,128)(2,1)} async-done(((bf16[64,48,384]{2,1,0:T(8,128)(2,1)}), bf16[64,48,384]{2,1,0:T(8,128)(2,1)}, u32[]{:S(2)}, u32[]{:S(2)}) %all-to-all-start.2) | async-done | bytes 2359328 | tf_op jit(solution)/shard_map/all_to_all | solution.py:434
  290.0 5.2 %exchange.1 = (f32[24,1600]{1,0:T(8,128)S(1)}, f32[24,1600]{1,0:T(8,128)S(1)}, f32[24,1600]{1,0:T(8,128)S(1)}, f32[24,1600]{1,0:T(8,128)S(1)}) custom-call(s32[192]{0:T(256)S(1)} %reshape.26.place, bf16[64,32,384]{2,1,0:T(8,128)(2,1)S(1)} %slice.15.first, bf16[64,40,384]{2,1,0:T(8,128)(2,1)} %collective-permute-done.3.above, ...), custom_call_target="tpu_custom_call" | custom-call | tf_op jit(solution)/shard_map/exchange/pallas_call | solution.py:397
  295.2 0.7 collective-permute-start.5
  296.0 2.7 collective-permute-start.7
  298.6 3.8 %collective-permute-done.5 = f32[24,1600]{1,0:T(8,128)S(1)} collective-permute-done((f32[24,1600]{1,0:T(8,128)S(1)}, f32[24,1600]{1,0:T(8,128)S(1)}, u32[]{:S(2)}, u32[]{:S(2)}) %collective-permute-start.5) | collective-permute-done | bytes 153632 | tf_op jit(solution)/shard_map/ppermute | solution.py:431
  302.4 3.9 %collective-permute-done.6 = f32[24,1600]{1,0:T(8,128)S(1)} collective-permute-done((f32[24,1600]{1,0:T(8,128)S(1)}, f32[24,1600]{1,0:T(8,128)S(1)}, u32[]{:S(2)}, u32[]{:S(2)}) %collective-permute-start.6) | collective-permute-done | bytes 153632 | tf_op jit(solution)/shard_map/ppermute | solution.py:431
  306.3 0.7 add_add_fusion
  (28 shorter events, 0.3 us)
Async XLA Ops:
  0.0 240.8 %copy-start = (f32[512]{0:T(512)S(1)}, f32[512]{0:T(512)}, u32[]{:S(2)}) copy-start(f32[512]{0:T(512)} %param.13) | copy-start | bytes 6148
  0.0 69.7 %collective-permute-start.1 = (bf16[8,384,512]{2,1,0:T(8,128)(2,1)}, bf16[8,384,512]{2,1,0:T(8,128)(2,1)}, u32[]{:S(2)}, u32[]{:S(2)}) collective-permute-start(bf16[8,384,512]{2,1,0:T(8,128)(2,1)} %ints.1), channel_id=1, source_target_pairs={{0,1},{1,2},{2,3},{3,0},{4,5},{5,6},{6,7},{7,4},{8,9},{9,10},{10,1... | collective-permute-start | bytes 9437192 | tf_op jit(solution)/shard_map/ppermute | solution.py:431
  2.1 68.8 %collective-permute-start = (bf16[8,384,512]{2,1,0:T(8,128)(2,1)}, bf16[8,384,512]{2,1,0:T(8,128)(2,1)}, u32[]{:S(2)}, u32[]{:S(2)}) collective-permute-start(bf16[8,384,512]{2,1,0:T(8,128)(2,1)} %ints.1), channel_id=1, source_target_pairs={{0,3},{1,0},{2,1},{3,2},{4,7},{5,4},{6,5},{7,6},{8,11},{9,8},{10,9... | collective-permute-start | bytes 9437192 | tf_op jit(solution)/shard_map/ppermute | solution.py:431
  8.8 77.5 %all-to-all-start = ((bf16[64,168,128]{2,1,0:T(8,128)(2,1)}), bf16[64,168,128]{2,1,0:T(8,128)(2,1)S(1)}, u32[]{:S(2)}, u32[]{:S(2)}) async-start(bf16[64,168,128]{2,1,0:T(8,128)(2,1)} %get-tuple-element.23), calls=%async_computation | async-start | bytes 5505024 | tf_op jit(solution)/shard_map/all_to_all | solution.py:434
  95.5 0.8 copy-start.1
  96.3 131.1 %all-to-all-start.1 = ((bf16[64,112,384]{2,1,0:T(8,128)(2,1)}), bf16[64,112,384]{2,1,0:T(8,128)(2,1)}, u32[]{:S(2)}, u32[]{:S(2)}) async-start(bf16[64,112,384]{2,1,0:T(8,128)(2,1)} %get-tuple-element.30), calls=%async_computation.1 | async-start | bytes 11010048 | tf_op jit(solution)/shard_map/all_to_all | solution.py:434
  103.4 62.4 %collective-permute-start.2 = (bf16[64,168,128]{2,1,0:T(8,128)(2,1)S(1)}, bf16[64,168,128]{2,1,0:T(8,128)(2,1)S(1)}, u32[]{:S(2)}, u32[]{:S(2)}) collective-permute-start(bf16[64,168,128]{2,1,0:T(8,128)(2,1)S(1)} %all-to-all-done.held), channel_id=1, source_target_pairs={{0,2},{1,3},{2,0},{3,1},{4,6},{5,7},{6,4},{7,5},{8,10},{9,11},{10,... | collective-permute-start | bytes 8257544 | tf_op jit(solution)/shard_map/ppermute | solution.py:431
  165.8 1.6 copy-start.7
  227.4 62.5 %all-to-all-start.2 = ((bf16[64,48,384]{2,1,0:T(8,128)(2,1)}), bf16[64,48,384]{2,1,0:T(8,128)(2,1)}, u32[]{:S(2)}, u32[]{:S(2)}) async-start(bf16[64,48,384]{2,1,0:T(8,128)(2,1)} %far.1), calls=%async_computation.2 | async-start | bytes 4718592 | tf_op jit(solution)/shard_map/all_to_all | solution.py:434
  233.4 7.3 %copy-start.5 = (s32[96,2]{0,1:T(2,128)S(1)}, s32[96,2]{0,1:T(2,128)}, u32[]{:S(2)}) copy-start(s32[96,2]{0,1:T(2,128)} %param.9) | copy-start | bytes 2308
  233.4 8.8 %copy-start.4 = (f32[24,40]{1,0:T(8,128)S(1)}, f32[24,40]{1,0:T(8,128)}, u32[]{:S(2)}) copy-start(f32[24,40]{1,0:T(8,128)} %param.12) | copy-start | bytes 11524
  233.4 9.2 %copy-start.6 = (s32[192]{0:T(256)S(1)}, s32[192]{0:T(256)}, u32[]{:S(2)}) copy-start(s32[192]{0:T(256)} %get-tuple-element.22) | copy-start | bytes 2308
  233.4 9.4 %copy-start.3 = (bf16[24,1600]{1,0:T(8,128)(2,1)S(1)}, bf16[24,1600]{1,0:T(8,128)(2,1)}, u32[]{:S(2)}) copy-start(bf16[24,1600]{1,0:T(8,128)(2,1)} %param.11) | copy-start | bytes 230404
  238.0 51.9 %collective-permute-start.4 = (bf16[64,40,384]{2,1,0:T(8,128)(2,1)}, bf16[64,40,384]{2,1,0:T(8,128)(2,1)S(1)}, u32[]{:S(2)}, u32[]{:S(2)}) collective-permute-start(bf16[64,40,384]{2,1,0:T(8,128)(2,1)} %get-tuple-element.39), channel_id=1, source_target_pairs={{0,1},{1,2},{2,3},{3,0},{4,5},{5,6},{6,7},{7,4},{8,9},{9,10},{10,1... | collective-permute-start | bytes 5898248 | tf_op jit(solution)/shard_map/ppermute | solution.py:431
  238.0 51.9 %collective-permute-start.3 = (bf16[64,40,384]{2,1,0:T(8,128)(2,1)}, bf16[64,40,384]{2,1,0:T(8,128)(2,1)}, u32[]{:S(2)}, u32[]{:S(2)}) collective-permute-start(bf16[64,40,384]{2,1,0:T(8,128)(2,1)} %get-tuple-element.40), channel_id=1, source_target_pairs={{0,3},{1,0},{2,1},{3,2},{4,7},{5,4},{6,5},{7,6},{8,11},{9,8},{10,9... | collective-permute-start | bytes 5898248 | tf_op jit(solution)/shard_map/ppermute | solution.py:431
  290.0 16.3 %copy-start.2 = (f32[24,1600]{1,0:T(8,128)S(1)}, f32[24,1600]{1,0:T(8,128)}, u32[]{:S(2)}) copy-start(f32[24,1600]{1,0:T(8,128)} %convert_multiply_fusion) | copy-start | bytes 460804
  295.2 7.2 %collective-permute-start.5 = (f32[24,1600]{1,0:T(8,128)S(1)}, f32[24,1600]{1,0:T(8,128)S(1)}, u32[]{:S(2)}, u32[]{:S(2)}) collective-permute-start(f32[24,1600]{1,0:T(8,128)S(1)} %get-tuple-element.35), channel_id=1, source_target_pairs={{0,2},{1,3},{2,0},{3,1},{4,6},{5,7},{6,4},{7,5},{8,10},{9,11},{10,... | collective-permute-start | bytes 460808 | tf_op jit(solution)/shard_map/ppermute | solution.py:431
  296.0 10.3 %collective-permute-start.6 = (f32[24,1600]{1,0:T(8,128)S(1)}, f32[24,1600]{1,0:T(8,128)S(1)}, u32[]{:S(2)}, u32[]{:S(2)}) collective-permute-start(f32[24,1600]{1,0:T(8,128)S(1)} %get-tuple-element.36), channel_id=1, source_target_pairs={{0,1},{1,2},{2,3},{3,0},{4,5},{5,6},{6,7},{7,4},{8,9},{9,10},{10,1... | collective-permute-start | bytes 460808 | tf_op jit(solution)/shard_map/ppermute | solution.py:431
  296.0 10.3 %collective-permute-start.7 = (f32[24,1600]{1,0:T(8,128)S(1)}, f32[24,1600]{1,0:T(8,128)S(1)}, u32[]{:S(2)}, u32[]{:S(2)}) collective-permute-start(f32[24,1600]{1,0:T(8,128)S(1)} %get-tuple-element.37), channel_id=1, source_target_pairs={{0,3},{1,0},{2,1},{3,2},{4,7},{5,4},{6,5},{7,6},{8,11},{9,8},{10,9... | collective-permute-start | bytes 460808 | tf_op jit(solution)/shard_map/ppermute | solution.py:431

commit v6 on v5

--- a/solution.py
+++ b/solution.py
@@ -9,6 +9,7 @@
 
 CAP = 4
 TOGETHER = 8
+SIZES = (6, 12)
 
 
 LANES = 128
@@ -159,33 +160,39 @@
     keeper, naux, npao = own.shape
     items, tail, _ = rest.shape
     main = npno - tail
-    loads = [
-        pltpu.make_async_copy(
-            share.at[o], blocks.at[o, pl.ds(k * naux, naux)], sems.at[4 + 3 * o + k]
-        )
-        for o in range(keeper)
-        for k, share in enumerate((own, above, below))
-    ]
-    for load in loads:
-        load.start()
+
+    def loads(o):
+        return [
+            pltpu.make_async_copy(
+                share.at[o], blocks.at[o, pl.ds(k * naux, naux)], sems.at[4 + 3 * o + k]
+            )
+            for k, share in enumerate((own, above, below))
+        ]
+
+    for o in range(keeper):
+        for load in loads(o):
+            load.start()
     sort_entries(held, number, row, count, order, sems.at[1], keeper, npno * npao // LANES)
 
     def goes(e):
         return pltpu.make_async_copy(halves.at[e], out.at[e], sems.at[2])
 
-    for o in range(keeper):
-        for k in range(3):
-            loads[3 * o + k].wait()
+    def orbital(o, _):
+        for load in loads(o):
+            load.wait()
         n = count[o]
 
-        def block(b, _):
-            at = [b * TOGETHER + t for t in range(TOGETHER)]
+        def block(first, size):
+            at = [first + t for t in range(size)]
             ids = [order[o * items + jnp.minimum(k, n - 1)] for k in at]
             for t, e in enumerate(ids):
                 for rows, lanes, place in pieces(npno, npao):
                     stacked[t * npno + rows.start : t * npno + rows.stop, lanes] = held[e, place, :]
             value = lax.dot_general(
-                stacked[...], blocks[o], (((1,), (1,)), ((), ())), preferred_element_type=jnp.float32
+                stacked[: size * npno],
+                blocks[o],
+                (((1,), (1,)), ((), ())),
+                preferred_element_type=jnp.float32,
             )
             for t, e in enumerate(ids):
                 rows = value[t * npno : (t + 1) * npno].astype(out.dtype)
@@ -199,9 +206,30 @@
                 def _():
                     goes(e).start()
 
-            return 0
-
-        lax.fori_loop(0, (n + TOGETHER - 1) // TOGETHER, block, 0)
+        most = SIZES[-1]
+        if len(SIZES) == 1:
+
+            def wide(b, _):
+                block(b * most, most)
+                return 0
+
+            lax.fori_loop(0, (n + most - 1) // most, wide, 0)
+        else:
+            whole = (n + most - SIZES[0] - 1) // most
+
+            def wide(b, _):
+                block(b * most, most)
+                return 0
+
+            lax.fori_loop(0, whole, wide, 0)
+
+            @pl.when(n > whole * most)
+            def _():
+                block(whole * most, SIZES[0])
+
+        return 0
+
+    lax.fori_loop(0, keeper, orbital, 0)
 
     back = pltpu.make_async_copy(rest, rest_out, sems.at[3])
     back.start()
@@ -233,7 +261,7 @@
             pltpu.SMEM((keeper + 1,), jnp.int32),
             pltpu.VMEM((SPARE, LANES), jnp.int32),
             pltpu.SMEM((SPARE, LANES), jnp.int32),
-            pltpu.VMEM((TOGETHER * npno, npao), jnp.bfloat16),
+            pltpu.VMEM((SIZES[-1] * npno, npao), jnp.bfloat16),
             pltpu.VMEM((keeper, 3 * naux, npao), jnp.bfloat16),
             pltpu.VMEM((items, rows, naux), jnp.bfloat16),
             pltpu.VMEM((items, tail, naux), jnp.bfloat16),
@@ -249,18 +277,16 @@
     )(record, own, above, below)
 
 
-def far_kernel(npno, record, ints, rest_in, out, held, order, count, number, row, stacked, blocks, halves, rest, sems):
+def far_kernel(
+    npno, held, ints, rest, out, order, count, number, row, stacked, blocks, halves, sems
+):
     keeper, naux, npao = ints.shape
     items = held.shape[0]
     deep = stacked.shape[1]
-    whole = pltpu.make_async_copy(record, held, sems.at[0])
-    load = pltpu.make_async_copy(ints, blocks, sems.at[1])
-    rest_load = pltpu.make_async_copy(rest_in, rest, sems.at[2])
-    for copy in (whole, load, rest_load):
-        copy.start()
+    load = pltpu.make_async_copy(ints, blocks, sems.at[0])
+    load.start()
     stacked[...] = jnp.zeros_like(stacked)
-    whole.wait()
-    sort_entries(held, number, row, count, order, sems.at[3], keeper, npno * npao // LANES)
+    sort_entries(held, number, row, count, order, sems.at[1], keeper, npno * npao // LANES)
     load.wait()
     for o in range(keeper):
         n = count[o]
@@ -281,14 +307,12 @@
 
         lax.fori_loop(0, (n + TOGETHER - 1) // TOGETHER, block, 0)
 
-    rest_load.wait()
-
     def join(e, _):
         halves[e, npno:] = rest[e]
         return 0
 
     lax.fori_loop(0, items, join, 0, unroll=8)
-    back = pltpu.make_async_copy(halves, out, sems.at[4])
+    back = pltpu.make_async_copy(halves, out, sems.at[2])
     back.start()
     back.wait()
 
@@ -297,13 +321,13 @@
     keeper, naux, npao = ints.shape
     items, tail, _ = rest.shape
     hbm = pl.BlockSpec(memory_space=pltpu.HBM)
+    vmem = pl.BlockSpec(memory_space=pltpu.VMEM)
     return pl.pallas_call(
         functools.partial(far_kernel, npno),
         out_shape=jax.ShapeDtypeStruct((items, npno + tail, naux), jnp.bfloat16),
-        in_specs=[hbm] * 3,
+        in_specs=[vmem, hbm, vmem],
         out_specs=hbm,
         scratch_shapes=[
-            pltpu.VMEM(record.shape, record.dtype),
             pltpu.SMEM(((keeper + 1) * items,), jnp.int32),
             pltpu.SMEM((keeper + 1,), jnp.int32),
             pltpu.VMEM((SPARE, LANES), jnp.int32),
@@ -311,10 +335,9 @@
             pltpu.VMEM((TOGETHER, -(-npno // 16) * 16, npao), jnp.bfloat16),
             pltpu.VMEM(ints.shape, jnp.bfloat16),
             pltpu.VMEM((items, npno + tail, naux), jnp.bfloat16),
-            pltpu.VMEM(rest.shape, jnp.bfloat16),
-            pltpu.SemaphoreType.DMA((5,)),
+            pltpu.SemaphoreType.DMA((3,)),
         ],
-        compiler_params=pltpu.CompilerParams(vmem_limit_bytes=60 * 2**20),
+        compiler_params=pltpu.CompilerParams(vmem_limit_bytes=48 * 2**20),
         cost_estimate=pl.CostEstimate(
             flops=16 * items * npno * npao * naux,
             bytes_accessed=2 * (keeper * npao * naux + items * npno * (npao + naux)),

time: 308 us -> 306 us (level)
    all_to_all x3, waiting for transfers between devices: 112 us -> 115 us  [there(): return lax.all_to_all(value, 'orb', split_axis=0, concat_axis=0, tiled=True)]
where the time goes in v6:
time: 306 us; the launch traced here: 305 us
  waiting for transfers between devices  234 us (76%)
  starting transfers between devices  35.3 us (12%)
  Pallas kernels  26.7 us (9%)
  local copies, waits for them, and re-layouts  7.91 us (3%)
    ppermute x8, waiting for transfers between devices, shifted(): lax.ppermute(value, 'rep', [(i, (i + by) % n_rep) for i in range(n_rep)])  119 us
    all_to_all x3, waiting for transfers between devices, there(): return lax.all_to_all(value, 'orb', split_axis=0, concat_axis=0, tiled=True)  115 us
    all_to_all x3, starting transfers between devices, there(): return lax.all_to_all(value, 'orb', split_axis=0, concat_axis=0, tiled=True)  24.7 us
    ppermute x8, starting transfers between devices, shifted(): lax.ppermute(value, 'rep', [(i, (i + by) % n_rep) for i in range(n_rep)])  10.5 us
    pallas_call x1, Pallas kernels, near_halves(): pl.pallas_call(functools.partial(near_kernel, npno), out_shape=[jax.Shape...  9.22 us
    pallas_call x1, Pallas kernels, far_halves(): pl.pallas_call(functools.partial(far_kernel, npno), out_shape=jax.ShapeDt...  7.16 us
  transfers between devices with their start and end apart: 11, of which 8 were waited for; matrix products, arithmetic and copies ran while one was open for 3% of the time, Pallas kernels for 4%

profile of v6, /device:TPU:1, one launch (start us, length us, event | category | flops | bytes accessed | tf_op | source)
XLA Modules:
  0.0 305.4 jit_solution(8302137206407003626)
XLA Ops:
  0.0 2.1 collective-permute-start.1
  2.1 1.5 collective-permute-start
  3.7 5.1 %route.1 = (bf16[64,168,128]{2,1,0:T(8,128)(2,1)}, s32[192]{0:T(256)}) custom-call(s32[2,96]{1,0:T(2,128)} %bitcast.8, s32[512]{0:T(512)} %place.1, s32[1]{0:T(128)} %bitcast.1.plane, bf16[192,40,512]{2,1,0:T(8,128)(2,1)} %bitcast.7), custom_call_target="tpu_custom_call" | custom-call | tf_op jit(solution)/shard_map/route/pallas_call | solution.py:106
  8.8 12.6 %all-to-all-start = ((bf16[64,168,128]{2,1,0:T(8,128)(2,1)}), bf16[64,168,128]{2,1,0:T(8,128)(2,1)S(1)}, u32[]{:S(2)}, u32[]{:S(2)}) async-start(bf16[64,168,128]{2,1,0:T(8,128)(2,1)} %get-tuple-element.23), calls=%async_computation | async-start | bytes 5505024 | tf_op jit(solution)/shard_map/all_to_all | solution.py:457
  21.4 48.3 %collective-permute-done.1.below_in = bf16[8,384,512]{2,1,0:T(8,128)(2,1)} collective-permute-done((bf16[8,384,512]{2,1,0:T(8,128)(2,1)}, bf16[8,384,512]{2,1,0:T(8,128)(2,1)}, u32[]{:S(2)}, u32[]{:S(2)}) %collective-permute-start.1) | collective-permute-done | bytes 3145760 | tf_op jit(solution)/shard_map/ppermute | solution.py:454
  69.7 1.3 collective-permute-done.above_in
  70.9 15.5 %all-to-all-done.held = bf16[64,168,128]{2,1,0:T(8,128)(2,1)S(1)} async-done(((bf16[64,168,128]{2,1,0:T(8,128)(2,1)}), bf16[64,168,128]{2,1,0:T(8,128)(2,1)S(1)}, u32[]{:S(2)}, u32[]{:S(2)}) %all-to-all-start) | async-done | bytes 2752544 | tf_op jit(solution)/shard_map/all_to_all | solution.py:457
  86.4 9.2 %near.1 = (bf16[64,112,384]{2,1,0:T(8,128)(2,1)}, bf16[64,8,384]{2,1,0:T(8,128)(2,1)S(1)}) custom-call(bf16[64,168,128]{2,1,0:T(8,128)(2,1)S(1)} %all-to-all-done.held, bf16[8,384,512]{2,1,0:T(8,128)(2,1)} %ints.1, bf16[8,384,512]{2,1,0:T(8,128)(2,1)} %get-tuple-element.27.above, bf16[8,384,512]{2,1,0:T(8,128)(2,1)} %get-tuple-element.28.below), custom_call_target="tpu_custom_call" | custom-call | flops 3019898880 | bytes 17956864 | tf_op jit(solution)/shard_map/near/pallas_call | solution.py:251
  95.7 6.2 %all-to-all-start.1 = ((bf16[64,112,384]{2,1,0:T(8,128)(2,1)}), bf16[64,112,384]{2,1,0:T(8,128)(2,1)}, u32[]{:S(2)}, u32[]{:S(2)}) async-start(bf16[64,112,384]{2,1,0:T(8,128)(2,1)} %get-tuple-element.30), calls=%async_computation.1 | async-start | bytes 11010048 | tf_op jit(solution)/shard_map/all_to_all | solution.py:457
  101.8 0.8 collective-permute-start.2
  102.6 61.6 %collective-permute-done.2.held = bf16[64,168,128]{2,1,0:T(8,128)(2,1)S(1)} collective-permute-done((bf16[64,168,128]{2,1,0:T(8,128)(2,1)S(1)}, bf16[64,168,128]{2,1,0:T(8,128)(2,1)S(1)}, u32[]{:S(2)}, u32[]{:S(2)}) %collective-permute-start.2) | collective-permute-done | bytes 2752544 | tf_op jit(solution)/shard_map/ppermute | solution.py:454
  164.3 7.2 %far.1 = bf16[64,48,384]{2,1,0:T(8,128)(2,1)} custom-call(bf16[64,168,128]{2,1,0:T(8,128)(2,1)S(1)} %collective-permute-done.2.held, bf16[8,384,512]{2,1,0:T(8,128)(2,1)} %ints.1, bf16[64,8,384]{2,1,0:T(8,128)(2,1)S(1)} %get-tuple-element.29.rest), custom_call_target="tpu_custom_call" | custom-call | flops 8053063680 | bytes 7733248 | tf_op jit(solution)/shard_map/far/pallas_call | solution.py:325
  171.4 54.4 %all-to-all-done.1 = bf16[64,112,384]{2,1,0:T(8,128)(2,1)} async-done(((bf16[64,112,384]{2,1,0:T(8,128)(2,1)}), bf16[64,112,384]{2,1,0:T(8,128)(2,1)}, u32[]{:S(2)}, u32[]{:S(2)}) %all-to-all-start.1) | async-done | bytes 5505056 | tf_op jit(solution)/shard_map/all_to_all | solution.py:457
  225.8 6.0 %all-to-all-start.2 = ((bf16[64,48,384]{2,1,0:T(8,128)(2,1)}), bf16[64,48,384]{2,1,0:T(8,128)(2,1)}, u32[]{:S(2)}, u32[]{:S(2)}) async-start(bf16[64,48,384]{2,1,0:T(8,128)(2,1)} %far.1), calls=%async_computation.2 | async-start | bytes 4718592 | tf_op jit(solution)/shard_map/all_to_all | solution.py:457
  231.8 4.4 %fusion.5 = (bf16[64,40,384]{2,1,0:T(8,128)(2,1)}, bf16[64,40,384]{2,1,0:T(8,128)(2,1)}) fusion(bf16[64,112,384]{2,1,0:T(8,128)(2,1)} %all-to-all-done.1), kind=kLoop, calls=%fused_computation.25 | loop fusion | bytes 7864320 | tf_op jit(solution)/shard_map/slice | solution.py:476
  236.3 2.7 collective-permute-start.3
  239.0 0.1 constant_dynamic-slice_fusion
  239.1 0.7 gather_fusion.1
  239.8 0.7 gather_fusion
  240.5 0.2 broadcast_add_fusion
  240.7 0.2 add.79
  240.9 0.1 reshape.25
  241.0 0.1 reshape.26.place
  241.1 0.7 convert_multiply_fusion
  241.9 1.6 slice.15.first
  243.4 44.9 %all-to-all-done.2.last = bf16[64,48,384]{2,1,0:T(8,128)(2,1)} async-done(((bf16[64,48,384]{2,1,0:T(8,128)(2,1)}), bf16[64,48,384]{2,1,0:T(8,128)(2,1)}, u32[]{:S(2)}, u32[]{:S(2)}) %all-to-all-start.2) | async-done | bytes 2359328 | tf_op jit(solution)/shard_map/all_to_all | solution.py:457
  288.4 5.2 %exchange.1 = (f32[24,1600]{1,0:T(8,128)S(1)}, f32[24,1600]{1,0:T(8,128)S(1)}, f32[24,1600]{1,0:T(8,128)S(1)}, f32[24,1600]{1,0:T(8,128)S(1)}) custom-call(s32[192]{0:T(256)S(1)} %reshape.26.place, bf16[64,32,384]{2,1,0:T(8,128)(2,1)S(1)} %slice.15.first, bf16[64,40,384]{2,1,0:T(8,128)(2,1)} %collective-permute-done.3.above, ...), custom_call_target="tpu_custom_call" | custom-call | tf_op jit(solution)/shard_map/exchange/pallas_call | solution.py:420
  293.6 0.8 collective-permute-start.5
  294.4 2.7 collective-permute-start.7
  297.1 3.8 %collective-permute-done.5 = f32[24,1600]{1,0:T(8,128)S(1)} collective-permute-done((f32[24,1600]{1,0:T(8,128)S(1)}, f32[24,1600]{1,0:T(8,128)S(1)}, u32[]{:S(2)}, u32[]{:S(2)}) %collective-permute-start.5) | collective-permute-done | bytes 153632 | tf_op jit(solution)/shard_map/ppermute | solution.py:454
  300.8 3.9 %collective-permute-done.6 = f32[24,1600]{1,0:T(8,128)S(1)} collective-permute-done((f32[24,1600]{1,0:T(8,128)S(1)}, f32[24,1600]{1,0:T(8,128)S(1)}, u32[]{:S(2)}, u32[]{:S(2)}) %collective-permute-start.6) | collective-permute-done | bytes 153632 | tf_op jit(solution)/shard_map/ppermute | solution.py:454
  304.7 0.7 add_add_fusion
  (24 shorter events, 0.1 us)
Async XLA Ops:
  0.0 239.1 %copy-start = (f32[512]{0:T(512)S(1)}, f32[512]{0:T(512)}, u32[]{:S(2)}) copy-start(f32[512]{0:T(512)} %param.13) | copy-start | bytes 6148
  0.0 69.7 %collective-permute-start.1 = (bf16[8,384,512]{2,1,0:T(8,128)(2,1)}, bf16[8,384,512]{2,1,0:T(8,128)(2,1)}, u32[]{:S(2)}, u32[]{:S(2)}) collective-permute-start(bf16[8,384,512]{2,1,0:T(8,128)(2,1)} %ints.1), channel_id=1, source_target_pairs={{0,1},{1,2},{2,3},{3,0},{4,5},{5,6},{6,7},{7,4},{8,9},{9,10},{10,1... | collective-permute-start | bytes 9437192 | tf_op jit(solution)/shard_map/ppermute | solution.py:454
  2.1 68.8 %collective-permute-start = (bf16[8,384,512]{2,1,0:T(8,128)(2,1)}, bf16[8,384,512]{2,1,0:T(8,128)(2,1)}, u32[]{:S(2)}, u32[]{:S(2)}) collective-permute-start(bf16[8,384,512]{2,1,0:T(8,128)(2,1)} %ints.1), channel_id=1, source_target_pairs={{0,3},{1,0},{2,1},{3,2},{4,7},{5,4},{6,5},{7,6},{8,11},{9,8},{10,9... | collective-permute-start | bytes 9437192 | tf_op jit(solution)/shard_map/ppermute | solution.py:454
  8.8 77.7 %all-to-all-start = ((bf16[64,168,128]{2,1,0:T(8,128)(2,1)}), bf16[64,168,128]{2,1,0:T(8,128)(2,1)S(1)}, u32[]{:S(2)}, u32[]{:S(2)}) async-start(bf16[64,168,128]{2,1,0:T(8,128)(2,1)} %get-tuple-element.23), calls=%async_computation | async-start | bytes 5505024 | tf_op jit(solution)/shard_map/all_to_all | solution.py:457
  95.7 130.2 %all-to-all-start.1 = ((bf16[64,112,384]{2,1,0:T(8,128)(2,1)}), bf16[64,112,384]{2,1,0:T(8,128)(2,1)}, u32[]{:S(2)}, u32[]{:S(2)}) async-start(bf16[64,112,384]{2,1,0:T(8,128)(2,1)} %get-tuple-element.30), calls=%async_computation.1 | async-start | bytes 11010048 | tf_op jit(solution)/shard_map/all_to_all | solution.py:457
  101.8 62.4 %collective-permute-start.2 = (bf16[64,168,128]{2,1,0:T(8,128)(2,1)S(1)}, bf16[64,168,128]{2,1,0:T(8,128)(2,1)S(1)}, u32[]{:S(2)}, u32[]{:S(2)}) collective-permute-start(bf16[64,168,128]{2,1,0:T(8,128)(2,1)S(1)} %all-to-all-done.held), channel_id=1, source_target_pairs={{0,2},{1,3},{2,0},{3,1},{4,6},{5,7},{6,4},{7,5},{8,10},{9,11},{10,... | collective-permute-start | bytes 8257544 | tf_op jit(solution)/shard_map/ppermute | solution.py:454
  225.8 62.5 %all-to-all-start.2 = ((bf16[64,48,384]{2,1,0:T(8,128)(2,1)}), bf16[64,48,384]{2,1,0:T(8,128)(2,1)}, u32[]{:S(2)}, u32[]{:S(2)}) async-start(bf16[64,48,384]{2,1,0:T(8,128)(2,1)} %far.1), calls=%async_computation.2 | async-start | bytes 4718592 | tf_op jit(solution)/shard_map/all_to_all | solution.py:457
  231.8 7.2 %copy-start.4 = (s32[96,2]{0,1:T(2,128)S(1)}, s32[96,2]{0,1:T(2,128)}, u32[]{:S(2)}) copy-start(s32[96,2]{0,1:T(2,128)} %param.9) | copy-start | bytes 2308
  231.8 8.7 %copy-start.3 = (f32[24,40]{1,0:T(8,128)S(1)}, f32[24,40]{1,0:T(8,128)}, u32[]{:S(2)}) copy-start(f32[24,40]{1,0:T(8,128)} %param.12) | copy-start | bytes 11524
  231.8 9.1 %copy-start.5 = (s32[192]{0:T(256)S(1)}, s32[192]{0:T(256)}, u32[]{:S(2)}) copy-start(s32[192]{0:T(256)} %get-tuple-element.22) | copy-start | bytes 2308
  231.8 9.3 %copy-start.2 = (bf16[24,1600]{1,0:T(8,128)(2,1)S(1)}, bf16[24,1600]{1,0:T(8,128)(2,1)}, u32[]{:S(2)}) copy-start(bf16[24,1600]{1,0:T(8,128)(2,1)} %param.11) | copy-start | bytes 230404
  236.3 52.1 %collective-permute-start.4 = (bf16[64,40,384]{2,1,0:T(8,128)(2,1)}, bf16[64,40,384]{2,1,0:T(8,128)(2,1)S(1)}, u32[]{:S(2)}, u32[]{:S(2)}) collective-permute-start(bf16[64,40,384]{2,1,0:T(8,128)(2,1)} %get-tuple-element.39), channel_id=1, source_target_pairs={{0,1},{1,2},{2,3},{3,0},{4,5},{5,6},{6,7},{7,4},{8,9},{9,10},{10,1... | collective-permute-start | bytes 5898248 | tf_op jit(solution)/shard_map/ppermute | solution.py:454
  236.3 52.1 %collective-permute-start.3 = (bf16[64,40,384]{2,1,0:T(8,128)(2,1)}, bf16[64,40,384]{2,1,0:T(8,128)(2,1)}, u32[]{:S(2)}, u32[]{:S(2)}) collective-permute-start(bf16[64,40,384]{2,1,0:T(8,128)(2,1)} %get-tuple-element.40), channel_id=1, source_target_pairs={{0,3},{1,0},{2,1},{3,2},{4,7},{5,4},{6,5},{7,6},{8,11},{9,8},{10,9... | collective-permute-start | bytes 5898248 | tf_op jit(solution)/shard_map/ppermute | solution.py:454
  288.4 16.3 %copy-start.1 = (f32[24,1600]{1,0:T(8,128)S(1)}, f32[24,1600]{1,0:T(8,128)}, u32[]{:S(2)}) copy-start(f32[24,1600]{1,0:T(8,128)} %convert_multiply_fusion) | copy-start | bytes 460804
  293.6 7.2 %collective-permute-start.5 = (f32[24,1600]{1,0:T(8,128)S(1)}, f32[24,1600]{1,0:T(8,128)S(1)}, u32[]{:S(2)}, u32[]{:S(2)}) collective-permute-start(f32[24,1600]{1,0:T(8,128)S(1)} %get-tuple-element.35), channel_id=1, source_target_pairs={{0,2},{1,3},{2,0},{3,1},{4,6},{5,7},{6,4},{7,5},{8,10},{9,11},{10,... | collective-permute-start | bytes 460808 | tf_op jit(solution)/shard_map/ppermute | solution.py:454
  294.4 10.3 %collective-permute-start.6 = (f32[24,1600]{1,0:T(8,128)S(1)}, f32[24,1600]{1,0:T(8,128)S(1)}, u32[]{:S(2)}, u32[]{:S(2)}) collective-permute-start(f32[24,1600]{1,0:T(8,128)S(1)} %get-tuple-element.36), channel_id=1, source_target_pairs={{0,1},{1,2},{2,3},{3,0},{4,5},{5,6},{6,7},{7,4},{8,9},{9,10},{10,1... | collective-permute-start | bytes 460808 | tf_op jit(solution)/shard_map/ppermute | solution.py:454
  294.4 10.3 %collective-permute-start.7 = (f32[24,1600]{1,0:T(8,128)S(1)}, f32[24,1600]{1,0:T(8,128)S(1)}, u32[]{:S(2)}, u32[]{:S(2)}) collective-permute-start(f32[24,1600]{1,0:T(8,128)S(1)} %get-tuple-element.37), channel_id=1, source_target_pairs={{0,3},{1,0},{2,1},{3,2},{4,7},{5,4},{6,5},{7,6},{8,11},{9,8},{10,9... | collective-permute-start | bytes 460808 | tf_op jit(solution)/shard_map/ppermute | solution.py:454

commit v7 on v6

--- a/solution.py
+++ b/solution.py
@@ -9,7 +9,7 @@
 
 CAP = 4
 TOGETHER = 8
-SIZES = (6, 12)
+SIZES = (8, 12)
 
 
 LANES = 128
@@ -37,7 +37,7 @@
 
 
 def route_kernel(
-    keeper, orbitals, place, plane, vectors, sent, slot, count, row, held, record, sems
+    keeper, orbitals, place, plane, source, vectors, sent, slot, count, row, held, record, sems
 ):
     owners, npno, npao = held.shape
     pairs = orbitals.shape[1]
@@ -49,7 +49,7 @@
         return 0
 
     lax.fori_loop(0, owners, clear, 0, unroll=16)
-    mine = plane[0]
+    mine, turn = plane[0], source[0]
 
     def fetch(e, owner):
         return pltpu.make_async_copy(vectors.at[e], held.at[owner], sems.at[0])
@@ -61,9 +61,10 @@
                 owner, of = parted(place[orbitals[side, q]], keeper)
                 position = count[owner]
                 count[owner] = position + 1
-                slot[q * 2 + side] = position * owners + owner
-
-                @pl.when(position == mine)
+                turned = parted(position + owner + turn, CAP)[1]
+                slot[q * 2 + side] = turned * owners + owner
+
+                @pl.when(turned == mine)
                 def _():
                     row[owner] = of
                     fetch(q * 2 + side, owner).start()
@@ -98,7 +99,7 @@
         out.wait()
 
 
-def route(orbitals, orbital_place, plane, vectors, owners, keeper):
+def route(orbitals, orbital_place, at, vectors, owners, keeper):
     entries, npno, npao = vectors.shape
     depth = npno * npao // LANES + SPARE
     smem = pl.BlockSpec(memory_space=pltpu.SMEM)
@@ -109,7 +110,7 @@
             jax.ShapeDtypeStruct((owners, depth, LANES), vectors.dtype),
             jax.ShapeDtypeStruct((entries,), jnp.int32),
         ),
-        in_specs=[smem, smem, smem, hbm],
+        in_specs=[smem] * 4 + [hbm],
         out_specs=(hbm, smem),
         scratch_shapes=[
             pltpu.SMEM((owners,), jnp.int32),
@@ -120,7 +121,7 @@
         ],
         compiler_params=pltpu.CompilerParams(vmem_limit_bytes=60 * 2**20),
         name="route",
-    )(orbitals, orbital_place, plane, vectors)
+    )(orbitals, orbital_place, *at, vectors)
 
 
 def sort_entries(held, number, row, count, order, sem, keeper, at):
@@ -445,6 +446,7 @@
     n_orb = lax.axis_size("orb")
     n_rep = lax.axis_size("rep")
     rep = lax.axis_index("rep")
+    at = [lax.axis_index(name).reshape(1).astype(jnp.int32) for name in ("rep", "orb")]
     keeper, naux, npao = ints_block.shape
     pair_dev = pair_vectors.shape[0]
     npno = pair_vectors.shape[2]
@@ -457,7 +459,7 @@
         return lax.all_to_all(value, "orb", split_axis=0, concat_axis=0, tiled=True)
 
     sent, slot = route(
-        pair_orbitals.T, orbital_place, rep.reshape(1).astype(jnp.int32), vectors, n_orb, keeper
+        pair_orbitals.T, orbital_place, at, vectors, n_orb, keeper
     )
     own = there(sent)
 

time: 306 us -> 305 us (level)
  waiting for transfers between devices: 234 us -> 230 us
where the time goes in v7:
time: 305 us; the launch traced here: 304 us
  waiting for transfers between devices  230 us (75%)
  starting transfers between devices  36.8 us (12%)
  Pallas kernels  27.4 us (9%)
  local copies, waits for them, and re-layouts  7.92 us (3%)
    ppermute x8, waiting for transfers between devices, shifted(): lax.ppermute(value, 'rep', [(i, (i + by) % n_rep) for i in range(n_rep)])  116 us
    all_to_all x3, waiting for transfers between devices, there(): return lax.all_to_all(value, 'orb', split_axis=0, concat_axis=0, tiled=True)  114 us
    all_to_all x3, starting transfers between devices, there(): return lax.all_to_all(value, 'orb', split_axis=0, concat_axis=0, tiled=True)  23.9 us
    ppermute x8, starting transfers between devices, shifted(): lax.ppermute(value, 'rep', [(i, (i + by) % n_rep) for i in range(n_rep)])  12.9 us
    pallas_call x1, Pallas kernels, near_halves(): pl.pallas_call(functools.partial(near_kernel, npno), out_shape=[jax.Shape...  8.68 us
    pallas_call x1, Pallas kernels, far_halves(): pl.pallas_call(functools.partial(far_kernel, npno), out_shape=jax.ShapeDt...  8.04 us
  transfers between devices with their start and end apart: 11, of which 8 were waited for; matrix products, arithmetic and copies ran while one was open for 3% of the time, Pallas kernels for 4%

profile of v7, /device:TPU:1, one launch (start us, length us, event | category | flops | bytes accessed | tf_op | source)
XLA Modules:
  0.0 304.4 jit_solution(10296280579492790108)
XLA Ops:
  0.0 2.1 collective-permute-start.1
  2.1 1.5 collective-permute-start
  3.7 5.5 %route.1 = (bf16[64,168,128]{2,1,0:T(8,128)(2,1)}, s32[192]{0:T(256)}) custom-call(s32[2,96]{1,0:T(2,128)} %bitcast.9, s32[512]{0:T(512)} %place.1, s32[1]{0:T(128)} %bitcast.1.plane, s32[1]{0:T(128)} %bitcast.2.source, bf16[192,40,512]{2,1,0:T(8,128)(2,1)} %bitcast.8), custom_call_target="tpu_custom_call" | custom-call | tf_op jit(solution)/shard_map/route/pallas_call | solution.py:107
  9.1 12.6 %all-to-all-start = ((bf16[64,168,128]{2,1,0:T(8,128)(2,1)}), bf16[64,168,128]{2,1,0:T(8,128)(2,1)S(1)}, u32[]{:S(2)}, u32[]{:S(2)}) async-start(bf16[64,168,128]{2,1,0:T(8,128)(2,1)} %get-tuple-element.23), calls=%async_computation | async-start | bytes 5505024 | tf_op jit(solution)/shard_map/all_to_all | solution.py:459
  21.7 48.0 %collective-permute-done.1.below_in = bf16[8,384,512]{2,1,0:T(8,128)(2,1)} collective-permute-done((bf16[8,384,512]{2,1,0:T(8,128)(2,1)}, bf16[8,384,512]{2,1,0:T(8,128)(2,1)}, u32[]{:S(2)}, u32[]{:S(2)}) %collective-permute-start.1) | collective-permute-done | bytes 3145760 | tf_op jit(solution)/shard_map/ppermute | solution.py:456
  69.7 1.3 collective-permute-done.above_in
  70.9 15.9 %all-to-all-done.held = bf16[64,168,128]{2,1,0:T(8,128)(2,1)S(1)} async-done(((bf16[64,168,128]{2,1,0:T(8,128)(2,1)}), bf16[64,168,128]{2,1,0:T(8,128)(2,1)S(1)}, u32[]{:S(2)}, u32[]{:S(2)}) %all-to-all-start) | async-done | bytes 2752544 | tf_op jit(solution)/shard_map/all_to_all | solution.py:459
  86.8 8.7 %near.1 = (bf16[64,112,384]{2,1,0:T(8,128)(2,1)}, bf16[64,8,384]{2,1,0:T(8,128)(2,1)S(1)}) custom-call(bf16[64,168,128]{2,1,0:T(8,128)(2,1)S(1)} %all-to-all-done.held, bf16[8,384,512]{2,1,0:T(8,128)(2,1)} %ints.1, bf16[8,384,512]{2,1,0:T(8,128)(2,1)} %get-tuple-element.27.above, bf16[8,384,512]{2,1,0:T(8,128)(2,1)} %get-tuple-element.28.below), custom_call_target="tpu_custom_call" | custom-call | flops 3019898880 | bytes 17956864 | tf_op jit(solution)/shard_map/near/pallas_call | solution.py:252
  95.5 5.4 %all-to-all-start.1 = ((bf16[64,112,384]{2,1,0:T(8,128)(2,1)}), bf16[64,112,384]{2,1,0:T(8,128)(2,1)}, u32[]{:S(2)}, u32[]{:S(2)}) async-start(bf16[64,112,384]{2,1,0:T(8,128)(2,1)} %get-tuple-element.30), calls=%async_computation.1 | async-start | bytes 11010048 | tf_op jit(solution)/shard_map/all_to_all | solution.py:459
  100.8 2.0 collective-permute-start.2
  102.8 60.4 %collective-permute-done.2.held = bf16[64,168,128]{2,1,0:T(8,128)(2,1)S(1)} collective-permute-done((bf16[64,168,128]{2,1,0:T(8,128)(2,1)S(1)}, bf16[64,168,128]{2,1,0:T(8,128)(2,1)S(1)}, u32[]{:S(2)}, u32[]{:S(2)}) %collective-permute-start.2) | collective-permute-done | bytes 2752544 | tf_op jit(solution)/shard_map/ppermute | solution.py:456
  163.3 8.0 %far.1 = bf16[64,48,384]{2,1,0:T(8,128)(2,1)} custom-call(bf16[64,168,128]{2,1,0:T(8,128)(2,1)S(1)} %collective-permute-done.2.held, bf16[8,384,512]{2,1,0:T(8,128)(2,1)} %ints.1, bf16[64,8,384]{2,1,0:T(8,128)(2,1)S(1)} %get-tuple-element.29.rest), custom_call_target="tpu_custom_call" | custom-call | flops 8053063680 | bytes 7733248 | tf_op jit(solution)/shard_map/far/pallas_call | solution.py:326
  171.3 53.5 %all-to-all-done.1 = bf16[64,112,384]{2,1,0:T(8,128)(2,1)} async-done(((bf16[64,112,384]{2,1,0:T(8,128)(2,1)}), bf16[64,112,384]{2,1,0:T(8,128)(2,1)}, u32[]{:S(2)}, u32[]{:S(2)}) %all-to-all-start.1) | async-done | bytes 5505056 | tf_op jit(solution)/shard_map/all_to_all | solution.py:459
  224.8 6.0 %all-to-all-start.2 = ((bf16[64,48,384]{2,1,0:T(8,128)(2,1)}), bf16[64,48,384]{2,1,0:T(8,128)(2,1)}, u32[]{:S(2)}, u32[]{:S(2)}) async-start(bf16[64,48,384]{2,1,0:T(8,128)(2,1)} %far.1), calls=%async_computation.2 | async-start | bytes 4718592 | tf_op jit(solution)/shard_map/all_to_all | solution.py:459
  230.8 4.4 %fusion.5 = (bf16[64,40,384]{2,1,0:T(8,128)(2,1)}, bf16[64,40,384]{2,1,0:T(8,128)(2,1)}) fusion(bf16[64,112,384]{2,1,0:T(8,128)(2,1)} %all-to-all-done.1), kind=kLoop, calls=%fused_computation.25 | loop fusion | bytes 7864320 | tf_op jit(solution)/shard_map/slice | solution.py:478
  235.3 0.6 collective-permute-start.4
  235.9 2.1 collective-permute-start.3
  238.1 0.7 gather_fusion.1
  238.8 0.7 gather_fusion
  239.5 0.2 broadcast_add_fusion
  239.7 0.2 add.79
  239.9 0.1 reshape.29
  240.1 0.7 convert_multiply_fusion
  240.9 1.6 slice.15.first
  242.4 44.9 %all-to-all-done.2.last = bf16[64,48,384]{2,1,0:T(8,128)(2,1)} async-done(((bf16[64,48,384]{2,1,0:T(8,128)(2,1)}), bf16[64,48,384]{2,1,0:T(8,128)(2,1)}, u32[]{:S(2)}, u32[]{:S(2)}) %all-to-all-start.2) | async-done | bytes 2359328 | tf_op jit(solution)/shard_map/all_to_all | solution.py:459
  287.4 5.2 %exchange.1 = (f32[24,1600]{1,0:T(8,128)S(1)}, f32[24,1600]{1,0:T(8,128)S(1)}, f32[24,1600]{1,0:T(8,128)S(1)}, f32[24,1600]{1,0:T(8,128)S(1)}) custom-call(s32[192]{0:T(256)S(1)} %reshape.30.place, bf16[64,32,384]{2,1,0:T(8,128)(2,1)S(1)} %slice.15.first, bf16[64,40,384]{2,1,0:T(8,128)(2,1)} %collective-permute-done.3.above, ...), custom_call_target="tpu_custom_call" | custom-call | tf_op jit(solution)/shard_map/exchange/pallas_call | solution.py:421
  292.6 1.9 collective-permute-start.5
  294.5 0.6 collective-permute-start.6
  295.2 2.1 collective-permute-start.7
  297.2 2.5 collective-permute-done.5
  299.8 3.9 %collective-permute-done.6 = f32[24,1600]{1,0:T(8,128)S(1)} collective-permute-done((f32[24,1600]{1,0:T(8,128)S(1)}, f32[24,1600]{1,0:T(8,128)S(1)}, u32[]{:S(2)}, u32[]{:S(2)}) %collective-permute-start.6) | collective-permute-done | bytes 153632 | tf_op jit(solution)/shard_map/ppermute | solution.py:456
  303.7 0.7 add_add_fusion
  (24 shorter events, 0.3 us)
Async XLA Ops:
  0.0 238.1 %copy-start = (f32[512]{0:T(512)S(1)}, f32[512]{0:T(512)}, u32[]{:S(2)}) copy-start(f32[512]{0:T(512)} %param.13) | copy-start | bytes 6148
  0.0 69.7 %collective-permute-start.1 = (bf16[8,384,512]{2,1,0:T(8,128)(2,1)}, bf16[8,384,512]{2,1,0:T(8,128)(2,1)}, u32[]{:S(2)}, u32[]{:S(2)}) collective-permute-start(bf16[8,384,512]{2,1,0:T(8,128)(2,1)} %ints.1), channel_id=1, source_target_pairs={{0,1},{1,2},{2,3},{3,0},{4,5},{5,6},{6,7},{7,4},{8,9},{9,10},{10,1... | collective-permute-start | bytes 9437192 | tf_op jit(solution)/shard_map/ppermute | solution.py:456
  2.1 68.8 %collective-permute-start = (bf16[8,384,512]{2,1,0:T(8,128)(2,1)}, bf16[8,384,512]{2,1,0:T(8,128)(2,1)}, u32[]{:S(2)}, u32[]{:S(2)}) collective-permute-start(bf16[8,384,512]{2,1,0:T(8,128)(2,1)} %ints.1), channel_id=1, source_target_pairs={{0,3},{1,0},{2,1},{3,2},{4,7},{5,4},{6,5},{7,6},{8,11},{9,8},{10,9... | collective-permute-start | bytes 9437192 | tf_op jit(solution)/shard_map/ppermute | solution.py:456
  9.1 77.7 %all-to-all-start = ((bf16[64,168,128]{2,1,0:T(8,128)(2,1)}), bf16[64,168,128]{2,1,0:T(8,128)(2,1)S(1)}, u32[]{:S(2)}, u32[]{:S(2)}) async-start(bf16[64,168,128]{2,1,0:T(8,128)(2,1)} %get-tuple-element.23), calls=%async_computation | async-start | bytes 5505024 | tf_op jit(solution)/shard_map/all_to_all | solution.py:459
  95.5 129.4 %all-to-all-start.1 = ((bf16[64,112,384]{2,1,0:T(8,128)(2,1)}), bf16[64,112,384]{2,1,0:T(8,128)(2,1)}, u32[]{:S(2)}, u32[]{:S(2)}) async-start(bf16[64,112,384]{2,1,0:T(8,128)(2,1)} %get-tuple-element.30), calls=%async_computation.1 | async-start | bytes 11010048 | tf_op jit(solution)/shard_map/all_to_all | solution.py:459
  100.8 62.4 %collective-permute-start.2 = (bf16[64,168,128]{2,1,0:T(8,128)(2,1)S(1)}, bf16[64,168,128]{2,1,0:T(8,128)(2,1)S(1)}, u32[]{:S(2)}, u32[]{:S(2)}) collective-permute-start(bf16[64,168,128]{2,1,0:T(8,128)(2,1)S(1)} %all-to-all-done.held), channel_id=1, source_target_pairs={{0,2},{1,3},{2,0},{3,1},{4,6},{5,7},{6,4},{7,5},{8,10},{9,11},{10,... | collective-permute-start | bytes 8257544 | tf_op jit(solution)/shard_map/ppermute | solution.py:456
  224.8 62.5 %all-to-all-start.2 = ((bf16[64,48,384]{2,1,0:T(8,128)(2,1)}), bf16[64,48,384]{2,1,0:T(8,128)(2,1)}, u32[]{:S(2)}, u32[]{:S(2)}) async-start(bf16[64,48,384]{2,1,0:T(8,128)(2,1)} %far.1), calls=%async_computation.2 | async-start | bytes 4718592 | tf_op jit(solution)/shard_map/all_to_all | solution.py:459
  230.8 7.2 %copy-start.4 = (s32[96,2]{0,1:T(2,128)S(1)}, s32[96,2]{0,1:T(2,128)}, u32[]{:S(2)}) copy-start(s32[96,2]{0,1:T(2,128)} %param.9) | copy-start | bytes 2308
  230.8 8.7 %copy-start.3 = (f32[24,40]{1,0:T(8,128)S(1)}, f32[24,40]{1,0:T(8,128)}, u32[]{:S(2)}) copy-start(f32[24,40]{1,0:T(8,128)} %param.12) | copy-start | bytes 11524
  230.8 9.1 %copy-start.5 = (s32[192]{0:T(256)S(1)}, s32[192]{0:T(256)}, u32[]{:S(2)}) copy-start(s32[192]{0:T(256)} %get-tuple-element.22) | copy-start | bytes 2308
  230.8 9.3 %copy-start.2 = (bf16[24,1600]{1,0:T(8,128)(2,1)S(1)}, bf16[24,1600]{1,0:T(8,128)(2,1)}, u32[]{:S(2)}) copy-start(bf16[24,1600]{1,0:T(8,128)(2,1)} %param.11) | copy-start | bytes 230404
  235.3 52.1 %collective-permute-start.4 = (bf16[64,40,384]{2,1,0:T(8,128)(2,1)}, bf16[64,40,384]{2,1,0:T(8,128)(2,1)S(1)}, u32[]{:S(2)}, u32[]{:S(2)}) collective-permute-start(bf16[64,40,384]{2,1,0:T(8,128)(2,1)} %get-tuple-element.39), channel_id=1, source_target_pairs={{0,1},{1,2},{2,3},{3,0},{4,5},{5,6},{6,7},{7,4},{8,9},{9,10},{10,1... | collective-permute-start | bytes 5898248 | tf_op jit(solution)/shard_map/ppermute | solution.py:456
  235.9 51.5 %collective-permute-start.3 = (bf16[64,40,384]{2,1,0:T(8,128)(2,1)}, bf16[64,40,384]{2,1,0:T(8,128)(2,1)}, u32[]{:S(2)}, u32[]{:S(2)}) collective-permute-start(bf16[64,40,384]{2,1,0:T(8,128)(2,1)} %get-tuple-element.40), channel_id=1, source_target_pairs={{0,3},{1,0},{2,1},{3,2},{4,7},{5,4},{6,5},{7,6},{8,11},{9,8},{10,9... | collective-permute-start | bytes 5898248 | tf_op jit(solution)/shard_map/ppermute | solution.py:456
  287.4 16.3 %copy-start.1 = (f32[24,1600]{1,0:T(8,128)S(1)}, f32[24,1600]{1,0:T(8,128)}, u32[]{:S(2)}) copy-start(f32[24,1600]{1,0:T(8,128)} %convert_multiply_fusion) | copy-start | bytes 460804
  292.6 7.1 %collective-permute-start.5 = (f32[24,1600]{1,0:T(8,128)S(1)}, f32[24,1600]{1,0:T(8,128)S(1)}, u32[]{:S(2)}, u32[]{:S(2)}) collective-permute-start(f32[24,1600]{1,0:T(8,128)S(1)} %get-tuple-element.35), channel_id=1, source_target_pairs={{0,2},{1,3},{2,0},{3,1},{4,6},{5,7},{6,4},{7,5},{8,10},{9,11},{10,... | collective-permute-start | bytes 460808 | tf_op jit(solution)/shard_map/ppermute | solution.py:456
  294.5 9.1 %collective-permute-start.6 = (f32[24,1600]{1,0:T(8,128)S(1)}, f32[24,1600]{1,0:T(8,128)S(1)}, u32[]{:S(2)}, u32[]{:S(2)}) collective-permute-start(f32[24,1600]{1,0:T(8,128)S(1)} %get-tuple-element.36), channel_id=1, source_target_pairs={{0,1},{1,2},{2,3},{3,0},{4,5},{5,6},{6,7},{7,4},{8,9},{9,10},{10,1... | collective-permute-start | bytes 460808 | tf_op jit(solution)/shard_map/ppermute | solution.py:456
  295.2 8.5 %collective-permute-start.7 = (f32[24,1600]{1,0:T(8,128)S(1)}, f32[24,1600]{1,0:T(8,128)S(1)}, u32[]{:S(2)}, u32[]{:S(2)}) collective-permute-start(f32[24,1600]{1,0:T(8,128)S(1)} %get-tuple-element.37), channel_id=1, source_target_pairs={{0,3},{1,0},{2,1},{3,2},{4,7},{5,4},{6,5},{7,6},{8,11},{9,8},{10,9... | collective-permute-start | bytes 460808 | tf_op jit(solution)/shard_map/ppermute | solution.py:456

commit v8 on v7

--- a/solution.py
+++ b/solution.py
@@ -429,7 +429,7 @@
             pltpu.VMEM((pairs * npno, LANES), jnp.float32),
             pltpu.SemaphoreType.DMA((4,)),
         ],
-        compiler_params=pltpu.CompilerParams(vmem_limit_bytes=48 * 2**20),
+        compiler_params=pltpu.CompilerParams(vmem_limit_bytes=46 * 2**20),
         name="exchange",
     )(place, first, above, last, below)
 

time: 305 us -> 305 us (level)
  no operation moved by 1% of the time
where the time goes in v8:
time: 305 us
  waiting for transfers between devices  231 us (76%)
  starting transfers between devices  37.3 us (12%)
  Pallas kernels  26.2 us (9%)
  local copies, waits for them, and re-layouts  7.92 us (3%)
    ppermute x8, waiting for transfers between devices, shifted(): lax.ppermute(value, 'rep', [(i, (i + by) % n_rep) for i in range(n_rep)])  117 us
    all_to_all x3, waiting for transfers between devices, there(): return lax.all_to_all(value, 'orb', split_axis=0, concat_axis=0, tiled=True)  115 us
    all_to_all x3, starting transfers between devices, there(): return lax.all_to_all(value, 'orb', split_axis=0, concat_axis=0, tiled=True)  24.8 us
    ppermute x8, starting transfers between devices, shifted(): lax.ppermute(value, 'rep', [(i, (i + by) % n_rep) for i in range(n_rep)])  12.5 us
    pallas_call x1, Pallas kernels, near_halves(): pl.pallas_call(functools.partial(near_kernel, npno), out_shape=[jax.Shape...  8.06 us
    pallas_call x1, Pallas kernels, far_halves(): pl.pallas_call(functools.partial(far_kernel, npno), out_shape=jax.ShapeDt...  7.61 us
  transfers between devices with their start and end apart: 11, of which 8 were waited for; matrix products, arithmetic and copies ran while one was open for 3% of the time, Pallas kernels for 4%

profile of v8, /device:TPU:1, one launch (start us, length us, event | category | flops | bytes accessed | tf_op | source)
XLA Modules:
  0.0 304.6 jit_solution(11936557375170247565)
XLA Ops:
  0.0 2.1 collective-permute-start.1
  2.1 1.5 collective-permute-start
  3.7 5.3 %route.1 = (bf16[64,168,128]{2,1,0:T(8,128)(2,1)}, s32[192]{0:T(256)}) custom-call(s32[2,96]{1,0:T(2,128)} %bitcast.9, s32[512]{0:T(512)} %place.1, s32[1]{0:T(128)} %bitcast.1.plane, s32[1]{0:T(128)} %bitcast.2.source, bf16[192,40,512]{2,1,0:T(8,128)(2,1)} %bitcast.8), custom_call_target="tpu_custom_call" | custom-call | tf_op jit(solution)/shard_map/route/pallas_call | solution.py:107
  9.0 12.7 %all-to-all-start = ((bf16[64,168,128]{2,1,0:T(8,128)(2,1)}), bf16[64,168,128]{2,1,0:T(8,128)(2,1)S(1)}, u32[]{:S(2)}, u32[]{:S(2)}) async-start(bf16[64,168,128]{2,1,0:T(8,128)(2,1)} %get-tuple-element.23), calls=%async_computation | async-start | bytes 5505024 | tf_op jit(solution)/shard_map/all_to_all | solution.py:459
  21.7 47.9 %collective-permute-done.1.below_in = bf16[8,384,512]{2,1,0:T(8,128)(2,1)} collective-permute-done((bf16[8,384,512]{2,1,0:T(8,128)(2,1)}, bf16[8,384,512]{2,1,0:T(8,128)(2,1)}, u32[]{:S(2)}, u32[]{:S(2)}) %collective-permute-start.1) | collective-permute-done | bytes 3145760 | tf_op jit(solution)/shard_map/ppermute | solution.py:456
  69.7 1.3 collective-permute-done.above_in
  70.9 15.9 %all-to-all-done.held = bf16[64,168,128]{2,1,0:T(8,128)(2,1)S(1)} async-done(((bf16[64,168,128]{2,1,0:T(8,128)(2,1)}), bf16[64,168,128]{2,1,0:T(8,128)(2,1)S(1)}, u32[]{:S(2)}, u32[]{:S(2)}) %all-to-all-start) | async-done | bytes 2752544 | tf_op jit(solution)/shard_map/all_to_all | solution.py:459
  86.8 8.1 %near.1 = (bf16[64,112,384]{2,1,0:T(8,128)(2,1)}, bf16[64,8,384]{2,1,0:T(8,128)(2,1)S(1)}) custom-call(bf16[64,168,128]{2,1,0:T(8,128)(2,1)S(1)} %all-to-all-done.held, bf16[8,384,512]{2,1,0:T(8,128)(2,1)} %ints.1, bf16[8,384,512]{2,1,0:T(8,128)(2,1)} %get-tuple-element.27.above, bf16[8,384,512]{2,1,0:T(8,128)(2,1)} %get-tuple-element.28.below), custom_call_target="tpu_custom_call" | custom-call | flops 3019898880 | bytes 17956864 | tf_op jit(solution)/shard_map/near/pallas_call | solution.py:252
  94.9 6.1 %all-to-all-start.1 = ((bf16[64,112,384]{2,1,0:T(8,128)(2,1)}), bf16[64,112,384]{2,1,0:T(8,128)(2,1)}, u32[]{:S(2)}, u32[]{:S(2)}) async-start(bf16[64,112,384]{2,1,0:T(8,128)(2,1)} %get-tuple-element.30), calls=%async_computation.1 | async-start | bytes 11010048 | tf_op jit(solution)/shard_map/all_to_all | solution.py:459
  101.0 1.7 collective-permute-start.2
  102.7 60.7 %collective-permute-done.2.held = bf16[64,168,128]{2,1,0:T(8,128)(2,1)S(1)} collective-permute-done((bf16[64,168,128]{2,1,0:T(8,128)(2,1)S(1)}, bf16[64,168,128]{2,1,0:T(8,128)(2,1)S(1)}, u32[]{:S(2)}, u32[]{:S(2)}) %collective-permute-start.2) | collective-permute-done | bytes 2752544 | tf_op jit(solution)/shard_map/ppermute | solution.py:456
  163.4 7.6 %far.1 = bf16[64,48,384]{2,1,0:T(8,128)(2,1)} custom-call(bf16[64,168,128]{2,1,0:T(8,128)(2,1)S(1)} %collective-permute-done.2.held, bf16[8,384,512]{2,1,0:T(8,128)(2,1)} %ints.1, bf16[64,8,384]{2,1,0:T(8,128)(2,1)S(1)} %get-tuple-element.29.rest), custom_call_target="tpu_custom_call" | custom-call | flops 8053063680 | bytes 7733248 | tf_op jit(solution)/shard_map/far/pallas_call | solution.py:326
  171.0 54.0 %all-to-all-done.1 = bf16[64,112,384]{2,1,0:T(8,128)(2,1)} async-done(((bf16[64,112,384]{2,1,0:T(8,128)(2,1)}), bf16[64,112,384]{2,1,0:T(8,128)(2,1)}, u32[]{:S(2)}, u32[]{:S(2)}) %all-to-all-start.1) | async-done | bytes 5505056 | tf_op jit(solution)/shard_map/all_to_all | solution.py:459
  225.0 6.0 %all-to-all-start.2 = ((bf16[64,48,384]{2,1,0:T(8,128)(2,1)}), bf16[64,48,384]{2,1,0:T(8,128)(2,1)}, u32[]{:S(2)}, u32[]{:S(2)}) async-start(bf16[64,48,384]{2,1,0:T(8,128)(2,1)} %far.1), calls=%async_computation.2 | async-start | bytes 4718592 | tf_op jit(solution)/shard_map/all_to_all | solution.py:459
  231.0 4.4 %fusion.5 = (bf16[64,40,384]{2,1,0:T(8,128)(2,1)}, bf16[64,40,384]{2,1,0:T(8,128)(2,1)}) fusion(bf16[64,112,384]{2,1,0:T(8,128)(2,1)} %all-to-all-done.1), kind=kLoop, calls=%fused_computation.25 | loop fusion | bytes 7864320 | tf_op jit(solution)/shard_map/slice | solution.py:478
  235.5 2.7 collective-permute-start.3
  238.2 0.7 gather_fusion.1
  239.0 0.7 gather_fusion
  239.7 0.2 broadcast_add_fusion
  239.9 0.2 add.79
  240.1 0.1 reshape.29
  240.2 0.1 reshape.30.place
  240.3 0.7 convert_multiply_fusion
  241.0 1.6 slice.15.first
  242.6 44.9 %all-to-all-done.2.last = bf16[64,48,384]{2,1,0:T(8,128)(2,1)} async-done(((bf16[64,48,384]{2,1,0:T(8,128)(2,1)}), bf16[64,48,384]{2,1,0:T(8,128)(2,1)}, u32[]{:S(2)}, u32[]{:S(2)}) %all-to-all-start.2) | async-done | bytes 2359328 | tf_op jit(solution)/shard_map/all_to_all | solution.py:459
  287.6 5.2 %exchange.1 = (f32[24,1600]{1,0:T(8,128)S(1)}, f32[24,1600]{1,0:T(8,128)S(1)}, f32[24,1600]{1,0:T(8,128)S(1)}, f32[24,1600]{1,0:T(8,128)S(1)}) custom-call(s32[192]{0:T(256)S(1)} %reshape.30.place, bf16[64,32,384]{2,1,0:T(8,128)(2,1)S(1)} %slice.15.first, bf16[64,40,384]{2,1,0:T(8,128)(2,1)} %collective-permute-done.3.above, ...), custom_call_target="tpu_custom_call" | custom-call | tf_op jit(solution)/shard_map/exchange/pallas_call | solution.py:421
  292.8 1.7 collective-permute-start.5
  294.5 0.4 collective-permute-start.6
  294.9 2.3 collective-permute-start.7
  297.2 2.7 collective-permute-done.5
  299.9 3.9 %collective-permute-done.6 = f32[24,1600]{1,0:T(8,128)S(1)} collective-permute-done((f32[24,1600]{1,0:T(8,128)S(1)}, f32[24,1600]{1,0:T(8,128)S(1)}, u32[]{:S(2)}, u32[]{:S(2)}) %collective-permute-start.6) | collective-permute-done | bytes 153632 | tf_op jit(solution)/shard_map/ppermute | solution.py:456
  303.9 0.7 add_add_fusion
  (24 shorter events, 0.2 us)
Async XLA Ops:
  0.0 238.2 %copy-start = (f32[512]{0:T(512)S(1)}, f32[512]{0:T(512)}, u32[]{:S(2)}) copy-start(f32[512]{0:T(512)} %param.13) | copy-start | bytes 6148
  0.0 69.7 %collective-permute-start.1 = (bf16[8,384,512]{2,1,0:T(8,128)(2,1)}, bf16[8,384,512]{2,1,0:T(8,128)(2,1)}, u32[]{:S(2)}, u32[]{:S(2)}) collective-permute-start(bf16[8,384,512]{2,1,0:T(8,128)(2,1)} %ints.1), channel_id=1, source_target_pairs={{0,1},{1,2},{2,3},{3,0},{4,5},{5,6},{6,7},{7,4},{8,9},{9,10},{10,1... | collective-permute-start | bytes 9437192 | tf_op jit(solution)/shard_map/ppermute | solution.py:456
  2.1 68.8 %collective-permute-start = (bf16[8,384,512]{2,1,0:T(8,128)(2,1)}, bf16[8,384,512]{2,1,0:T(8,128)(2,1)}, u32[]{:S(2)}, u32[]{:S(2)}) collective-permute-start(bf16[8,384,512]{2,1,0:T(8,128)(2,1)} %ints.1), channel_id=1, source_target_pairs={{0,3},{1,0},{2,1},{3,2},{4,7},{5,4},{6,5},{7,6},{8,11},{9,8},{10,9... | collective-permute-start | bytes 9437192 | tf_op jit(solution)/shard_map/ppermute | solution.py:456
  9.0 77.8 %all-to-all-start = ((bf16[64,168,128]{2,1,0:T(8,128)(2,1)}), bf16[64,168,128]{2,1,0:T(8,128)(2,1)S(1)}, u32[]{:S(2)}, u32[]{:S(2)}) async-start(bf16[64,168,128]{2,1,0:T(8,128)(2,1)} %get-tuple-element.23), calls=%async_computation | async-start | bytes 5505024 | tf_op jit(solution)/shard_map/all_to_all | solution.py:459
  94.9 130.1 %all-to-all-start.1 = ((bf16[64,112,384]{2,1,0:T(8,128)(2,1)}), bf16[64,112,384]{2,1,0:T(8,128)(2,1)}, u32[]{:S(2)}, u32[]{:S(2)}) async-start(bf16[64,112,384]{2,1,0:T(8,128)(2,1)} %get-tuple-element.30), calls=%async_computation.1 | async-start | bytes 11010048 | tf_op jit(solution)/shard_map/all_to_all | solution.py:459
  101.0 62.4 %collective-permute-start.2 = (bf16[64,168,128]{2,1,0:T(8,128)(2,1)S(1)}, bf16[64,168,128]{2,1,0:T(8,128)(2,1)S(1)}, u32[]{:S(2)}, u32[]{:S(2)}) collective-permute-start(bf16[64,168,128]{2,1,0:T(8,128)(2,1)S(1)} %all-to-all-done.held), channel_id=1, source_target_pairs={{0,2},{1,3},{2,0},{3,1},{4,6},{5,7},{6,4},{7,5},{8,10},{9,11},{10,... | collective-permute-start | bytes 8257544 | tf_op jit(solution)/shard_map/ppermute | solution.py:456
  225.0 62.5 %all-to-all-start.2 = ((bf16[64,48,384]{2,1,0:T(8,128)(2,1)}), bf16[64,48,384]{2,1,0:T(8,128)(2,1)}, u32[]{:S(2)}, u32[]{:S(2)}) async-start(bf16[64,48,384]{2,1,0:T(8,128)(2,1)} %far.1), calls=%async_computation.2 | async-start | bytes 4718592 | tf_op jit(solution)/shard_map/all_to_all | solution.py:459
  231.0 7.2 %copy-start.4 = (s32[96,2]{0,1:T(2,128)S(1)}, s32[96,2]{0,1:T(2,128)}, u32[]{:S(2)}) copy-start(s32[96,2]{0,1:T(2,128)} %param.9) | copy-start | bytes 2308
  231.0 8.7 %copy-start.3 = (f32[24,40]{1,0:T(8,128)S(1)}, f32[24,40]{1,0:T(8,128)}, u32[]{:S(2)}) copy-start(f32[24,40]{1,0:T(8,128)} %param.12) | copy-start | bytes 11524
  231.0 9.1 %copy-start.5 = (s32[192]{0:T(256)S(1)}, s32[192]{0:T(256)}, u32[]{:S(2)}) copy-start(s32[192]{0:T(256)} %get-tuple-element.22) | copy-start | bytes 2308
  231.0 9.3 %copy-start.2 = (bf16[24,1600]{1,0:T(8,128)(2,1)S(1)}, bf16[24,1600]{1,0:T(8,128)(2,1)}, u32[]{:S(2)}) copy-start(bf16[24,1600]{1,0:T(8,128)(2,1)} %param.11) | copy-start | bytes 230404
  235.5 52.1 %collective-permute-start.4 = (bf16[64,40,384]{2,1,0:T(8,128)(2,1)}, bf16[64,40,384]{2,1,0:T(8,128)(2,1)S(1)}, u32[]{:S(2)}, u32[]{:S(2)}) collective-permute-start(bf16[64,40,384]{2,1,0:T(8,128)(2,1)} %get-tuple-element.39), channel_id=1, source_target_pairs={{0,1},{1,2},{2,3},{3,0},{4,5},{5,6},{6,7},{7,4},{8,9},{9,10},{10,1... | collective-permute-start | bytes 5898248 | tf_op jit(solution)/shard_map/ppermute | solution.py:456
  235.5 52.1 %collective-permute-start.3 = (bf16[64,40,384]{2,1,0:T(8,128)(2,1)}, bf16[64,40,384]{2,1,0:T(8,128)(2,1)}, u32[]{:S(2)}, u32[]{:S(2)}) collective-permute-start(bf16[64,40,384]{2,1,0:T(8,128)(2,1)} %get-tuple-element.40), channel_id=1, source_target_pairs={{0,3},{1,0},{2,1},{3,2},{4,7},{5,4},{6,5},{7,6},{8,11},{9,8},{10,9... | collective-permute-start | bytes 5898248 | tf_op jit(solution)/shard_map/ppermute | solution.py:456
  287.6 16.3 %copy-start.1 = (f32[24,1600]{1,0:T(8,128)S(1)}, f32[24,1600]{1,0:T(8,128)}, u32[]{:S(2)}) copy-start(f32[24,1600]{1,0:T(8,128)} %convert_multiply_fusion) | copy-start | bytes 460804
  292.8 7.2 %collective-permute-start.5 = (f32[24,1600]{1,0:T(8,128)S(1)}, f32[24,1600]{1,0:T(8,128)S(1)}, u32[]{:S(2)}, u32[]{:S(2)}) collective-permute-start(f32[24,1600]{1,0:T(8,128)S(1)} %get-tuple-element.35), channel_id=1, source_target_pairs={{0,2},{1,3},{2,0},{3,1},{4,6},{5,7},{6,4},{7,5},{8,10},{9,11},{10,... | collective-permute-start | bytes 460808 | tf_op jit(solution)/shard_map/ppermute | solution.py:456
  294.5 9.3 %collective-permute-start.6 = (f32[24,1600]{1,0:T(8,128)S(1)}, f32[24,1600]{1,0:T(8,128)S(1)}, u32[]{:S(2)}, u32[]{:S(2)}) collective-permute-start(f32[24,1600]{1,0:T(8,128)S(1)} %get-tuple-element.36), channel_id=1, source_target_pairs={{0,1},{1,2},{2,3},{3,0},{4,5},{5,6},{6,7},{7,4},{8,9},{9,10},{10,1... | collective-permute-start | bytes 460808 | tf_op jit(solution)/shard_map/ppermute | solution.py:456
  294.9 8.9 %collective-permute-start.7 = (f32[24,1600]{1,0:T(8,128)S(1)}, f32[24,1600]{1,0:T(8,128)S(1)}, u32[]{:S(2)}, u32[]{:S(2)}) collective-permute-start(f32[24,1600]{1,0:T(8,128)S(1)} %get-tuple-element.37), channel_id=1, source_target_pairs={{0,3},{1,0},{2,1},{3,2},{4,7},{5,4},{6,5},{7,6},{8,11},{9,8},{10,9... | collective-permute-start | bytes 460808 | tf_op jit(solution)/shard_map/ppermute | solution.py:456

commit v9 on v8

--- a/solution.py
+++ b/solution.py
@@ -366,22 +366,20 @@
     )(above, below)
 
 
-def exchange_kernel(place, first, above, last, below, *refs):
-    planes = len(refs) - 4
-    outs, (halves, late, product, sems) = refs[:planes], refs[planes:]
-    owners, main, _ = first.shape
-    npno = halves.shape[1]
+def exchange_kernel(place, near, above, late, below, *refs):
+    planes = len(refs) - 3
+    outs, (halves, product, sems) = refs[:planes], refs[planes:]
+    owners, npno, _ = above.shape
+    main = npno // 16 * 16
     copies = [
-        pltpu.make_async_copy(last, late, sems.at[0]),
+        pltpu.make_async_copy(above, halves.at[pl.ds(owners, owners)], sems.at[0]),
+        pltpu.make_async_copy(below, halves.at[pl.ds(3 * owners, owners)], sems.at[1]),
         pltpu.make_async_copy(
-            first, halves.at[pl.ds(0, owners), pl.ds(0, main)], sems.at[1]
+            near.at[:, pl.ds(0, main)], halves.at[pl.ds(0, owners), pl.ds(0, main)], sems.at[2]
         ),
-        pltpu.make_async_copy(above, halves.at[pl.ds(owners, owners)], sems.at[2]),
-        pltpu.make_async_copy(below, halves.at[pl.ds(3 * owners, owners)], sems.at[3]),
     ]
     for copy in copies:
         copy.start()
-    copies[0].wait()
 
     def join(e, _):
         halves[e, main:] = late[e, npno:]
@@ -389,7 +387,7 @@
         return 0
 
     lax.fori_loop(0, owners, join, 0, unroll=4)
-    for copy in copies[1:]:
+    for copy in copies:
         copy.wait()
     each = outs[0].shape[0]
 
@@ -412,7 +410,7 @@
             outs[g][:, x * npno : (x + 1) * npno] = rows[:, :npno]
 
 
-def exchange_of(place, planes, first, above, last, below):
+def exchange_of(place, planes, near, above, last, below):
     owners, npno, naux = above.shape
     pairs = place.shape[0] // 2
     hbm = pl.BlockSpec(memory_space=pltpu.HBM)
@@ -421,17 +419,16 @@
     return pl.pallas_call(
         exchange_kernel,
         out_shape=[out] * planes,
-        in_specs=[pl.BlockSpec(memory_space=pltpu.SMEM)] + [hbm] * 4,
+        in_specs=[pl.BlockSpec(memory_space=pltpu.SMEM)] + [hbm, hbm, vmem, hbm],
         out_specs=[vmem] * planes,
         scratch_shapes=[
             pltpu.VMEM((CAP * owners, npno, naux), jnp.bfloat16),
-            pltpu.VMEM(last.shape, jnp.bfloat16),
             pltpu.VMEM((pairs * npno, LANES), jnp.float32),
-            pltpu.SemaphoreType.DMA((4,)),
+            pltpu.SemaphoreType.DMA((3,)),
         ],
         compiler_params=pltpu.CompilerParams(vmem_limit_bytes=46 * 2**20),
         name="exchange",
-    )(place, first, above, last, below)
+    )(place, near, above, last, below)
 
 
 def body(
@@ -473,7 +470,6 @@
     last = there(last)
 
     main = npno // 16 * 16
-    first = near[:, :main]
     above = shifted(near[:, main + npno :], n_rep - 1)
     below = shifted(near[:, main : main + npno], 1)
     place = (slot // n_orb - rep) % n_rep * n_orb + slot % n_orb
@@ -485,7 +481,7 @@
     local = gap.reshape(mine, npno * npno) * amplitudes.astype(jnp.float32)
     last, local = lax.optimization_barrier((last, local))
     place = jnp.roll(place.reshape(n_rep, 2 * mine), -rep, axis=0).reshape(-1)
-    products = exchange_of(place, n_rep, first, above, last, below)
+    products = exchange_of(place, n_rep, near, above, last, below)
     exchange = products[0]
     for by in (2, 1, n_rep - 1):
         exchange = exchange + shifted(products[by], by)

time: 305 us -> 305 us (level)
  transfers between devices with their start and end apart: 11 -> 11, of which waited for: 8 -> 8; matrix products, arithmetic and copies ran while one was open for 3% -> 2% of each run, Pallas kernels for 4% -> 4%
where the time goes in v9:
time: 305 us
  waiting for transfers between devices  234 us (77%)
  starting transfers between devices  37.6 us (12%)
  Pallas kernels  24.8 us (8%)
  local copies, waits for them, and re-layouts  7.77 us (3%)
    all_to_all x3, waiting for transfers between devices, there(): return lax.all_to_all(value, 'orb', split_axis=0, concat_axis=0, tiled=True)  117 us
    ppermute x8, waiting for transfers between devices, shifted(): lax.ppermute(value, 'rep', [(i, (i + by) % n_rep) for i in range(n_rep)])  116 us
    all_to_all x3, starting transfers between devices, there(): return lax.all_to_all(value, 'orb', split_axis=0, concat_axis=0, tiled=True)  24.8 us
    ppermute x8, starting transfers between devices, shifted(): lax.ppermute(value, 'rep', [(i, (i + by) % n_rep) for i in range(n_rep)])  12.8 us
    pallas_call x1, Pallas kernels, near_halves(): pl.pallas_call(functools.partial(near_kernel, npno), out_shape=[jax.Shape...  7.93 us
  transfers between devices with their start and end apart: 11, of which 8 were waited for; matrix products, arithmetic and copies ran while one was open for 2% of the time, Pallas kernels for 4%

profile of v9, /device:TPU:1, one launch (start us, length us, event | category | flops | bytes accessed | tf_op | source)
XLA Modules:
  0.0 304.9 jit_solution(7484718989395021181)
XLA Ops:
  0.0 2.1 collective-permute-start.1
  2.1 1.5 collective-permute-start
  3.7 5.4 %route.1 = (bf16[64,168,128]{2,1,0:T(8,128)(2,1)}, s32[192]{0:T(256)}) custom-call(s32[2,96]{1,0:T(2,128)} %bitcast.9, s32[512]{0:T(512)} %place.1, s32[1]{0:T(128)} %bitcast.1.plane, s32[1]{0:T(128)} %bitcast.2.source, bf16[192,40,512]{2,1,0:T(8,128)(2,1)} %bitcast.8), custom_call_target="tpu_custom_call" | custom-call | tf_op jit(solution)/shard_map/route/pallas_call | solution.py:107
  9.1 12.6 %all-to-all-start = ((bf16[64,168,128]{2,1,0:T(8,128)(2,1)}), bf16[64,168,128]{2,1,0:T(8,128)(2,1)S(1)}, u32[]{:S(2)}, u32[]{:S(2)}) async-start(bf16[64,168,128]{2,1,0:T(8,128)(2,1)} %get-tuple-element.23), calls=%async_computation | async-start | bytes 5505024 | tf_op jit(solution)/shard_map/all_to_all | solution.py:456
  21.7 47.9 %collective-permute-done.1.below_in = bf16[8,384,512]{2,1,0:T(8,128)(2,1)} collective-permute-done((bf16[8,384,512]{2,1,0:T(8,128)(2,1)}, bf16[8,384,512]{2,1,0:T(8,128)(2,1)}, u32[]{:S(2)}, u32[]{:S(2)}) %collective-permute-start.1) | collective-permute-done | bytes 3145760 | tf_op jit(solution)/shard_map/ppermute | solution.py:453
  69.7 1.3 collective-permute-done.above_in
  70.9 15.9 %all-to-all-done.held = bf16[64,168,128]{2,1,0:T(8,128)(2,1)S(1)} async-done(((bf16[64,168,128]{2,1,0:T(8,128)(2,1)}), bf16[64,168,128]{2,1,0:T(8,128)(2,1)S(1)}, u32[]{:S(2)}, u32[]{:S(2)}) %all-to-all-start) | async-done | bytes 2752544 | tf_op jit(solution)/shard_map/all_to_all | solution.py:456
  86.8 7.9 %near.1 = (bf16[64,112,384]{2,1,0:T(8,128)(2,1)}, bf16[64,8,384]{2,1,0:T(8,128)(2,1)S(1)}) custom-call(bf16[64,168,128]{2,1,0:T(8,128)(2,1)S(1)} %all-to-all-done.held, bf16[8,384,512]{2,1,0:T(8,128)(2,1)} %ints.1, bf16[8,384,512]{2,1,0:T(8,128)(2,1)} %get-tuple-element.27.above, bf16[8,384,512]{2,1,0:T(8,128)(2,1)} %get-tuple-element.28.below), custom_call_target="tpu_custom_call" | custom-call | flops 3019898880 | bytes 17956864 | tf_op jit(solution)/shard_map/near/pallas_call | solution.py:252
  94.7 6.4 %all-to-all-start.1 = ((bf16[64,112,384]{2,1,0:T(8,128)(2,1)}), bf16[64,112,384]{2,1,0:T(8,128)(2,1)}, u32[]{:S(2)}, u32[]{:S(2)}) async-start(bf16[64,112,384]{2,1,0:T(8,128)(2,1)} %get-tuple-element.30), calls=%async_computation.1 | async-start | bytes 11010048 | tf_op jit(solution)/shard_map/all_to_all | solution.py:456
  101.2 1.9 collective-permute-start.2
  103.1 60.5 %collective-permute-done.2.held = bf16[64,168,128]{2,1,0:T(8,128)(2,1)S(1)} collective-permute-done((bf16[64,168,128]{2,1,0:T(8,128)(2,1)S(1)}, bf16[64,168,128]{2,1,0:T(8,128)(2,1)S(1)}, u32[]{:S(2)}, u32[]{:S(2)}) %collective-permute-start.2) | collective-permute-done | bytes 2752544 | tf_op jit(solution)/shard_map/ppermute | solution.py:453
  163.6 5.9 %far.1 = bf16[64,48,384]{2,1,0:T(8,128)(2,1)S(1)} custom-call(bf16[64,168,128]{2,1,0:T(8,128)(2,1)S(1)} %collective-permute-done.2.held, bf16[8,384,512]{2,1,0:T(8,128)(2,1)} %ints.1, bf16[64,8,384]{2,1,0:T(8,128)(2,1)S(1)} %get-tuple-element.29.rest), custom_call_target="tpu_custom_call" | custom-call | flops 8053063680 | bytes 7733248 | tf_op jit(solution)/shard_map/far/pallas_call | solution.py:326
  169.5 1.4 copy-done.1
  170.9 54.3 %all-to-all-done.1.near = bf16[64,112,384]{2,1,0:T(8,128)(2,1)} async-done(((bf16[64,112,384]{2,1,0:T(8,128)(2,1)}), bf16[64,112,384]{2,1,0:T(8,128)(2,1)}, u32[]{:S(2)}, u32[]{:S(2)}) %all-to-all-start.1) | async-done | bytes 5505056 | tf_op jit(solution)/shard_map/all_to_all | solution.py:456
  225.2 5.8 %all-to-all-start.2 = ((bf16[64,48,384]{2,1,0:T(8,128)(2,1)}), bf16[64,48,384]{2,1,0:T(8,128)(2,1)S(1)}, u32[]{:S(2)}, u32[]{:S(2)}) async-start(bf16[64,48,384]{2,1,0:T(8,128)(2,1)} %copy-done.1), calls=%async_computation.2 | async-start | bytes 4718592 | tf_op jit(solution)/shard_map/all_to_all | solution.py:456
  231.0 4.5 %fusion.5 = (bf16[64,40,384]{2,1,0:T(8,128)(2,1)}, bf16[64,40,384]{2,1,0:T(8,128)(2,1)}) fusion(bf16[64,112,384]{2,1,0:T(8,128)(2,1)} %all-to-all-done.1.near), kind=kLoop, calls=%fused_computation.25 | loop fusion | bytes 7864320 | tf_op jit(solution)/shard_map/slice | solution.py:474
  235.5 2.7 collective-permute-start.3
  238.3 0.7 gather_fusion.1
  239.0 0.7 gather_fusion
  239.7 0.2 broadcast_add_fusion
  239.9 0.2 add.79
  240.1 0.1 reshape.29
  240.2 0.1 reshape.30.place
  240.3 0.1 convert_multiply_fusion
  240.4 47.2 %all-to-all-done.2.late = bf16[64,48,384]{2,1,0:T(8,128)(2,1)S(1)} async-done(((bf16[64,48,384]{2,1,0:T(8,128)(2,1)}), bf16[64,48,384]{2,1,0:T(8,128)(2,1)S(1)}, u32[]{:S(2)}, u32[]{:S(2)}) %all-to-all-start.2) | async-done | bytes 2359328 | tf_op jit(solution)/shard_map/all_to_all | solution.py:456
  287.6 5.5 %exchange.1 = (f32[24,1600]{1,0:T(8,128)S(1)}, f32[24,1600]{1,0:T(8,128)S(1)}, f32[24,1600]{1,0:T(8,128)S(1)}, f32[24,1600]{1,0:T(8,128)S(1)}) custom-call(s32[192]{0:T(256)S(1)} %reshape.30.place, bf16[64,112,384]{2,1,0:T(8,128)(2,1)} %all-to-all-done.1.near, bf16[64,40,384]{2,1,0:T(8,128)(2,1)} %collective-permute-done.3.above, ...), custom_call_target="tpu_custom_call" | custom-call | tf_op jit(solution)/shard_map/exchange/pallas_call | solution.py:419
  293.1 1.9 collective-permute-start.5
  295.0 0.2 collective-permute-start.6
  295.2 2.5 collective-permute-start.7
  297.7 2.6 collective-permute-done.5
  300.3 3.9 %collective-permute-done.6 = f32[24,1600]{1,0:T(8,128)S(1)} collective-permute-done((f32[24,1600]{1,0:T(8,128)S(1)}, f32[24,1600]{1,0:T(8,128)S(1)}, u32[]{:S(2)}, u32[]{:S(2)}) %collective-permute-start.6) | collective-permute-done | bytes 153632 | tf_op jit(solution)/shard_map/ppermute | solution.py:453
  304.2 0.7 add_add_fusion
  (23 shorter events, 0.2 us)
Async XLA Ops:
  0.0 238.3 %copy-start = (f32[512]{0:T(512)S(1)}, f32[512]{0:T(512)}, u32[]{:S(2)}) copy-start(f32[512]{0:T(512)} %param.13) | copy-start | bytes 6148
  0.0 69.7 %collective-permute-start.1 = (bf16[8,384,512]{2,1,0:T(8,128)(2,1)}, bf16[8,384,512]{2,1,0:T(8,128)(2,1)}, u32[]{:S(2)}, u32[]{:S(2)}) collective-permute-start(bf16[8,384,512]{2,1,0:T(8,128)(2,1)} %ints.1), channel_id=1, source_target_pairs={{0,1},{1,2},{2,3},{3,0},{4,5},{5,6},{6,7},{7,4},{8,9},{9,10},{10,1... | collective-permute-start | bytes 9437192 | tf_op jit(solution)/shard_map/ppermute | solution.py:453
  2.1 68.8 %collective-permute-start = (bf16[8,384,512]{2,1,0:T(8,128)(2,1)}, bf16[8,384,512]{2,1,0:T(8,128)(2,1)}, u32[]{:S(2)}, u32[]{:S(2)}) collective-permute-start(bf16[8,384,512]{2,1,0:T(8,128)(2,1)} %ints.1), channel_id=1, source_target_pairs={{0,3},{1,0},{2,1},{3,2},{4,7},{5,4},{6,5},{7,6},{8,11},{9,8},{10,9... | collective-permute-start | bytes 9437192 | tf_op jit(solution)/shard_map/ppermute | solution.py:453
  9.1 77.7 %all-to-all-start = ((bf16[64,168,128]{2,1,0:T(8,128)(2,1)}), bf16[64,168,128]{2,1,0:T(8,128)(2,1)S(1)}, u32[]{:S(2)}, u32[]{:S(2)}) async-start(bf16[64,168,128]{2,1,0:T(8,128)(2,1)} %get-tuple-element.23), calls=%async_computation | async-start | bytes 5505024 | tf_op jit(solution)/shard_map/all_to_all | solution.py:456
  94.7 130.4 %all-to-all-start.1 = ((bf16[64,112,384]{2,1,0:T(8,128)(2,1)}), bf16[64,112,384]{2,1,0:T(8,128)(2,1)}, u32[]{:S(2)}, u32[]{:S(2)}) async-start(bf16[64,112,384]{2,1,0:T(8,128)(2,1)} %get-tuple-element.30), calls=%async_computation.1 | async-start | bytes 11010048 | tf_op jit(solution)/shard_map/all_to_all | solution.py:456
  101.2 62.4 %collective-permute-start.2 = (bf16[64,168,128]{2,1,0:T(8,128)(2,1)S(1)}, bf16[64,168,128]{2,1,0:T(8,128)(2,1)S(1)}, u32[]{:S(2)}, u32[]{:S(2)}) collective-permute-start(bf16[64,168,128]{2,1,0:T(8,128)(2,1)S(1)} %all-to-all-done.held), channel_id=1, source_target_pairs={{0,2},{1,3},{2,0},{3,1},{4,6},{5,7},{6,4},{7,5},{8,10},{9,11},{10,... | collective-permute-start | bytes 8257544 | tf_op jit(solution)/shard_map/ppermute | solution.py:453
  169.5 1.4 copy-start.1
  225.2 62.4 %all-to-all-start.2 = ((bf16[64,48,384]{2,1,0:T(8,128)(2,1)}), bf16[64,48,384]{2,1,0:T(8,128)(2,1)S(1)}, u32[]{:S(2)}, u32[]{:S(2)}) async-start(bf16[64,48,384]{2,1,0:T(8,128)(2,1)} %copy-done.1), calls=%async_computation.2 | async-start | bytes 4718592 | tf_op jit(solution)/shard_map/all_to_all | solution.py:456
  231.0 7.2 %copy-start.4 = (s32[96,2]{0,1:T(2,128)S(1)}, s32[96,2]{0,1:T(2,128)}, u32[]{:S(2)}) copy-start(s32[96,2]{0,1:T(2,128)} %param.9) | copy-start | bytes 2308
  231.0 8.7 %copy-start.3 = (f32[24,40]{1,0:T(8,128)S(1)}, f32[24,40]{1,0:T(8,128)}, u32[]{:S(2)}) copy-start(f32[24,40]{1,0:T(8,128)} %param.12) | copy-start | bytes 11524
  231.0 9.1 %copy-start.5 = (s32[192]{0:T(256)S(1)}, s32[192]{0:T(256)}, u32[]{:S(2)}) copy-start(s32[192]{0:T(256)} %get-tuple-element.22) | copy-start | bytes 2308
  231.0 9.3 %copy-start.2 = (bf16[24,1600]{1,0:T(8,128)(2,1)S(1)}, bf16[24,1600]{1,0:T(8,128)(2,1)}, u32[]{:S(2)}) copy-start(bf16[24,1600]{1,0:T(8,128)(2,1)} %param.11) | copy-start | bytes 230404
  235.5 52.1 %collective-permute-start.4 = (bf16[64,40,384]{2,1,0:T(8,128)(2,1)}, bf16[64,40,384]{2,1,0:T(8,128)(2,1)}, u32[]{:S(2)}, u32[]{:S(2)}) collective-permute-start(bf16[64,40,384]{2,1,0:T(8,128)(2,1)} %get-tuple-element.39), channel_id=1, source_target_pairs={{0,1},{1,2},{2,3},{3,0},{4,5},{5,6},{6,7},{7,4},{8,9},{9,10},{10,1... | collective-permute-start | bytes 5898248 | tf_op jit(solution)/shard_map/ppermute | solution.py:453
  235.5 52.1 %collective-permute-start.3 = (bf16[64,40,384]{2,1,0:T(8,128)(2,1)}, bf16[64,40,384]{2,1,0:T(8,128)(2,1)}, u32[]{:S(2)}, u32[]{:S(2)}) collective-permute-start(bf16[64,40,384]{2,1,0:T(8,128)(2,1)} %get-tuple-element.40), channel_id=1, source_target_pairs={{0,3},{1,0},{2,1},{3,2},{4,7},{5,4},{6,5},{7,6},{8,11},{9,8},{10,9... | collective-permute-start | bytes 5898248 | tf_op jit(solution)/shard_map/ppermute | solution.py:453
  293.1 7.1 %collective-permute-start.5 = (f32[24,1600]{1,0:T(8,128)S(1)}, f32[24,1600]{1,0:T(8,128)S(1)}, u32[]{:S(2)}, u32[]{:S(2)}) collective-permute-start(f32[24,1600]{1,0:T(8,128)S(1)} %get-tuple-element.35), channel_id=1, source_target_pairs={{0,2},{1,3},{2,0},{3,1},{4,6},{5,7},{6,4},{7,5},{8,10},{9,11},{10,... | collective-permute-start | bytes 460808 | tf_op jit(solution)/shard_map/ppermute | solution.py:453
  295.0 9.2 %collective-permute-start.6 = (f32[24,1600]{1,0:T(8,128)S(1)}, f32[24,1600]{1,0:T(8,128)S(1)}, u32[]{:S(2)}, u32[]{:S(2)}) collective-permute-start(f32[24,1600]{1,0:T(8,128)S(1)} %get-tuple-element.36), channel_id=1, source_target_pairs={{0,1},{1,2},{2,3},{3,0},{4,5},{5,6},{6,7},{7,4},{8,9},{9,10},{10,1... | collective-permute-start | bytes 460808 | tf_op jit(solution)/shard_map/ppermute | solution.py:453
  295.2 9.0 %collective-permute-start.7 = (f32[24,1600]{1,0:T(8,128)S(1)}, f32[24,1600]{1,0:T(8,128)S(1)}, u32[]{:S(2)}, u32[]{:S(2)}) collective-permute-start(f32[24,1600]{1,0:T(8,128)S(1)} %get-tuple-element.37), channel_id=1, source_target_pairs={{0,3},{1,0},{2,1},{3,2},{4,7},{5,4},{6,5},{7,6},{8,11},{9,8},{10,9... | collective-permute-start | bytes 460808 | tf_op jit(solution)/shard_map/ppermute | solution.py:453
